TPU v7x, 32 devices: a whole 2x2x4 slice. The times are simulated.
32 devices in a mesh: dp: 16 (over z, y, core), tensor: 2 (over x).
Axes of the slice: x: 2, y: 2, z: 4, core: 2. Of those that a mesh axis runs over, the one named last changes fastest.
Arguments:
- tokens: bfloat16 [4096, 2304], P(('dp', 'tensor')), may hold values from -6 to 6
- cotangent: bfloat16 [4096, 2304], P(('dp', 'tensor')), may hold values from -6 to 6
- prefix: int32 [1], replicated, may hold values from 409 to 2048, as said below
- q_weight: float32 [2304, 2048], P('dp', 'tensor'), may hold values from -0.125 to 0.125
- k_weight: float32 [2304, 1024], P('dp', 'tensor'), may hold values from -0.125 to 0.125
- v_weight: float32 [2304, 1024], P('dp', 'tensor'), may hold values from -0.125 to 0.125
- out_weight: float32 [2048, 2304], P('tensor', 'dp'), may hold values from -0.125 to 0.125
- gate_weight: float32 [2304, 9216], P('dp', 'tensor'), may hold values from -0.125 to 0.125
- up_weight: float32 [2304, 9216], P('dp', 'tensor'), may hold values from -0.125 to 0.125
- down_weight: float32 [9216, 2304], P('tensor', 'dp'), may hold values from -0.0625 to 0.0625
- attn_gain: float32 [2304], P('dp'), may hold values from -0.5 to 0.5
- post_attn_gain: float32 [2304], P('dp'), may hold values from -0.5 to 0.5
- ffn_gain: float32 [2304], P('dp'), may hold values from -0.5 to 0.5
- post_ffn_gain: float32 [2304], P('dp'), may hold values from -0.5 to 0.5
Outputs:
- layer_out: bfloat16 [4096, 2304], P(('dp', 'tensor'))
- input_grad: float32 [4096, 2304], P(('dp', 'tensor'))
- q_grad: float32 [2304, 2048], P('dp', 'tensor')
- k_grad: float32 [2304, 1024], P('dp', 'tensor')
- v_grad: float32 [2304, 1024], P('dp', 'tensor')
- out_grad: float32 [2048, 2304], P('tensor', 'dp')
- gate_grad: float32 [2304, 9216], P('dp', 'tensor')
- up_grad: float32 [2304, 9216], P('dp', 'tensor')
- down_grad: float32 [9216, 2304], P('tensor', 'dp')
- attn_gain_grad: float32 [2304], P('dp')
- post_attn_gain_grad: float32 [2304], P('dp')
- ffn_gain_grad: float32 [2304], P('dp')
- post_ffn_gain_grad: float32 [2304], P('dp')
Inputs may be any that keep to these rules, and one draw needn't show every extreme that they name: prefix[s] is the count of leading positions of sequence s that attend both ways.
All inputs are finite; a program needn't handle non-finite values.
Results may differ from a plain program's by a relative error of at most 0.018.
Values may be sent and summed in bfloat16 or wider, within the bound.
No kernel may reach another device: no remote copies, remote signals or barrier semaphores. Data moves between devices by JAX's collectives and lax.ppermute only.
A program may use at most 640 MiB of HBM per device.

v0:
```python
import jax
import jax.numpy as jnp
from jax import lax
from jax.sharding import PartitionSpec as P

HEAD_DIM = 256
SEQ_LEN = 4096


norm_eps = 1e-06
score_cap = 50.0
rope_base = 10000.0


def shifted(value, axis, steps):
    count = lax.axis_size(axis)
    leading, last = (max(0, -steps), min(count, count - steps))
    return lax.ppermute(value, axis, [(source, source + steps) for source in range(leading, last)])


def rms_scale(values, gain_vec):
    return (
        values
        * lax.rsqrt(jnp.mean(values * values, axis=-1, keepdims=True) + norm_eps)
        * (1.0 + gain_vec)
    )


def rope_angles(positions, head_width):
    half_width = head_width // 2
    frequency = rope_base ** (-2.0 * jnp.arange(half_width).astype(jnp.float32) / head_width)
    return positions.astype(jnp.float32)[:, None] * frequency[None, :]


def rotate(values, angles):
    half_width = values.shape[-1] // 2
    cosine = jnp.cos(angles)[:, None, :]
    sine_part = jnp.sin(angles)[:, None, :]
    front_half = values[..., :half_width]
    back_half = values[..., half_width:]
    return jnp.concatenate(
        [front_half * cosine - back_half * sine_part, back_half * cosine + front_half * sine_part],
        axis=-1,
    )


def gelu_times(gate_part, up_part):
    return jax.nn.gelu(gate_part, approximate=True) * up_part


def contract_rows(left, right):
    return lax.dot_general(
        left, right, (((0,), (0,)), ((), ())), preferred_element_type=jnp.float32
    )


def contract_cols(left, right):
    return lax.dot_general(
        left, right, (((1,), (1,)), ((), ())), preferred_element_type=jnp.float32
    )


def fetch(rows_part, cols_part, gain_part):
    return (
        lax.all_gather(rows_part, "dp", axis=0, tiled=True),
        lax.all_gather(cols_part, "dp", axis=1, tiled=True),
        lax.all_gather(gain_part, "dp", axis=1, tiled=True),
    )


def gather_rows(values):
    return lax.all_gather(values, "tensor", axis=0, tiled=True)


def sum_rows(values):
    return lax.psum_scatter(values, "tensor", scatter_dimension=0, tiled=True)


def gather_grads(values):
    return lax.all_gather(values, "tensor", axis=0, tiled=True)


def sum_grads(values):
    return lax.psum_scatter(values, "tensor", scatter_dimension=0, tiled=True)


def reduce_tokens(left, right):
    dp_count = lax.axis_size("dp")
    inner_depth = left.shape[1]
    col_count = right.shape[1]
    pieces = 1
    while col_count // pieces > 2048 and col_count % (2 * pieces) == 0:
        pieces = pieces * 2
    block_width = col_count // pieces
    results = []
    for number in range(pieces):
        partial_term = contract_rows(
            left, right[:, number * block_width : (number + 1) * block_width]
        )
        arranged = partial_term.reshape(dp_count, inner_depth // dp_count, block_width)
        received = lax.all_to_all(
            arranged.astype(jnp.bfloat16), "dp", split_axis=0, concat_axis=0, tiled=True
        ).astype(arranged.dtype)
        results.append(jnp.sum(received, axis=0))
    return jnp.concatenate(results, axis=1)


def sequence_window(kv_rows, span, place):
    pieces = []
    for offset in range(1 - span, span):
        if offset == 0:
            pieces.append(kv_rows)
        else:
            pieces.append(shifted(kv_rows, "dp", -offset))
    relative = jnp.concatenate(pieces, axis=0)
    group_rows = kv_rows.shape[0]
    return lax.dynamic_slice_in_dim(relative, (span - 1 - place) * group_rows, span * group_rows, 0)


def return_grads(window_grads, span, place, group_rows):
    relative = jnp.zeros(((2 * span - 1) * group_rows, window_grads.shape[1]), jnp.float32)
    relative = lax.dynamic_update_slice_in_dim(
        relative, window_grads, (span - 1 - place) * group_rows, 0
    )
    total = relative[(span - 1) * group_rows : span * group_rows]
    for offset in range(1 - span, span):
        if offset != 0:
            start_row = (offset + span - 1) * group_rows
            total = total + shifted(
                relative[start_row : start_row + group_rows].astype(jnp.bfloat16), "dp", offset
            ).astype(jnp.float32)
    return total


def attention_scores(query_groups, key_window, query_pos, prefix_len):
    raw_scores = jnp.einsum(
        "tkgd,skd->kgts", query_groups, key_window, preferred_element_type=jnp.float32
    ) * HEAD_DIM ** (-0.5)
    capped = score_cap * jnp.tanh(raw_scores / score_cap)
    key_pos = jnp.arange(key_window.shape[0], dtype=jnp.int32)
    visible = (key_pos[None, :] <= query_pos[:, None]) | (key_pos[None, :] < prefix_len)
    return (raw_scores, jnp.where(visible, capped, -1e30))


def body(
    tokens,
    cotangent,
    prefix,
    q_weight,
    k_weight,
    v_weight,
    out_weight,
    gate_weight,
    up_weight,
    down_weight,
    attn_gain,
    post_attn_gain,
    ffn_gain,
    post_ffn_gain,
):
    bfloat = jnp.bfloat16
    single = jnp.float32
    q_cols = q_weight.shape[1]
    kv_cols = k_weight.shape[1]
    ff_cols = down_weight.shape[0]
    heads_local = q_cols // HEAD_DIM
    kv_local = kv_cols // HEAD_DIM
    group_size = heads_local // kv_local
    attn_rows_w = jnp.concatenate([q_weight, k_weight, v_weight], axis=1).astype(bfloat)
    attn_cols_w = out_weight.astype(bfloat)
    attn_gains_w = jnp.stack([attn_gain, post_attn_gain]).astype(bfloat)
    ffn_rows_w = jnp.concatenate([gate_weight, up_weight], axis=1).astype(bfloat)
    ffn_cols_w = down_weight.astype(bfloat)
    ffn_gains_w = jnp.stack([ffn_gain, post_ffn_gain]).astype(bfloat)
    qkv_full, out_full, attn_gains = fetch(attn_rows_w, attn_cols_w, attn_gains_w)
    gain_one = attn_gains[0].astype(single)
    gain_two = attn_gains[1].astype(single)
    resid = tokens.astype(single)
    normed_one = rms_scale(resid, gain_one)
    hidden_one = gather_rows(normed_one.astype(bfloat))
    group_rows = hidden_one.shape[0]
    span = SEQ_LEN // group_rows
    dp_index = lax.axis_index("dp")
    place = dp_index % span
    global_rows = dp_index * group_rows + jnp.arange(group_rows, dtype=jnp.int32)
    query_pos = global_rows % SEQ_LEN
    prefix_len = lax.dynamic_index_in_dim(
        prefix, dp_index * group_rows // SEQ_LEN, 0, keepdims=False
    )
    angles = rope_angles(query_pos, HEAD_DIM)
    projected = jnp.dot(hidden_one, qkv_full, preferred_element_type=single)
    query_rot = rotate(
        projected[:, :q_cols].reshape(group_rows, heads_local, HEAD_DIM), angles
    ).astype(bfloat)
    key_rot = rotate(
        projected[:, q_cols : q_cols + kv_cols].reshape(group_rows, kv_local, HEAD_DIM), angles
    ).astype(bfloat)
    value_rows = projected[:, q_cols + kv_cols :].astype(bfloat)
    kv_rows = jnp.concatenate([key_rot.reshape(group_rows, kv_cols), value_rows], axis=1)
    window = sequence_window(kv_rows, span, place)
    key_window = window[:, :kv_cols].reshape(SEQ_LEN, kv_local, HEAD_DIM)
    value_window = window[:, kv_cols:].reshape(SEQ_LEN, kv_local, HEAD_DIM)
    query_groups = query_rot.reshape(group_rows, kv_local, group_size, HEAD_DIM)
    raw_scores, masked = attention_scores(query_groups, key_window, query_pos, prefix_len)
    row_top = jnp.max(masked, axis=-1, keepdims=True)
    log_total = row_top + jnp.log(jnp.sum(jnp.exp(masked - row_top), axis=-1, keepdims=True))
    attn_probs = jnp.exp(masked - log_total).astype(bfloat)
    mixed_heads = jnp.einsum(
        "kgts,skd->tkgd", attn_probs, value_window, preferred_element_type=single
    )
    mixed_heads = mixed_heads.reshape(group_rows, q_cols).astype(bfloat)
    attn_sum = sum_rows(jnp.dot(mixed_heads, out_full, preferred_element_type=single))
    resid_two = resid + rms_scale(attn_sum, gain_two)
    gate_up_full, down_full, ffn_gains = fetch(ffn_rows_w, ffn_cols_w, ffn_gains_w)
    gain_three = ffn_gains[0].astype(single)
    gain_four = ffn_gains[1].astype(single)
    normed_three = rms_scale(resid_two, gain_three)
    hidden_two = gather_rows(normed_three.astype(bfloat))
    gate_up = jnp.dot(hidden_two, gate_up_full, preferred_element_type=single)
    gate_part = gate_up[:, :ff_cols]
    up_part = gate_up[:, ff_cols:]
    inner = gelu_times(gate_part, up_part).astype(bfloat)
    ffn_sum = sum_rows(jnp.dot(inner, down_full, preferred_element_type=single))
    layer_out = resid_two + rms_scale(ffn_sum, gain_four)
    upstream = cotangent.astype(single)
    gate_up_back, down_back = (gate_up_full, down_full)
    unused_out, post_ffn_pull = jax.vjp(rms_scale, ffn_sum, gain_four)
    ffn_grad, gain_four_grad = post_ffn_pull(upstream)
    ffn_grad_rows = gather_grads(ffn_grad.astype(bfloat))
    inner_grad = contract_cols(ffn_grad_rows, down_back)
    unused_inner, gelu_pull = jax.vjp(gelu_times, gate_part, up_part)
    gate_grad_part, up_grad_part = gelu_pull(inner_grad)
    gate_up_grad = jnp.concatenate([gate_grad_part, up_grad_part], axis=1).astype(bfloat)
    normed_three_grad = sum_grads(contract_cols(gate_up_grad, gate_up_back))
    gate_up_block = reduce_tokens(hidden_two, gate_up_grad)
    down_block = reduce_tokens(ffn_grad_rows, inner)
    unused_three, ffn_norm_pull = jax.vjp(rms_scale, resid_two, gain_three)
    resid_two_extra, gain_three_grad = ffn_norm_pull(normed_three_grad)
    resid_two_grad = upstream + resid_two_extra
    unused_two, post_attn_pull = jax.vjp(rms_scale, attn_sum, gain_two)
    attn_grad, gain_two_grad = post_attn_pull(resid_two_grad)
    attn_grad_rows = gather_grads(attn_grad.astype(bfloat))
    qkv_back, out_back = (qkv_full, out_full)
    mixed_grad = contract_cols(attn_grad_rows, out_back).astype(bfloat)
    mixed_grad_groups = mixed_grad.reshape(group_rows, kv_local, group_size, HEAD_DIM)
    raw_again, masked_again = attention_scores(query_groups, key_window, query_pos, prefix_len)
    probs_again = jnp.exp(masked_again - log_total)
    prob_grad = jnp.einsum(
        "tkgd,skd->kgts", mixed_grad_groups, value_window, preferred_element_type=single
    )
    value_grad = jnp.einsum(
        "kgts,tkgd->skd",
        probs_again.astype(bfloat),
        mixed_grad_groups,
        preferred_element_type=single,
    )
    capped_grad = probs_again * (
        prob_grad - jnp.sum(probs_again * prob_grad, axis=-1, keepdims=True)
    )
    slope = jnp.tanh(raw_again / score_cap)
    raw_grad = (capped_grad * (1.0 - slope * slope)).astype(bfloat)
    query_grad = jnp.einsum(
        "kgts,skd->tkgd", raw_grad, key_window, preferred_element_type=single
    ) * HEAD_DIM ** (-0.5)
    key_grad = jnp.einsum(
        "kgts,tkgd->skd", raw_grad, query_groups, preferred_element_type=single
    ) * HEAD_DIM ** (-0.5)
    window_grads = jnp.concatenate(
        [key_grad.reshape(SEQ_LEN, kv_cols), value_grad.reshape(SEQ_LEN, kv_cols)], axis=1
    )
    own_grads = return_grads(window_grads, span, place, group_rows)
    query_back = rotate(query_grad.reshape(group_rows, heads_local, HEAD_DIM), -angles).reshape(
        group_rows, q_cols
    )
    key_back = rotate(
        own_grads[:, :kv_cols].reshape(group_rows, kv_local, HEAD_DIM), -angles
    ).reshape(group_rows, kv_cols)
    qkv_grad = jnp.concatenate([query_back, key_back, own_grads[:, kv_cols:]], axis=1).astype(
        bfloat
    )
    normed_one_grad = sum_grads(contract_cols(qkv_grad, qkv_back))
    qkv_block = reduce_tokens(hidden_one, qkv_grad)
    out_block = reduce_tokens(attn_grad_rows, mixed_heads)
    unused_one, attn_norm_pull = jax.vjp(rms_scale, resid, gain_one)
    resid_extra, gain_one_grad = attn_norm_pull(normed_one_grad)
    input_grad = resid_two_grad + resid_extra
    gain_stack = jnp.stack([gain_one_grad, gain_two_grad, gain_three_grad, gain_four_grad])
    gain_parts = lax.psum_scatter(gain_stack, ("dp", "tensor"), scatter_dimension=1, tiled=True)
    gain_rows = lax.all_gather(gain_parts, "tensor", axis=1, tiled=True)
    return (
        layer_out.astype(bfloat),
        input_grad,
        qkv_block[:, :q_cols],
        qkv_block[:, q_cols : q_cols + kv_cols],
        qkv_block[:, q_cols + kv_cols :],
        out_block.T,
        gate_up_block[:, :ff_cols],
        gate_up_block[:, ff_cols:],
        down_block.T,
        gain_rows[0],
        gain_rows[1],
        gain_rows[2],
        gain_rows[3],
    )


def solution(mesh):
    return jax.shard_map(
        body,
        mesh=mesh,
        in_specs=(
            P(("dp", "tensor"), None),
            P(("dp", "tensor"), None),
            P(),
            P("dp", "tensor"),
            P("dp", "tensor"),
            P("dp", "tensor"),
            P("tensor", "dp"),
            P("dp", "tensor"),
            P("dp", "tensor"),
            P("tensor", "dp"),
            P("dp"),
            P("dp"),
            P("dp"),
            P("dp"),
        ),
        out_specs=(
            P(("dp", "tensor"), None),
            P(("dp", "tensor"), None),
            P("dp", "tensor"),
            P("dp", "tensor"),
            P("dp", "tensor"),
            P("tensor", "dp"),
            P("dp", "tensor"),
            P("dp", "tensor"),
            P("tensor", "dp"),
            P("dp"),
            P("dp"),
            P("dp"),
            P("dp"),
        ),
        check_vma=False,
    )
```

profile of v0, /device:TPU:0, one launch (start us, length us, event | category | flops | bytes accessed | tf_op | source)
XLA Modules:
  0.0 3282.4 jit_solution(16406684130065684168)
XLA Ops:
  8.7 23.1 all-gather
  43.8 12.3 all-gather.12.cloned.1.call-done
  56.1 84.3 %all-gather.14.cloned.1.call-done = bf16[2304,2048]{1,0:T(8,128)(2,1)} async-done(((bf16[144,2048]{1,0:T(8,128)(2,1)}), bf16[2304,2048]{1,0:T(8,128)(2,1)}) %all-gather.14.cloned.1.call-update) | async-done | bytes 9437200 | tf_op jit(solution)/shard_map/all_gather | solution.py:65
  226.5 43.8 %collective-permute-start.10 = (bf16[256,1024]{1,0:T(8,128)(2,1)}, bf16[256,1024]{1,0:T(8,128)(2,1)S(1)}, u32[]{:S(2)}, u32[]{:S(2)}) collective-permute-start(bf16[256,1024]{1,0:T(8,128)(2,1)} %pad_maximum_fusion.5), channel_id=1, source_target_pairs={{0,10},{2,12},{4,14},{6,16},{8,18},{10,20},{12,22},{14,24},{16,26}... | collective-permute-start | bytes 1572872 | tf_op jit(solution)/shard_map/ppermute | solution.py:18
  271.2 34.0 %collective-permute-start.11 = (bf16[256,1024]{1,0:T(8,128)(2,1)}, bf16[256,1024]{1,0:T(8,128)(2,1)S(1)}, u32[]{:S(2)}, u32[]{:S(2)}) collective-permute-start(bf16[256,1024]{1,0:T(8,128)(2,1)} %pad_maximum_fusion.5), channel_id=1, source_target_pairs={{0,8},{2,10},{4,12},{6,14},{8,16},{10,18},{12,20},{14,22},{16,24},... | collective-permute-start | bytes 1572872 | tf_op jit(solution)/shard_map/ppermute | solution.py:18
  311.0 10.5 collective-permute-start.14
  338.5 13.1 collective-permute-done.16
  362.7 34.1 %collective-permute-done.18 = bf16[256,1024]{1,0:T(8,128)(2,1)S(1)} collective-permute-done((bf16[256,1024]{1,0:T(8,128)(2,1)}, bf16[256,1024]{1,0:T(8,128)(2,1)S(1)}, u32[]{:S(2)}, u32[]{:S(2)}) %collective-permute-start.18) | collective-permute-done | bytes 524320 | tf_op jit(solution)/shard_map/ppermute | solution.py:18
  414.4 110.1 %collective-permute-done.22 = bf16[256,1024]{1,0:T(8,128)(2,1)S(1)} collective-permute-done((bf16[256,1024]{1,0:T(8,128)(2,1)}, bf16[256,1024]{1,0:T(8,128)(2,1)S(1)}, u32[]{:S(2)}, u32[]{:S(2)}) %collective-permute-start.22) | collective-permute-done | bytes 524320 | tf_op jit(solution)/shard_map/ppermute | solution.py:18
  564.0 11.2 copy.113
  596.4 9.6 fusion.31
  611.7 17.1 all-gather.1
  629.6 14.2 reduce-scatter.6.cloned.1.call-done
  655.9 15.0 all-gather.18.cloned.1.call-done
  670.9 212.2 %all-gather.20.cloned.1.call-done = bf16[2304,9216]{1,0:T(8,128)(2,1)} async-done(((bf16[144,9216]{1,0:T(8,128)(2,1)}), bf16[2304,9216]{1,0:T(8,128)(2,1)}) %all-gather.20.cloned.1.call-update) | async-done | bytes 42467344 | tf_op jit(solution)/shard_map/all_gather | solution.py:65
  883.1 22.6 fusion.127
  910.4 85.0 %all-gather.22.cloned.1.call-done = bf16[4608,2304]{0,1:T(8,128)(2,1)} async-done(((bf16[4608,144]{0,1:T(8,128)(2,1)}), bf16[4608,2304]{0,1:T(8,128)(2,1)}) %all-gather.22.cloned.1.call-update) | async-done | bytes 21233680 | tf_op jit(solution)/shard_map/all_gather | solution.py:66
  995.5 11.4 fusion.128
  1007.0 34.8 %reduce-scatter.8.cloned.1.call-done = f32[128,2304]{1,0:T(8,128)} async-done(((f32[256,2304]{1,0:T(8,128)}), f32[128,2304]{1,0:T(8,128)}) %reduce-scatter.8.cloned.1.call-update) | async-done | bytes 1179664 | tf_op jit(solution)/shard_map/reduce_scatter | solution.py:76
  1049.0 23.0 all-gather.24.cloned.1.call-done
  1088.4 91.8 %all-to-all-done.10 = bf16[16,144,1152]{2,1,0:T(8,128)(2,1)} async-done(((bf16[16,144,1152]{2,1,0:T(8,128)(2,1)}), bf16[16,144,1152]{2,1,0:T(8,128)(2,1)}, u32[]{:S(2)}, u32[]{:S(2)}) %all-to-all-start.10) | async-done | bytes 5308448 | tf_op jit(solution)/shard_map/all_to_all | solution.py:101
  1180.2 24.6 all-to-all-start.11
  1209.9 92.0 %all-to-all-done.11 = bf16[16,144,1152]{2,1,0:T(8,128)(2,1)} async-done(((bf16[16,144,1152]{2,1,0:T(8,128)(2,1)}), bf16[16,144,1152]{2,1,0:T(8,128)(2,1)}, u32[]{:S(2)}, u32[]{:S(2)}) %all-to-all-start.11) | async-done | bytes 5308448 | tf_op jit(solution)/shard_map/all_to_all | solution.py:101
  1301.9 24.2 all-to-all-start.12
  1331.1 92.0 %all-to-all-done.12 = bf16[16,144,1152]{2,1,0:T(8,128)(2,1)} async-done(((bf16[16,144,1152]{2,1,0:T(8,128)(2,1)}), bf16[16,144,1152]{2,1,0:T(8,128)(2,1)}, u32[]{:S(2)}, u32[]{:S(2)}) %all-to-all-start.12) | async-done | bytes 5308448 | tf_op jit(solution)/shard_map/all_to_all | solution.py:101
  1423.1 24.2 all-to-all-start.13
  1447.3 14.9 fusion.16
  1467.7 76.6 %all-to-all-done.13 = bf16[16,144,1152]{2,1,0:T(8,128)(2,1)} async-done(((bf16[16,144,1152]{2,1,0:T(8,128)(2,1)}), bf16[16,144,1152]{2,1,0:T(8,128)(2,1)}, u32[]{:S(2)}, u32[]{:S(2)}) %all-to-all-start.13) | async-done | bytes 5308448 | tf_op jit(solution)/shard_map/all_to_all | solution.py:101
  1544.3 24.2 all-to-all-start.6
  1573.7 91.9 %all-to-all-done.6 = bf16[16,144,1152]{2,1,0:T(8,128)(2,1)} async-done(((bf16[16,144,1152]{2,1,0:T(8,128)(2,1)}), bf16[16,144,1152]{2,1,0:T(8,128)(2,1)}, u32[]{:S(2)}, u32[]{:S(2)}) %all-to-all-start.6) | async-done | bytes 5308448 | tf_op jit(solution)/shard_map/all_to_all | solution.py:101
  1665.6 24.3 all-to-all-start.7
  1695.2 91.9 %all-to-all-done.7 = bf16[16,144,1152]{2,1,0:T(8,128)(2,1)} async-done(((bf16[16,144,1152]{2,1,0:T(8,128)(2,1)}), bf16[16,144,1152]{2,1,0:T(8,128)(2,1)}, u32[]{:S(2)}, u32[]{:S(2)}) %all-to-all-start.7) | async-done | bytes 5308448 | tf_op jit(solution)/shard_map/all_to_all | solution.py:101
  1787.0 24.2 all-to-all-start.8
  1816.3 92.0 %all-to-all-done.8 = bf16[16,144,1152]{2,1,0:T(8,128)(2,1)} async-done(((bf16[16,144,1152]{2,1,0:T(8,128)(2,1)}), bf16[16,144,1152]{2,1,0:T(8,128)(2,1)}, u32[]{:S(2)}, u32[]{:S(2)}) %all-to-all-start.8) | async-done | bytes 5308448 | tf_op jit(solution)/shard_map/all_to_all | solution.py:101
  1908.3 24.2 all-to-all-start.9
  1937.6 91.9 %all-to-all-done.9 = bf16[16,144,1152]{2,1,0:T(8,128)(2,1)} async-done(((bf16[16,144,1152]{2,1,0:T(8,128)(2,1)}), bf16[16,144,1152]{2,1,0:T(8,128)(2,1)}, u32[]{:S(2)}, u32[]{:S(2)}) %all-to-all-start.9) | async-done | bytes 5308448 | tf_op jit(solution)/shard_map/all_to_all | solution.py:101
  2029.5 24.2 all-to-all-start.2
  2058.8 92.0 %all-to-all-done.2 = bf16[16,144,1152]{2,1,0:T(8,128)(2,1)} async-done(((bf16[16,144,1152]{2,1,0:T(8,128)(2,1)}), bf16[16,144,1152]{2,1,0:T(8,128)(2,1)}, u32[]{:S(2)}, u32[]{:S(2)}) %all-to-all-start.2) | async-done | bytes 5308448 | tf_op jit(solution)/shard_map/all_to_all | solution.py:101
  2150.8 24.2 all-to-all-start.3
  2180.0 92.0 %all-to-all-done.3 = bf16[16,144,1152]{2,1,0:T(8,128)(2,1)} async-done(((bf16[16,144,1152]{2,1,0:T(8,128)(2,1)}), bf16[16,144,1152]{2,1,0:T(8,128)(2,1)}, u32[]{:S(2)}, u32[]{:S(2)}) %all-to-all-start.3) | async-done | bytes 5308448 | tf_op jit(solution)/shard_map/all_to_all | solution.py:101
  2272.0 24.2 all-to-all-start.4
  2301.4 91.9 %all-to-all-done.4 = bf16[16,144,1152]{2,1,0:T(8,128)(2,1)} async-done(((bf16[16,144,1152]{2,1,0:T(8,128)(2,1)}), bf16[16,144,1152]{2,1,0:T(8,128)(2,1)}, u32[]{:S(2)}, u32[]{:S(2)}) %all-to-all-start.4) | async-done | bytes 5308448 | tf_op jit(solution)/shard_map/all_to_all | solution.py:101
  2393.3 24.3 all-to-all-start.5
  2417.8 19.5 fusion.17
  2437.4 35.2 %reduce-scatter.10.cloned.1.call-done = f32[128,2304]{1,0:T(8,128)} async-done(((f32[256,2304]{1,0:T(8,128)}), f32[128,2304]{1,0:T(8,128)}) %reduce-scatter.10.cloned.1.call-update) | async-done | bytes 1179664 | tf_op jit(solution)/shard_map/reduce_scatter | solution.py:84
  2479.9 22.9 all-gather.26.cloned.1.call-done
  2520.6 18.6 all-to-all-start.1
  2539.3 29.1 bitcast_multiply_fusion.2
  2568.3 12.0 fusion.118
  2590.2 9.7 convert.124
  2632.3 11.0 collective-permute-done.42
  2647.1 20.1 collective-permute-start.48
  2689.0 12.0 collective-permute-start.54
  2701.1 65.0 %collective-permute-start.55 = (bf16[256,1024]{0,1:T(8,128)(2,1)}, bf16[256,1024]{0,1:T(8,128)(2,1)S(1)}, u32[]{:S(2)}, u32[]{:S(2)}) collective-permute-start(bf16[256,1024]{0,1:T(8,128)(2,1)} %get-tuple-element.33), channel_id=1, source_target_pairs={{0,22},{2,24},{4,26},{6,28},{8,30},{1,23},{3,25},{5,27},{7,29},{9,... | collective-permute-start | bytes 1572872 | tf_op jit(solution)/shard_map/ppermute | solution.py:18
  2771.1 18.3 collective-permute-start.56
  2789.5 11.2 collective-permute-start.57
  2800.7 17.1 collective-permute-start.58
  2817.9 23.8 collective-permute-start.59
  2849.6 11.6 collective-permute-done.31
  2865.5 74.5 %collective-permute-done.34 = bf16[256,1024]{0,1:T(8,128)(2,1)} collective-permute-done((bf16[256,1024]{0,1:T(8,128)(2,1)}, bf16[256,1024]{0,1:T(8,128)(2,1)}, u32[]{:S(2)}, u32[]{:S(2)}) %collective-permute-start.34) | collective-permute-done | bytes 524320 | tf_op jit(solution)/shard_map/ppermute | solution.py:18
  2952.4 26.5 fusion.30
  2980.3 15.7 collective-permute-done.40
  3010.7 18.5 all-to-all-start
  3085.8 169.6 %all-reduce = f32[4,2304]{1,0:T(4,128)S(1)} all-reduce(f32[4,2304]{1,0:T(4,128)S(1)} %pad_maximum_fusion.14), channel_id=6, replica_groups=mesh['dp'=16,'tensor'=2] {'dp','tensor'}, use_global_device_ids=true, to_apply=%region_33.34.clone | all-reduce | flops 9216 | bytes 73728
  (433 shorter events, 524.7 us)
Async XLA Ops:
  7.2 48.9 %all-gather.12.cloned.1.call-start = ((), (), s32[]{:S(2)}) async-start(), calls=%async_computation.18 | async-start | bytes 1769472 | tf_op jit(solution)/shard_map/all_gather | solution.py:72
  35.9 104.5 %all-gather.14.cloned.1.call-start = ((), (), s32[]{:S(2)}) async-start(), calls=%async_computation.19 | async-start | bytes 10027008 | tf_op jit(solution)/shard_map/all_gather | solution.py:65
  39.9 566.2 %all-gather.16.cloned.1.call-start = ((), (), s32[]{:S(2)}) async-start(), calls=%async_computation.20 | async-start | bytes 5013504 | tf_op jit(solution)/shard_map/all_gather | solution.py:66
  40.8 603.0 %reduce-scatter.6.cloned.1.call-start = ((), (), s32[]{:S(2)}) async-start(), calls=%async_computation.21 | async-start | bytes 3538944 | tf_op jit(solution)/shard_map/reduce_scatter | solution.py:76
  160.1 44.0 %collective-permute-start.3 = (bf16[256,1024]{1,0:T(8,128)(2,1)}, bf16[256,1024]{1,0:T(8,128)(2,1)}, u32[]{:S(2)}, u32[]{:S(2)}) collective-permute-start(bf16[256,1024]{1,0:T(8,128)(2,1)} %pad_maximum_fusion.5), channel_id=1, source_target_pairs={{0,24},{2,26},{4,28},{6,30},{1,25},{3,27},{5,29},{7,31}} | collective-permute-start | bytes 1572872 | tf_op jit(solution)/shard_map/ppermute | solution.py:18
  162.2 53.1 %collective-permute-start.4 = (bf16[256,1024]{1,0:T(8,128)(2,1)}, bf16[256,1024]{1,0:T(8,128)(2,1)}, u32[]{:S(2)}, u32[]{:S(2)}) collective-permute-start(bf16[256,1024]{1,0:T(8,128)(2,1)} %pad_maximum_fusion.5), channel_id=1, source_target_pairs={{0,22},{2,24},{4,26},{6,28},{8,30},{1,23},{3,25},{5,27},{7,29},{9,... | collective-permute-start | bytes 1572872 | tf_op jit(solution)/shard_map/ppermute | solution.py:18
  170.4 56.2 %collective-permute-start.5 = (bf16[256,1024]{1,0:T(8,128)(2,1)}, bf16[256,1024]{1,0:T(8,128)(2,1)S(1)}, u32[]{:S(2)}, u32[]{:S(2)}) collective-permute-start(bf16[256,1024]{1,0:T(8,128)(2,1)} %pad_maximum_fusion.5), channel_id=1, source_target_pairs={{0,20},{2,22},{4,24},{6,26},{8,28},{10,30},{1,21},{3,23},{5,25},{7... | collective-permute-start | bytes 1572872 | tf_op jit(solution)/shard_map/ppermute | solution.py:18
  181.6 89.6 %collective-permute-start.6 = (bf16[256,1024]{1,0:T(8,128)(2,1)}, bf16[256,1024]{1,0:T(8,128)(2,1)S(1)}, u32[]{:S(2)}, u32[]{:S(2)}) collective-permute-start(bf16[256,1024]{1,0:T(8,128)(2,1)} %pad_maximum_fusion.5), channel_id=1, source_target_pairs={{0,18},{2,20},{4,22},{6,24},{8,26},{10,28},{12,30},{1,19},{3,21},{... | collective-permute-start | bytes 1572872 | tf_op jit(solution)/shard_map/ppermute | solution.py:18
  192.8 113.2 %collective-permute-start.7 = (bf16[256,1024]{1,0:T(8,128)(2,1)}, bf16[256,1024]{1,0:T(8,128)(2,1)S(1)}, u32[]{:S(2)}, u32[]{:S(2)}) collective-permute-start(bf16[256,1024]{1,0:T(8,128)(2,1)} %pad_maximum_fusion.5), channel_id=1, source_target_pairs={{0,16},{2,18},{4,20},{6,22},{8,24},{10,26},{12,28},{14,30},{1,17},... | collective-permute-start | bytes 1572872 | tf_op jit(solution)/shard_map/ppermute | solution.py:18
  204.1 104.2 %collective-permute-start.8 = (bf16[256,1024]{1,0:T(8,128)(2,1)}, bf16[256,1024]{1,0:T(8,128)(2,1)S(1)}, u32[]{:S(2)}, u32[]{:S(2)}) collective-permute-start(bf16[256,1024]{1,0:T(8,128)(2,1)} %pad_maximum_fusion.5), channel_id=1, source_target_pairs={{0,14},{2,16},{4,18},{6,20},{8,22},{10,24},{12,26},{14,28},{16,30}... | collective-permute-start | bytes 1572872 | tf_op jit(solution)/shard_map/ppermute | solution.py:18
  215.3 95.7 %collective-permute-start.9 = (bf16[256,1024]{1,0:T(8,128)(2,1)}, bf16[256,1024]{1,0:T(8,128)(2,1)S(1)}, u32[]{:S(2)}, u32[]{:S(2)}) collective-permute-start(bf16[256,1024]{1,0:T(8,128)(2,1)} %pad_maximum_fusion.5), channel_id=1, source_target_pairs={{0,12},{2,14},{4,16},{6,18},{8,20},{10,22},{12,24},{14,26},{16,28}... | collective-permute-start | bytes 1572872 | tf_op jit(solution)/shard_map/ppermute | solution.py:18
  226.5 95.8 %collective-permute-start.10 = (bf16[256,1024]{1,0:T(8,128)(2,1)}, bf16[256,1024]{1,0:T(8,128)(2,1)S(1)}, u32[]{:S(2)}, u32[]{:S(2)}) collective-permute-start(bf16[256,1024]{1,0:T(8,128)(2,1)} %pad_maximum_fusion.5), channel_id=1, source_target_pairs={{0,10},{2,12},{4,14},{6,16},{8,18},{10,20},{12,22},{14,24},{16,26}... | collective-permute-start | bytes 1572872 | tf_op jit(solution)/shard_map/ppermute | solution.py:18
  271.2 53.3 %collective-permute-start.11 = (bf16[256,1024]{1,0:T(8,128)(2,1)}, bf16[256,1024]{1,0:T(8,128)(2,1)S(1)}, u32[]{:S(2)}, u32[]{:S(2)}) collective-permute-start(bf16[256,1024]{1,0:T(8,128)(2,1)} %pad_maximum_fusion.5), channel_id=1, source_target_pairs={{0,8},{2,10},{4,12},{6,14},{8,16},{10,18},{12,20},{14,22},{16,24},... | collective-permute-start | bytes 1572872 | tf_op jit(solution)/shard_map/ppermute | solution.py:18
  328.8 68.1 %collective-permute-start.18 = (bf16[256,1024]{1,0:T(8,128)(2,1)}, bf16[256,1024]{1,0:T(8,128)(2,1)S(1)}, u32[]{:S(2)}, u32[]{:S(2)}) collective-permute-start(bf16[256,1024]{1,0:T(8,128)(2,1)} %pad_maximum_fusion.5), channel_id=1, source_target_pairs={{8,0},{10,2},{12,4},{14,6},{16,8},{18,10},{20,12},{22,14},{24,16},... | collective-permute-start | bytes 1572872 | tf_op jit(solution)/shard_map/ppermute | solution.py:18
  330.9 68.1 %collective-permute-start.19 = (bf16[256,1024]{1,0:T(8,128)(2,1)}, bf16[256,1024]{1,0:T(8,128)(2,1)S(1)}, u32[]{:S(2)}, u32[]{:S(2)}) collective-permute-start(bf16[256,1024]{1,0:T(8,128)(2,1)} %pad_maximum_fusion.5), channel_id=1, source_target_pairs={{10,0},{12,2},{14,4},{16,6},{18,8},{20,10},{22,12},{24,14},{26,16}... | collective-permute-start | bytes 1572872 | tf_op jit(solution)/shard_map/ppermute | solution.py:18
  336.4 73.7 %collective-permute-start.20 = (bf16[256,1024]{1,0:T(8,128)(2,1)}, bf16[256,1024]{1,0:T(8,128)(2,1)S(1)}, u32[]{:S(2)}, u32[]{:S(2)}) collective-permute-start(bf16[256,1024]{1,0:T(8,128)(2,1)} %pad_maximum_fusion.5), channel_id=1, source_target_pairs={{12,0},{14,2},{16,4},{18,6},{20,8},{22,10},{24,12},{26,14},{28,16}... | collective-permute-start | bytes 1572872 | tf_op jit(solution)/shard_map/ppermute | solution.py:18
  351.6 60.7 %collective-permute-start.21 = (bf16[256,1024]{1,0:T(8,128)(2,1)}, bf16[256,1024]{1,0:T(8,128)(2,1)S(1)}, u32[]{:S(2)}, u32[]{:S(2)}) collective-permute-start(bf16[256,1024]{1,0:T(8,128)(2,1)} %pad_maximum_fusion.5), channel_id=1, source_target_pairs={{14,0},{16,2},{18,4},{20,6},{22,8},{24,10},{26,12},{28,14},{30,16}... | collective-permute-start | bytes 1572872 | tf_op jit(solution)/shard_map/ppermute | solution.py:18
  360.6 163.9 %collective-permute-start.22 = (bf16[256,1024]{1,0:T(8,128)(2,1)}, bf16[256,1024]{1,0:T(8,128)(2,1)S(1)}, u32[]{:S(2)}, u32[]{:S(2)}) collective-permute-start(bf16[256,1024]{1,0:T(8,128)(2,1)} %pad_maximum_fusion.5), channel_id=1, source_target_pairs={{16,0},{18,2},{20,4},{22,6},{24,8},{26,10},{28,12},{30,14},{17,1},... | collective-permute-start | bytes 1572872 | tf_op jit(solution)/shard_map/ppermute | solution.py:18
  396.9 131.0 %collective-permute-start.23 = (bf16[256,1024]{1,0:T(8,128)(2,1)}, bf16[256,1024]{1,0:T(8,128)(2,1)S(1)}, u32[]{:S(2)}, u32[]{:S(2)}) collective-permute-start(bf16[256,1024]{1,0:T(8,128)(2,1)} %pad_maximum_fusion.5), channel_id=1, source_target_pairs={{18,0},{20,2},{22,4},{24,6},{26,8},{28,10},{30,12},{19,1},{21,3},{... | collective-permute-start | bytes 1572872 | tf_op jit(solution)/shard_map/ppermute | solution.py:18
  399.0 136.5 %collective-permute-start.24 = (bf16[256,1024]{1,0:T(8,128)(2,1)}, bf16[256,1024]{1,0:T(8,128)(2,1)S(1)}, u32[]{:S(2)}, u32[]{:S(2)}) collective-permute-start(bf16[256,1024]{1,0:T(8,128)(2,1)} %pad_maximum_fusion.5), channel_id=1, source_target_pairs={{20,0},{22,2},{24,4},{26,6},{28,8},{30,10},{21,1},{23,3},{25,5},{2... | collective-permute-start | bytes 1572872 | tf_op jit(solution)/shard_map/ppermute | solution.py:18
  410.1 133.3 %collective-permute-start.25 = (bf16[256,1024]{1,0:T(8,128)(2,1)}, bf16[256,1024]{1,0:T(8,128)(2,1)S(1)}, u32[]{:S(2)}, u32[]{:S(2)}) collective-permute-start(bf16[256,1024]{1,0:T(8,128)(2,1)} %pad_maximum_fusion.5), channel_id=1, source_target_pairs={{22,0},{24,2},{26,4},{28,6},{30,8},{23,1},{25,3},{27,5},{29,7},{31... | collective-permute-start | bytes 1572872 | tf_op jit(solution)/shard_map/ppermute | solution.py:18
  412.3 131.9 %collective-permute-start.26 = (bf16[256,1024]{1,0:T(8,128)(2,1)}, bf16[256,1024]{1,0:T(8,128)(2,1)S(1)}, u32[]{:S(2)}, u32[]{:S(2)}) collective-permute-start(bf16[256,1024]{1,0:T(8,128)(2,1)} %pad_maximum_fusion.5), channel_id=1, source_target_pairs={{24,0},{26,2},{28,4},{30,6},{25,1},{27,3},{29,5},{31,7}} | collective-permute-start | bytes 1572872 | tf_op jit(solution)/shard_map/ppermute | solution.py:18
  611.5 59.4 %all-gather.18.cloned.1.call-start = ((), (), s32[]{:S(2)}) async-start(), calls=%async_computation.22 | async-start | bytes 1769472 | tf_op jit(solution)/shard_map/all_gather | solution.py:72
  647.9 235.1 %all-gather.20.cloned.1.call-start = ((), (), s32[]{:S(2)}) async-start(), calls=%async_computation.23 | async-start | bytes 45121536 | tf_op jit(solution)/shard_map/all_gather | solution.py:65
  652.5 342.9 %all-gather.22.cloned.1.call-start = ((), (), s32[]{:S(2)}) async-start(), calls=%async_computation.24 | async-start | bytes 22560768 | tf_op jit(solution)/shard_map/all_gather | solution.py:66
  655.6 386.1 %reduce-scatter.8.cloned.1.call-start = ((), (), s32[]{:S(2)}) async-start(), calls=%async_computation.25 | async-start | bytes 3538944 | tf_op jit(solution)/shard_map/reduce_scatter | solution.py:76
  1006.9 65.1 %all-gather.24.cloned.1.call-start = ((), (), s32[]{:S(2)}) async-start(), calls=%async_computation.26 | async-start | bytes 1769472 | tf_op jit(solution)/shard_map/all_gather | solution.py:80
  1077.3 102.9 %all-to-all-start.10 = ((bf16[16,144,1152]{2,1,0:T(8,128)(2,1)}), bf16[16,144,1152]{2,1,0:T(8,128)(2,1)}, u32[]{:S(2)}, u32[]{:S(2)}) async-start(bf16[16,144,1152]{2,1,0:T(8,128)(2,1)} %bitcast.185), calls=%async_computation.14 | async-start | bytes 10616832 | tf_op jit(solution)/shard_map/all_to_all | solution.py:101
  1180.2 121.7 %all-to-all-start.11 = ((bf16[16,144,1152]{2,1,0:T(8,128)(2,1)}), bf16[16,144,1152]{2,1,0:T(8,128)(2,1)}, u32[]{:S(2)}, u32[]{:S(2)}) async-start(bf16[16,144,1152]{2,1,0:T(8,128)(2,1)} %bitcast.179), calls=%async_computation.15 | async-start | bytes 10616832 | tf_op jit(solution)/shard_map/all_to_all | solution.py:101
  1301.9 121.2 %all-to-all-start.12 = ((bf16[16,144,1152]{2,1,0:T(8,128)(2,1)}), bf16[16,144,1152]{2,1,0:T(8,128)(2,1)}, u32[]{:S(2)}, u32[]{:S(2)}) async-start(bf16[16,144,1152]{2,1,0:T(8,128)(2,1)} %bitcast.176), calls=%async_computation.16 | async-start | bytes 10616832 | tf_op jit(solution)/shard_map/all_to_all | solution.py:101
  1423.1 121.2 %all-to-all-start.13 = ((bf16[16,144,1152]{2,1,0:T(8,128)(2,1)}), bf16[16,144,1152]{2,1,0:T(8,128)(2,1)}, u32[]{:S(2)}, u32[]{:S(2)}) async-start(bf16[16,144,1152]{2,1,0:T(8,128)(2,1)} %bitcast.175), calls=%async_computation.17 | async-start | bytes 10616832 | tf_op jit(solution)/shard_map/all_to_all | solution.py:101
  1544.3 121.2 %all-to-all-start.6 = ((bf16[16,144,1152]{2,1,0:T(8,128)(2,1)}), bf16[16,144,1152]{2,1,0:T(8,128)(2,1)}, u32[]{:S(2)}, u32[]{:S(2)}) async-start(bf16[16,144,1152]{2,1,0:T(8,128)(2,1)} %bitcast.180), calls=%async_computation.10 | async-start | bytes 10616832 | tf_op jit(solution)/shard_map/all_to_all | solution.py:101
  1665.6 121.4 %all-to-all-start.7 = ((bf16[16,144,1152]{2,1,0:T(8,128)(2,1)}), bf16[16,144,1152]{2,1,0:T(8,128)(2,1)}, u32[]{:S(2)}, u32[]{:S(2)}) async-start(bf16[16,144,1152]{2,1,0:T(8,128)(2,1)} %bitcast.181), calls=%async_computation.11 | async-start | bytes 10616832 | tf_op jit(solution)/shard_map/all_to_all | solution.py:101
  1787.0 121.2 %all-to-all-start.8 = ((bf16[16,144,1152]{2,1,0:T(8,128)(2,1)}), bf16[16,144,1152]{2,1,0:T(8,128)(2,1)}, u32[]{:S(2)}, u32[]{:S(2)}) async-start(bf16[16,144,1152]{2,1,0:T(8,128)(2,1)} %bitcast.182), calls=%async_computation.12 | async-start | bytes 10616832 | tf_op jit(solution)/shard_map/all_to_all | solution.py:101
  1908.3 121.2 %all-to-all-start.9 = ((bf16[16,144,1152]{2,1,0:T(8,128)(2,1)}), bf16[16,144,1152]{2,1,0:T(8,128)(2,1)}, u32[]{:S(2)}, u32[]{:S(2)}) async-start(bf16[16,144,1152]{2,1,0:T(8,128)(2,1)} %bitcast.177), calls=%async_computation.13 | async-start | bytes 10616832 | tf_op jit(solution)/shard_map/all_to_all | solution.py:101
  2029.5 121.2 %all-to-all-start.2 = ((bf16[16,144,1152]{2,1,0:T(8,128)(2,1)}), bf16[16,144,1152]{2,1,0:T(8,128)(2,1)}, u32[]{:S(2)}, u32[]{:S(2)}) async-start(bf16[16,144,1152]{2,1,0:T(8,128)(2,1)} %bitcast.183), calls=%async_computation.6 | async-start | bytes 10616832 | tf_op jit(solution)/shard_map/all_to_all | solution.py:101
  2150.8 121.2 %all-to-all-start.3 = ((bf16[16,144,1152]{2,1,0:T(8,128)(2,1)}), bf16[16,144,1152]{2,1,0:T(8,128)(2,1)}, u32[]{:S(2)}, u32[]{:S(2)}) async-start(bf16[16,144,1152]{2,1,0:T(8,128)(2,1)} %bitcast.184), calls=%async_computation.7 | async-start | bytes 10616832 | tf_op jit(solution)/shard_map/all_to_all | solution.py:101
  2272.0 121.2 %all-to-all-start.4 = ((bf16[16,144,1152]{2,1,0:T(8,128)(2,1)}), bf16[16,144,1152]{2,1,0:T(8,128)(2,1)}, u32[]{:S(2)}, u32[]{:S(2)}) async-start(bf16[16,144,1152]{2,1,0:T(8,128)(2,1)} %bitcast.178), calls=%async_computation.8 | async-start | bytes 10616832 | tf_op jit(solution)/shard_map/all_to_all | solution.py:101
  2393.3 127.3 %all-to-all-start.5 = ((bf16[16,144,1152]{2,1,0:T(8,128)(2,1)}), bf16[16,144,1152]{2,1,0:T(8,128)(2,1)}, u32[]{:S(2)}, u32[]{:S(2)}) async-start(bf16[16,144,1152]{2,1,0:T(8,128)(2,1)} %bitcast.174), calls=%async_computation.9 | async-start | bytes 10616832 | tf_op jit(solution)/shard_map/all_to_all | solution.py:101
  2417.6 55.0 %reduce-scatter.10.cloned.1.call-start = ((), (), s32[]{:S(2)}) async-start(), calls=%async_computation.27 | async-start | bytes 3538944 | tf_op jit(solution)/shard_map/reduce_scatter | solution.py:84
  2437.3 65.5 %all-gather.26.cloned.1.call-start = ((), (), s32[]{:S(2)}) async-start(), calls=%async_computation.28 | async-start | bytes 1769472 | tf_op jit(solution)/shard_map/all_gather | solution.py:80
  2520.6 490.2 %all-to-all-start.1 = ((bf16[16,144,1024]{2,1,0:T(8,128)(2,1)}), bf16[16,144,1024]{2,1,0:T(8,128)(2,1)}, u32[]{:S(2)}, u32[]{:S(2)}) async-start(bf16[16,144,1024]{2,1,0:T(8,128)(2,1)} %convolution_convert_fusion.13), calls=%async_computation.5 | async-start | bytes 9437184 | tf_op jit(solution)/shard_map/all_to_all | solution.py:101
  2617.2 50.0 %collective-permute-start.44 = (bf16[256,1024]{0,1:T(8,128)(2,1)}, bf16[256,1024]{0,1:T(8,128)(2,1)}, u32[]{:S(2)}, u32[]{:S(2)}) collective-permute-start(bf16[256,1024]{0,1:T(8,128)(2,1)} %get-tuple-element.44), channel_id=1, source_target_pairs={{2,0},{4,2},{6,4},{8,6},{10,8},{12,10},{14,12},{16,14},{18,16},{20... | collective-permute-start | bytes 1572872 | tf_op jit(solution)/shard_map/ppermute | solution.py:18
  2618.5 57.1 %collective-permute-start.45 = (bf16[256,1024]{0,1:T(8,128)(2,1)}, bf16[256,1024]{0,1:T(8,128)(2,1)}, u32[]{:S(2)}, u32[]{:S(2)}) collective-permute-start(bf16[256,1024]{0,1:T(8,128)(2,1)} %get-tuple-element.43), channel_id=1, source_target_pairs={{0,2},{2,4},{4,6},{6,8},{8,10},{10,12},{12,14},{14,16},{16,18},{18... | collective-permute-start | bytes 1572872 | tf_op jit(solution)/shard_map/ppermute | solution.py:18
  2630.2 47.5 %collective-permute-start.46 = (bf16[256,1024]{0,1:T(8,128)(2,1)}, bf16[256,1024]{0,1:T(8,128)(2,1)}, u32[]{:S(2)}, u32[]{:S(2)}) collective-permute-start(bf16[256,1024]{0,1:T(8,128)(2,1)} %get-tuple-element.42), channel_id=1, source_target_pairs={{0,4},{2,6},{4,8},{6,10},{8,12},{10,14},{12,16},{14,18},{16,20},{1... | collective-permute-start | bytes 1572872 | tf_op jit(solution)/shard_map/ppermute | solution.py:18
  2643.3 37.9 %collective-permute-start.47 = (bf16[256,1024]{0,1:T(8,128)(2,1)}, bf16[256,1024]{0,1:T(8,128)(2,1)}, u32[]{:S(2)}, u32[]{:S(2)}) collective-permute-start(bf16[256,1024]{0,1:T(8,128)(2,1)} %get-tuple-element.41), channel_id=1, source_target_pairs={{0,6},{2,8},{4,10},{6,12},{8,14},{10,16},{12,18},{14,20},{16,22},{... | collective-permute-start | bytes 1572872 | tf_op jit(solution)/shard_map/ppermute | solution.py:18
  2677.7 93.4 %collective-permute-start.51 = (bf16[256,1024]{0,1:T(8,128)(2,1)}, bf16[256,1024]{0,1:T(8,128)(2,1)S(1)}, u32[]{:S(2)}, u32[]{:S(2)}) collective-permute-start(bf16[256,1024]{0,1:T(8,128)(2,1)} %get-tuple-element.37), channel_id=1, source_target_pairs={{0,14},{2,16},{4,18},{6,20},{8,22},{10,24},{12,26},{14,28},{16,30}... | collective-permute-start | bytes 1572872 | tf_op jit(solution)/shard_map/ppermute | solution.py:18
  2681.2 108.3 %collective-permute-start.52 = (bf16[256,1024]{0,1:T(8,128)(2,1)}, bf16[256,1024]{0,1:T(8,128)(2,1)S(1)}, u32[]{:S(2)}, u32[]{:S(2)}) collective-permute-start(bf16[256,1024]{0,1:T(8,128)(2,1)} %get-tuple-element.36), channel_id=1, source_target_pairs={{0,16},{2,18},{4,20},{6,22},{8,24},{10,26},{12,28},{14,30},{1,17},... | collective-permute-start | bytes 1572872 | tf_op jit(solution)/shard_map/ppermute | solution.py:18
  2683.1 117.6 %collective-permute-start.53 = (bf16[256,1024]{0,1:T(8,128)(2,1)}, bf16[256,1024]{0,1:T(8,128)(2,1)S(1)}, u32[]{:S(2)}, u32[]{:S(2)}) collective-permute-start(bf16[256,1024]{0,1:T(8,128)(2,1)} %get-tuple-element.35), channel_id=1, source_target_pairs={{0,18},{2,20},{4,22},{6,24},{8,26},{10,28},{12,30},{1,19},{3,21},{... | collective-permute-start | bytes 1572872 | tf_op jit(solution)/shard_map/ppermute | solution.py:18
  2689.0 128.8 %collective-permute-start.54 = (bf16[256,1024]{0,1:T(8,128)(2,1)}, bf16[256,1024]{0,1:T(8,128)(2,1)S(1)}, u32[]{:S(2)}, u32[]{:S(2)}) collective-permute-start(bf16[256,1024]{0,1:T(8,128)(2,1)} %get-tuple-element.34), channel_id=1, source_target_pairs={{0,20},{2,22},{4,24},{6,26},{8,28},{10,30},{1,21},{3,23},{5,25},{7... | collective-permute-start | bytes 1572872 | tf_op jit(solution)/shard_map/ppermute | solution.py:18
  2701.1 140.6 %collective-permute-start.55 = (bf16[256,1024]{0,1:T(8,128)(2,1)}, bf16[256,1024]{0,1:T(8,128)(2,1)S(1)}, u32[]{:S(2)}, u32[]{:S(2)}) collective-permute-start(bf16[256,1024]{0,1:T(8,128)(2,1)} %get-tuple-element.33), channel_id=1, source_target_pairs={{0,22},{2,24},{4,26},{6,28},{8,30},{1,23},{3,25},{5,27},{7,29},{9,... | collective-permute-start | bytes 1572872 | tf_op jit(solution)/shard_map/ppermute | solution.py:18
  2771.1 71.9 %collective-permute-start.56 = (bf16[256,1024]{0,1:T(8,128)(2,1)S(1)}, bf16[256,1024]{0,1:T(8,128)(2,1)S(1)}, u32[]{:S(2)}, u32[]{:S(2)}) collective-permute-start(bf16[256,1024]{0,1:T(8,128)(2,1)S(1)} %copy-done.34), channel_id=1, source_target_pairs={{0,24},{2,26},{4,28},{6,30},{1,25},{3,27},{5,29},{7,31}} | collective-permute-start | bytes 1572872 | tf_op jit(solution)/shard_map/ppermute | solution.py:18
  2789.5 54.9 %collective-permute-start.57 = (bf16[256,1024]{0,1:T(8,128)(2,1)S(1)}, bf16[256,1024]{0,1:T(8,128)(2,1)S(1)}, u32[]{:S(2)}, u32[]{:S(2)}) collective-permute-start(bf16[256,1024]{0,1:T(8,128)(2,1)S(1)} %copy-done.32), channel_id=1, source_target_pairs={{0,26},{2,28},{4,30},{1,27},{3,29},{5,31}} | collective-permute-start | bytes 1572872 | tf_op jit(solution)/shard_map/ppermute | solution.py:18
  2800.7 45.1 %collective-permute-start.58 = (bf16[256,1024]{0,1:T(8,128)(2,1)S(1)}, bf16[256,1024]{0,1:T(8,128)(2,1)S(1)}, u32[]{:S(2)}, u32[]{:S(2)}) collective-permute-start(bf16[256,1024]{0,1:T(8,128)(2,1)S(1)} %copy-done.30), channel_id=1, source_target_pairs={{0,28},{2,30},{1,29},{3,31}} | collective-permute-start | bytes 1572872 | tf_op jit(solution)/shard_map/ppermute | solution.py:18
  2845.8 94.2 %collective-permute-start.34 = (bf16[256,1024]{0,1:T(8,128)(2,1)}, bf16[256,1024]{0,1:T(8,128)(2,1)}, u32[]{:S(2)}, u32[]{:S(2)}) collective-permute-start(bf16[256,1024]{0,1:T(8,128)(2,1)} %get-tuple-element.55), channel_id=1, source_target_pairs={{22,0},{24,2},{26,4},{28,6},{30,8},{23,1},{25,3},{27,5},{29,7},{31... | collective-permute-start | bytes 1572872 | tf_op jit(solution)/shard_map/ppermute | solution.py:18
  2848.3 93.0 %collective-permute-start.35 = (bf16[256,1024]{0,1:T(8,128)(2,1)}, bf16[256,1024]{0,1:T(8,128)(2,1)}, u32[]{:S(2)}, u32[]{:S(2)}) collective-permute-start(bf16[256,1024]{0,1:T(8,128)(2,1)} %get-tuple-element.54), channel_id=1, source_target_pairs={{20,0},{22,2},{24,4},{26,6},{28,8},{30,10},{21,1},{23,3},{25,5},{2... | collective-permute-start | bytes 1572872 | tf_op jit(solution)/shard_map/ppermute | solution.py:18
  2861.2 89.9 %collective-permute-start.36 = (bf16[256,1024]{0,1:T(8,128)(2,1)}, bf16[256,1024]{0,1:T(8,128)(2,1)}, u32[]{:S(2)}, u32[]{:S(2)}) collective-permute-start(bf16[256,1024]{0,1:T(8,128)(2,1)} %get-tuple-element.53), channel_id=1, source_target_pairs={{18,0},{20,2},{22,4},{24,6},{26,8},{28,10},{30,12},{19,1},{21,3},{... | collective-permute-start | bytes 1572872 | tf_op jit(solution)/shard_map/ppermute | solution.py:18
  2862.9 117.4 %collective-permute-start.37 = (bf16[256,1024]{0,1:T(8,128)(2,1)}, bf16[256,1024]{0,1:T(8,128)(2,1)}, u32[]{:S(2)}, u32[]{:S(2)}) collective-permute-start(bf16[256,1024]{0,1:T(8,128)(2,1)} %get-tuple-element.52), channel_id=1, source_target_pairs={{16,0},{18,2},{20,4},{22,6},{24,8},{26,10},{28,12},{30,14},{17,1},... | collective-permute-start | bytes 1572872 | tf_op jit(solution)/shard_map/ppermute | solution.py:18
  2864.2 116.1 %collective-permute-start.38 = (bf16[256,1024]{0,1:T(8,128)(2,1)}, bf16[256,1024]{0,1:T(8,128)(2,1)}, u32[]{:S(2)}, u32[]{:S(2)}) collective-permute-start(bf16[256,1024]{0,1:T(8,128)(2,1)} %get-tuple-element.51), channel_id=1, source_target_pairs={{14,0},{16,2},{18,4},{20,6},{22,8},{24,10},{26,12},{28,14},{30,16}... | collective-permute-start | bytes 1572872 | tf_op jit(solution)/shard_map/ppermute | solution.py:18
  2940.0 40.3 %collective-permute-start.39 = (bf16[256,1024]{0,1:T(8,128)(2,1)}, bf16[256,1024]{0,1:T(8,128)(2,1)}, u32[]{:S(2)}, u32[]{:S(2)}) collective-permute-start(bf16[256,1024]{0,1:T(8,128)(2,1)} %get-tuple-element.50), channel_id=1, source_target_pairs={{12,0},{14,2},{16,4},{18,6},{20,8},{22,10},{24,12},{26,14},{28,16}... | collective-permute-start | bytes 1572872 | tf_op jit(solution)/shard_map/ppermute | solution.py:18
  2941.3 54.7 %collective-permute-start.40 = (bf16[256,1024]{0,1:T(8,128)(2,1)}, bf16[256,1024]{0,1:T(8,128)(2,1)}, u32[]{:S(2)}, u32[]{:S(2)}) collective-permute-start(bf16[256,1024]{0,1:T(8,128)(2,1)} %get-tuple-element.49), channel_id=1, source_target_pairs={{10,0},{12,2},{14,4},{16,6},{18,8},{20,10},{22,12},{24,14},{26,16}... | collective-permute-start | bytes 1572872 | tf_op jit(solution)/shard_map/ppermute | solution.py:18
  2951.1 45.0 %collective-permute-start.41 = (bf16[256,1024]{0,1:T(8,128)(2,1)}, bf16[256,1024]{0,1:T(8,128)(2,1)}, u32[]{:S(2)}, u32[]{:S(2)}) collective-permute-start(bf16[256,1024]{0,1:T(8,128)(2,1)} %get-tuple-element.48), channel_id=1, source_target_pairs={{8,0},{10,2},{12,4},{14,6},{16,8},{18,10},{20,12},{22,14},{24,16},... | collective-permute-start | bytes 1572872 | tf_op jit(solution)/shard_map/ppermute | solution.py:18
  3010.7 256.7 %all-to-all-start = ((bf16[16,144,2048]{2,1,0:T(8,128)(2,1)}), bf16[16,144,2048]{2,1,0:T(8,128)(2,1)}, u32[]{:S(2)}, u32[]{:S(2)}) async-start(bf16[16,144,2048]{2,1,0:T(8,128)(2,1)} %bitcast.173), calls=%async_computation.4 | async-start | bytes 18874368 | tf_op jit(solution)/shard_map/all_to_all | solution.py:101
  3029.3 54.7 %reduce-scatter.12.cloned.1.call-start = ((), (), s32[]{:S(2)}) async-start(), calls=%async_computation.29 | async-start | bytes 3538944 | tf_op jit(solution)/shard_map/reduce_scatter | solution.py:84
  (90 other events, 4455.7 us)
Sparse Core Ops, SparseCore 0:
  36.0 20.0 all-gather.11
  59.0 81.4 all-gather.13
  143.3 150.3 all-gather.15
  611.6 32.0 reduce-scatter.5
  648.1 22.7 all-gather.17
  673.0 210.0 all-gather.19
  885.3 110.0 all-gather.21
  1007.0 34.6 reduce-scatter.7
  1049.1 22.7 all-gather.23
  2437.5 35.0 reduce-scatter.9
  2480.0 22.7 all-gather.25
  3037.5 35.0 reduce-scatter.11
where the time goes:
time: 3290 us; the launch traced here: 3280 us
  waiting for transfers between devices  1900 us (58%)
  starting transfers between devices  659 us (20%)
  matrix products  254 us (8%)
  blocking collectives  214 us (7%)
  other arithmetic  143 us (4%)
  local copies, waits for them, and re-layouts  96 us (3%)
    all_to_all x14, waiting for transfers between devices, reduce_tokens(): lax.all_to_all(arranged.astype(jnp.bfloat16), 'dp', split_axis=0, concat_...  996 us
    ppermute x60, waiting for transfers between devices, shifted(): lax.ppermute(value, axis, [(source, source + steps) for source in range(l...  363 us
    ppermute x60, starting transfers between devices, shifted(): lax.ppermute(value, axis, [(source, source + steps) for source in range(l...  348 us
    all_to_all x14, starting transfers between devices, reduce_tokens(): lax.all_to_all(arranged.astype(jnp.bfloat16), 'dp', split_axis=0, concat_...  309 us
    all_gather x2, waiting for transfers between devices, fetch(): lax.all_gather(rows_part, 'dp', axis=0, tiled=True)  297 us
    unnamed x1, blocking collectives  170 us
    all_gather x2, waiting for transfers between devices, fetch(): lax.all_gather(cols_part, 'dp', axis=1, tiled=True)  85 us
    dot_general x14, matrix products, contract_rows(): lax.dot_general(left, right, (((0,), (0,)), ((), ())), preferred_element_...  71.1 us
  transfers between devices with their start and end apart: 86, of which 47 were waited for; matrix products, arithmetic and copies ran while one was open for 13% of the time, Pallas kernels for 0%

commit v1 on v0

v1 whole, which is shorter than its diff:
```python
import functools
import math

import jax
import jax.numpy as jnp
from jax import lax
from jax.experimental import pallas as pl
from jax.experimental.pallas import tpu as pltpu
from jax.sharding import PartitionSpec as P

HEAD_DIM = 256
SEQ_LEN = 4096

norm_eps = 1e-06
score_cap = 50.0
rope_base = 10000.0
exp2_cap = score_cap / math.log(2.0)

bf16 = jnp.bfloat16
f32 = jnp.float32

X, C, Y, ZL, ZH = 1, 2, 4, 8, 16
KEY_CHUNK = 512


def swap(value, mask):
    count = lax.axis_size("dp") * lax.axis_size("tensor")
    return lax.ppermute(value, ("dp", "tensor"), [(i, i ^ mask) for i in range(count)])


def device_index():
    return lax.axis_index("dp") * lax.axis_size("tensor") + lax.axis_index("tensor")


def bit(mask):
    return (device_index() // mask) % 2


def outer_masks():
    masks, mask = [], 2 * ZH
    while mask < lax.axis_size("dp") * lax.axis_size("tensor"):
        masks.append(mask)
        mask *= 2
    return masks


def pick(value, index, axis):
    return lax.dynamic_index_in_dim(value, index, axis, keepdims=False)


def ordered_stack(own, other, mask, axis):
    first = bit(mask) == 0
    return jnp.stack([jnp.where(first, own, other), jnp.where(first, other, own)], axis=axis)


def join(own, mask):
    stacked = ordered_stack(own, swap(own, mask), mask, 0)
    return stacked.reshape((2 * own.shape[0],) + own.shape[1:])


def halve(value, mask):
    half = value.reshape((2, value.shape[0] // 2) + value.shape[1:])
    here = bit(mask)
    sent = pick(half, 1 - here, 0).astype(bf16)
    return pick(half, here, 0).astype(f32) + swap(sent, mask).astype(f32)


def spread_rows(rows):
    return jnp.concatenate([rows, swap(rows, X), swap(rows, ZL), swap(rows, X | ZL)], axis=0)


def return_rows(own, others):
    count = own.shape[0]
    total = own
    for place, mask in enumerate((X, ZL, X | ZL)):
        part = others[place * count : (place + 1) * count]
        total = total + swap(part, mask).astype(f32)
    return total


def rms_scale(values, gain_vec):
    return (
        values
        * lax.rsqrt(jnp.mean(values * values, axis=-1, keepdims=True) + norm_eps)
        * (1.0 + gain_vec)
    )


def rotate(values, cosine, sine):
    half = HEAD_DIM // 2
    front, back = values[:, :half], values[:, half:]
    return jnp.concatenate([front * cosine - back * sine, back * cosine + front * sine], axis=-1)


def gelu_times(gate_part, up_part):
    return jax.nn.gelu(gate_part, approximate=True) * up_part


def mm(left, right):
    return jnp.dot(left, right, preferred_element_type=f32)


def contract_rows(left, right):
    return lax.dot_general(left, right, (((0,), (0,)), ((), ())), preferred_element_type=f32)


def contract_cols(left, right):
    return lax.dot_general(left, right, (((1,), (1,)), ((), ())), preferred_element_type=f32)


def visible_mask(base, row_count, limit):
    key_pos = lax.broadcasted_iota(jnp.int32, (row_count, limit.shape[1]), 0) + base
    return key_pos <= limit


def attend_kernel(base_ref, limit_ref, q_ref, k_ref, v_ref, o_ref, ob_ref, lse_ref, acc, total):
    step = pl.program_id(0)
    tokens = q_ref.shape[0]

    @pl.when(step == 0)
    def _():
        acc[...] = jnp.zeros_like(acc)
        total[...] = jnp.zeros_like(total)

    limit = limit_ref[...]
    for head in range(2):
        query = q_ref[:, head * HEAD_DIM : (head + 1) * HEAD_DIM]
        scores = contract_cols(k_ref[...], query)
        weights = jnp.exp2(jnp.tanh(scores * (1.0 / score_cap)) * exp2_cap)
        parts = []
        for sub in range(KEY_CHUNK // 128):
            base = base_ref[step * (KEY_CHUNK // 128) + sub]
            parts.append(
                jnp.where(visible_mask(base, 128, limit), weights[sub * 128 : (sub + 1) * 128], 0.0)
            )
        weights = jnp.concatenate(parts, axis=0)
        total[head * 8 : (head + 1) * 8] += jnp.sum(weights.reshape(KEY_CHUNK // 8, 8, tokens), axis=0)
        acc[head] += contract_rows(v_ref[...], weights.astype(bf16))

    @pl.when(step == pl.num_programs(0) - 1)
    def _():
        for head in range(2):
            denominator = jnp.sum(total[head * 8 : (head + 1) * 8], axis=0, keepdims=True)
            lse_ref[head : head + 1] = jnp.log2(denominator)
            mixed = (acc[head] * (1.0 / denominator)).T
            o_ref[:, head * HEAD_DIM : (head + 1) * HEAD_DIM] = mixed
            ob_ref[:, head * HEAD_DIM : (head + 1) * HEAD_DIM] = mixed.astype(bf16)


def attend(base, limit, query, keys, values):
    tokens, width = query.shape
    steps = keys.shape[0] // KEY_CHUNK
    whole = lambda shape: pl.BlockSpec(shape, lambda i: (0, 0))
    rows = pl.BlockSpec((KEY_CHUNK, HEAD_DIM), lambda i: (i, 0))
    area = keys.shape[0] * tokens * 2
    return pl.pallas_call(
        attend_kernel,
        grid=(steps,),
        in_specs=[
            pl.BlockSpec(memory_space=pltpu.SMEM),
            whole((1, tokens)),
            whole((tokens, width)),
            rows,
            rows,
        ],
        out_specs=[whole((tokens, width)), whole((tokens, width)), whole((2, tokens))],
        out_shape=[
            jax.ShapeDtypeStruct((tokens, width), f32),
            jax.ShapeDtypeStruct((tokens, width), bf16),
            jax.ShapeDtypeStruct((2, tokens), f32),
        ],
        scratch_shapes=[
            pltpu.VMEM((2, HEAD_DIM, tokens), f32),
            pltpu.VMEM((16, tokens), f32),
        ],
        compiler_params=pltpu.CompilerParams(
            dimension_semantics=("arbitrary",), vmem_limit_bytes=48 * 2**20
        ),
        cost_estimate=pl.CostEstimate(
            flops=4 * area * HEAD_DIM, bytes_accessed=8 * 2**20, transcendentals=2 * area
        ),
        name="attend",
    )(base, limit, query, keys, values)


def attend_back_kernel(
    base_ref, limit_ref, lse_ref, delta_ref, q_ref, do_ref, k_ref, v_ref, dq_ref, dkv_ref, acc
):
    step = pl.program_id(0)

    @pl.when(step == 0)
    def _():
        acc[...] = jnp.zeros_like(acc)

    limit = limit_ref[...]
    key_grad = None
    for head in range(2):
        cols = slice(head * HEAD_DIM, (head + 1) * HEAD_DIM)
        query, mixed_grad = q_ref[:, cols], do_ref[:, cols]
        scores = contract_cols(k_ref[...], query)
        slope = jnp.tanh(scores * (1.0 / score_cap))
        probs = jnp.exp2(slope * exp2_cap - lse_ref[head : head + 1])
        parts = []
        for sub in range(KEY_CHUNK // 128):
            base = base_ref[step * (KEY_CHUNK // 128) + sub]
            parts.append(
                jnp.where(visible_mask(base, 128, limit), probs[sub * 128 : (sub + 1) * 128], 0.0)
            )
        probs = jnp.concatenate(parts, axis=0)
        prob_grad = contract_cols(v_ref[...], mixed_grad)
        raw_grad = (probs * (prob_grad - delta_ref[head : head + 1]) * (1.0 - slope * slope)).astype(bf16)
        value_part = mm(probs.astype(bf16), mixed_grad)
        key_part = mm(raw_grad, query)
        if head == 0:
            key_grad, value_grad = key_part, value_part
        else:
            key_grad, value_grad = key_grad + key_part, value_grad + value_part
        acc[head] += contract_rows(k_ref[...], raw_grad)
    dkv_ref[:, :HEAD_DIM] = key_grad
    dkv_ref[:, HEAD_DIM:] = value_grad

    @pl.when(step == pl.num_programs(0) - 1)
    def _():
        for head in range(2):
            dq_ref[:, head * HEAD_DIM : (head + 1) * HEAD_DIM] = (acc[head] * HEAD_DIM ** (-0.5)).T


def attend_back(base, limit, lse, delta, query, mixed_grad, keys, values):
    tokens, width = query.shape
    steps = keys.shape[0] // KEY_CHUNK
    whole = lambda shape: pl.BlockSpec(shape, lambda i: (0, 0))
    rows = pl.BlockSpec((KEY_CHUNK, HEAD_DIM), lambda i: (i, 0))
    area = keys.shape[0] * tokens * 2
    return pl.pallas_call(
        attend_back_kernel,
        grid=(steps,),
        in_specs=[
            pl.BlockSpec(memory_space=pltpu.SMEM),
            whole((1, tokens)),
            whole((2, tokens)),
            whole((2, tokens)),
            whole((tokens, width)),
            whole((tokens, width)),
            rows,
            rows,
        ],
        out_specs=[
            whole((tokens, width)),
            pl.BlockSpec((KEY_CHUNK, 2 * HEAD_DIM), lambda i: (i, 0)),
        ],
        out_shape=[
            jax.ShapeDtypeStruct((tokens, width), f32),
            jax.ShapeDtypeStruct((keys.shape[0], 2 * HEAD_DIM), f32),
        ],
        scratch_shapes=[pltpu.VMEM((2, HEAD_DIM, tokens), f32)],
        compiler_params=pltpu.CompilerParams(
            dimension_semantics=("arbitrary",), vmem_limit_bytes=48 * 2**20
        ),
        cost_estimate=pl.CostEstimate(
            flops=10 * area * HEAD_DIM, bytes_accessed=16 * 2**20, transcendentals=2 * area
        ),
        name="attend_back",
    )(base, limit, lse, delta, query, mixed_grad, keys, values)


def gather_attention_weight(piece):
    rows = piece.shape[0]
    here = bit(ZL)
    own = pick(piece, here, 1)
    got = swap(pick(piece, 1 - here, 1), ZL)
    full = ordered_stack(own, got, ZL, 0).reshape(2 * rows, -1)
    full = join(full, ZH)
    full = join(full, Y)
    block = full.reshape(8, rows, -1)
    full = ordered_stack(block, swap(block, C), C, 1).reshape(16 * rows, -1)
    for mask in outer_masks():
        full = join(full, mask)
    return full


def reduce_attention_grad(value):
    for mask in reversed(outer_masks()):
        value = halve(value, mask)
    rows = value.shape[0] // 16
    here = bit(C)
    split = value.reshape(8, 2, rows, -1)
    sent = pick(split, 1 - here, 1).astype(bf16)
    value = (pick(split, here, 1).astype(f32) + swap(sent, C).astype(f32)).reshape(8 * rows, -1)
    value = halve(value, Y)
    value = halve(value, ZH)
    half = value.astype(bf16).reshape(2, rows, -1)
    here = bit(ZL)
    own = pick(half, here, 0)
    got = swap(pick(half, 1 - here, 0), ZL)
    return ordered_stack(own, got, ZL, 1).astype(f32)


def gather_ffn_weight(piece):
    rows = piece.shape[0]
    split = piece.reshape(rows, 2, 2, -1)
    here = bit(ZL)
    own = pick(split, here, 1)
    got = swap(pick(split, 1 - here, 1), ZL)
    split = ordered_stack(own, got, ZL, 0)
    here = bit(C)
    own = pick(split, here, 2)
    got = swap(pick(split, 1 - here, 2), C)
    full = ordered_stack(own, got, C, 1).reshape(4 * rows, -1)
    full = join(full, ZH)
    full = join(full, Y)
    for mask in outer_masks():
        full = join(full, mask)
    return full


def reduce_ffn_grad(left, right):
    masks = list(reversed(outer_masks())) + [Y, ZH]
    half_width = left.shape[1] // 2
    here = bit(masks[0])
    sent = contract_rows(lax.dynamic_slice_in_dim(left, (1 - here) * half_width, half_width, 1), right)
    got = swap(sent.astype(bf16), masks[0])
    kept = contract_rows(lax.dynamic_slice_in_dim(left, here * half_width, half_width, 1), right)
    value = kept + got.astype(f32)
    for mask in masks[1:]:
        value = halve(value, mask)
    rows = value.shape[0] // 4
    split = value.astype(bf16).reshape(2, 2, rows, -1)
    here = bit(ZL)
    own = pick(split, here, 0)
    got = swap(pick(split, 1 - here, 0), ZL)
    split = ordered_stack(own, got, ZL, 0)
    here = bit(C)
    own = pick(split, here, 1)
    got = swap(pick(split, 1 - here, 1), C)
    split = ordered_stack(own, got, C, 1)
    return jnp.concatenate(
        [split[a, b].astype(f32) for a in range(2) for b in range(2)], axis=1
    )


def reduce_gains(value):
    value = value.T
    for mask in list(reversed(outer_masks())) + [Y, ZH, ZL, C]:
        half = value.reshape((2, value.shape[0] // 2) + value.shape[1:])
        here = bit(mask)
        value = pick(half, here, 0) + swap(pick(half, 1 - here, 0), mask)
    return (value + swap(value, X)).T


def body(
    tokens,
    cotangent,
    prefix,
    q_weight,
    k_weight,
    v_weight,
    out_weight,
    gate_weight,
    up_weight,
    down_weight,
    attn_gain,
    post_attn_gain,
    ffn_gain,
    post_ffn_gain,
):
    own_rows, width = tokens.shape
    rows = q_weight.shape[0]
    outer = lax.axis_size("dp") // 16
    me = device_index()

    def permuted(value):
        lead = value.shape[0]
        split = value.reshape(lead, outer, 4, 2, 2 * rows)
        return split.swapaxes(2, 3).reshape(lead, width)

    def restored(value):
        lead = value.shape[0]
        split = value.reshape(lead, outer, 2, 4, 2 * rows)
        return split.swapaxes(2, 3).reshape(lead, width)

    gains_own = jnp.stack([attn_gain, post_attn_gain, ffn_gain, post_ffn_gain]).astype(bf16)
    gains = permuted(lax.all_gather(gains_own, "dp", axis=1, tiled=True)).astype(f32)
    gain_one, gain_two, gain_three, gain_four = (gains[i] for i in range(4))

    q_split = q_weight.astype(bf16).reshape(rows, 2, -1)
    k_split = k_weight.astype(bf16).reshape(rows, 2, -1)
    v_split = v_weight.astype(bf16).reshape(rows, 2, -1)
    qkv_full = gather_attention_weight(jnp.concatenate([q_split, k_split, v_split], axis=2))
    out_full = gather_attention_weight(out_weight.T.astype(bf16).reshape(rows, 2, -1))
    gate_full = gather_ffn_weight(gate_weight.astype(bf16))
    up_full = gather_ffn_weight(up_weight.astype(bf16))
    down_full = gather_ffn_weight(down_weight.T.astype(bf16))

    row_bases = [((me ^ mask) * own_rows) % SEQ_LEN for mask in (0, X, ZL, X | ZL)]
    lane = jnp.arange(own_rows, dtype=jnp.int32)
    query_pos = jnp.concatenate([base + lane for base in row_bases])
    key_bases = []
    for group in range(8):
        flips = (ZH if group & 1 else 0) | (Y if group & 2 else 0) | (C if group & 4 else 0)
        for mask in (0, X, ZL, X | ZL):
            key_bases.append(((me ^ (flips | mask)) * own_rows) % SEQ_LEN)
    key_bases = jnp.stack(key_bases).astype(jnp.int32)
    prefix_len = lax.dynamic_index_in_dim(prefix, me // 32, 0, keepdims=False)
    limit = jnp.maximum(query_pos, prefix_len - 1)[None, :].astype(jnp.int32)
    half = HEAD_DIM // 2
    frequency = rope_base ** (-2.0 * jnp.arange(half).astype(f32) / HEAD_DIM)
    angles = query_pos.astype(f32)[:, None] * frequency[None, :]
    cosine, sine = jnp.cos(angles), jnp.sin(angles)

    resid = permuted(tokens).astype(f32)
    upstream = permuted(cotangent).astype(f32)

    hidden_one = spread_rows(rms_scale(resid, gain_one).astype(bf16))
    projected = mm(hidden_one, qkv_full)
    scale = HEAD_DIM ** (-0.5)
    query_rot = jnp.concatenate(
        [
            rotate(projected[:, :HEAD_DIM], cosine, sine).astype(bf16) * bf16(scale),
            rotate(projected[:, HEAD_DIM : 2 * HEAD_DIM], cosine, sine).astype(bf16) * bf16(scale),
        ],
        axis=1,
    )
    keys = rotate(projected[:, 2 * HEAD_DIM : 3 * HEAD_DIM], cosine, sine).astype(bf16)
    values = projected[:, 3 * HEAD_DIM :].astype(bf16)
    for mask in (ZH, Y, C):
        keys = jnp.concatenate([keys, swap(keys, mask)], axis=0)
        values = jnp.concatenate([values, swap(values, mask)], axis=0)
    mixed, mixed_low, lse = attend(key_bases, limit, query_rot, keys, values)
    attn_others = contract_cols(mixed_low[own_rows:], out_full).astype(bf16)
    attn_own = contract_cols(mixed_low[:own_rows], out_full)
    attn_sum = return_rows(attn_own, attn_others)
    resid_two = resid + rms_scale(attn_sum, gain_two)

    hidden_two = spread_rows(rms_scale(resid_two, gain_three).astype(bf16))
    hidden_two = jnp.concatenate([hidden_two, swap(hidden_two, C)], axis=0)
    gate_part = mm(hidden_two, gate_full)
    up_part = mm(hidden_two, up_full)
    inner = gelu_times(gate_part, up_part).astype(bf16)

    def share_out(parts):
        group = parts[0][0].shape[0] // 2

        def product(low, high):
            total = contract_cols(parts[0][0][low:high], parts[0][1])
            for left, right in parts[1:]:
                total = total + contract_cols(left[low:high], right)
            return total

        got = swap(product(group, 2 * group).astype(bf16), C)
        total = product(0, group) + got.astype(f32)
        return return_rows(total[:own_rows], total[own_rows:].astype(bf16))

    ffn_sum = share_out([(inner, down_full)])
    layer_out = resid_two + rms_scale(ffn_sum, gain_four)

    unused_out, post_ffn_pull = jax.vjp(rms_scale, ffn_sum, gain_four)
    ffn_grad, gain_four_grad = post_ffn_pull(upstream)
    ffn_grad_rows = spread_rows(ffn_grad.astype(bf16))
    ffn_grad_rows = jnp.concatenate([ffn_grad_rows, swap(ffn_grad_rows, C)], axis=0)
    inner_grad = mm(ffn_grad_rows, down_full)
    unused_inner, gelu_pull = jax.vjp(gelu_times, gate_part, up_part)
    gate_grad_part, up_grad_part = gelu_pull(inner_grad)
    gate_grad_part = gate_grad_part.astype(bf16)
    up_grad_part = up_grad_part.astype(bf16)
    normed_three_grad = share_out([(gate_grad_part, gate_full), (up_grad_part, up_full)])
    down_block = reduce_ffn_grad(ffn_grad_rows, inner)
    gate_block = reduce_ffn_grad(hidden_two, gate_grad_part)
    up_block = reduce_ffn_grad(hidden_two, up_grad_part)
    unused_three, ffn_norm_pull = jax.vjp(rms_scale, resid_two, gain_three)
    resid_two_extra, gain_three_grad = ffn_norm_pull(normed_three_grad)
    resid_two_grad = upstream + resid_two_extra

    unused_two, post_attn_pull = jax.vjp(rms_scale, attn_sum, gain_two)
    attn_grad, gain_two_grad = post_attn_pull(resid_two_grad)
    attn_grad_rows = spread_rows(attn_grad.astype(bf16))
    mixed_grad = mm(attn_grad_rows, out_full).astype(bf16)
    delta = jnp.sum(
        (mixed_grad.astype(f32) * mixed).reshape(-1, 2, HEAD_DIM), axis=-1
    ).T
    query_grad, key_value_grad = attend_back(
        key_bases, limit, lse, delta, query_rot, mixed_grad, keys, values
    )
    for mask in (C, Y, ZH):
        count = key_value_grad.shape[0] // 2
        got = swap(key_value_grad[count:].astype(bf16), mask)
        key_value_grad = key_value_grad[:count].astype(f32) + got.astype(f32)
    out_block = reduce_attention_grad(contract_rows(attn_grad_rows, mixed_low))
    qkv_grad = jnp.concatenate(
        [
            rotate(query_grad[:, :HEAD_DIM], cosine, -sine),
            rotate(query_grad[:, HEAD_DIM:], cosine, -sine),
            rotate(key_value_grad[:, :HEAD_DIM], cosine, -sine),
            key_value_grad[:, HEAD_DIM:],
        ],
        axis=1,
    ).astype(bf16)
    normed_others = contract_cols(qkv_grad[own_rows:], qkv_full).astype(bf16)
    normed_own = contract_cols(qkv_grad[:own_rows], qkv_full)
    normed_one_grad = return_rows(normed_own, normed_others)
    qkv_block = reduce_attention_grad(contract_rows(hidden_one, qkv_grad))
    unused_one, attn_norm_pull = jax.vjp(rms_scale, resid, gain_one)
    resid_extra, gain_one_grad = attn_norm_pull(normed_one_grad)
    input_grad = restored(resid_two_grad + resid_extra)
    gain_rows = reduce_gains(
        jnp.stack([gain_one_grad, gain_two_grad, gain_three_grad, gain_four_grad])
    )
    return (
        restored(layer_out.astype(bf16)),
        input_grad,
        qkv_block[:, :, : 2 * HEAD_DIM].reshape(rows, -1),
        qkv_block[:, :, 2 * HEAD_DIM : 3 * HEAD_DIM].reshape(rows, -1),
        qkv_block[:, :, 3 * HEAD_DIM :].reshape(rows, -1),
        out_block.reshape(rows, -1).T,
        gate_block,
        up_block,
        down_block.T,
        gain_rows[0],
        gain_rows[1],
        gain_rows[2],
        gain_rows[3],
    )


def solution(mesh):
    weight_specs = (
        P("dp", "tensor"),
        P("dp", "tensor"),
        P("dp", "tensor"),
        P("tensor", "dp"),
        P("dp", "tensor"),
        P("dp", "tensor"),
        P("tensor", "dp"),
        P("dp"),
        P("dp"),
        P("dp"),
        P("dp"),
    )
    rows_spec = P(("dp", "tensor"), None)
    return jax.shard_map(
        body,
        mesh=mesh,
        in_specs=(rows_spec, rows_spec, P()) + weight_specs,
        out_specs=(rows_spec, rows_spec) + weight_specs,
        check_vma=False,
    )
```

time: 3290 us -> 1220 us (0.37)
  waiting for transfers between devices: 1900 us -> 790 us
  starting transfers between devices: 659 us -> 75.1 us
  blocking collectives: 214 us -> 23.2 us
  matrix products: 254 us -> 115 us
  other arithmetic: 143 us -> 81.7 us
    all_to_all x14 -> x0, waiting for transfers between devices: 996 us -> none  [reduce_tokens(): lax.all_to_all(arranged.astype(jnp.bfloat16), 'dp', split_axis=0, concat_...]
    all_gather x8 -> x0, waiting for transfers between devices: 455 us -> none  [the longest x2 297 us: fetch(): lax.all_gather(rows_part, 'dp', axis=0, tiled=True)]
    ppermute x60 -> x82, waiting for transfers between devices: 363 us -> 790 us  [swap(): lax.ppermute(value, ('dp', 'tensor'), [(i, i ^ mask) for i in range(count)])]
    all_to_all x14 -> x0, starting transfers between devices: 309 us -> none  [reduce_tokens(): lax.all_to_all(arranged.astype(jnp.bfloat16), 'dp', split_axis=0, concat_...]
    ppermute x60 -> x82, starting transfers between devices: 348 us -> 75.1 us  [swap(): lax.ppermute(value, ('dp', 'tensor'), [(i, i ^ mask) for i in range(count)])]
    unnamed x1 -> x0, blocking collectives: 170 us -> none
    dot_general x10 -> x5, matrix products: 137 us -> 39 us  [mm(): return jnp.dot(left, right, preferred_element_type=f32)]
    reduce_scatter x4 -> x0, waiting for transfers between devices: 84.1 us -> none  [the longest x2 49 us: sum_rows(): return lax.psum_scatter(values, 'tensor', scatter_dimension=0, tiled=True)]
  transfers between devices with their start and end apart: 86 -> 82, of which waited for: 47 -> 44; matrix products, arithmetic and copies ran while one was open for 13% -> 17% of each run, Pallas kernels for 0% -> 3%
where the time goes in v1:
time: 1220 us; the launch traced here: 1210 us
  waiting for transfers between devices  790 us (65%)
  matrix products  115 us (9%)
  local copies, waits for them, and re-layouts  88.1 us (7%)
  other arithmetic  81.7 us (7%)
  starting transfers between devices  75.1 us (6%)
  Pallas kernels  32.1 us (3%)
  blocking collectives  23.2 us (2%)
    ppermute x82, waiting for transfers between devices, swap(): lax.ppermute(value, ('dp', 'tensor'), [(i, i ^ mask) for i in range(count)])  790 us
    ppermute x82, starting transfers between devices, swap(): lax.ppermute(value, ('dp', 'tensor'), [(i, i ^ mask) for i in range(count)])  75.1 us
    dot_general x5, matrix products, mm(): return jnp.dot(left, right, preferred_element_type=f32)  39 us
    dot_general x10, matrix products, contract_cols(): lax.dot_general(left, right, (((1,), (1,)), ((), ())), preferred_element_...  38.3 us
    dot_general x8, matrix products, contract_rows(): lax.dot_general(left, right, (((0,), (0,)), ((), ())), preferred_element_...  37.5 us
    unnamed x239, local copies, waits for them, and re-layouts  26.3 us
    another operation x42, other arithmetic, ordered_stack(): jnp.stack([jnp.where(first, own, other), jnp.where(first, other, own)], a...  25.6 us
  transfers between devices with their start and end apart: 82, of which 44 were waited for; matrix products, arithmetic and copies ran while one was open for 17% of the time, Pallas kernels for 3%

profile of v1, /device:TPU:0, one launch (start us, length us, event | category | flops | bytes accessed | tf_op | source)
XLA Modules:
  0.0 1209.1 jit_solution(17508041215779946399)
XLA Ops:
  2.6 23.2 %all-gather = bf16[16,144,4]{1,2,0:T(4,128)(2,1)S(1)} all-gather(bf16[1,144,4]{1,2,0:T(4,128)(2,1)S(1)} %maximum_bitcast_fusion.1), channel_id=1, replica_groups=mesh['dp'=16,'tensor'=2] {'dp'}, dimensions={0}, use_global_device_ids=true | all-gather | bytes 19584 | tf_op jit(solution)/shard_map/all_gather | solution.py:382
  40.6 3.1 reshape.430
  48.6 3.1 reshape.434
  54.6 4.1 reshape.438
  58.7 4.4 constant_dynamic-slice_fusion.9
  71.9 26.9 %collective-permute-done.14 = bf16[288,512]{1,0:T(8,128)(2,1)S(1)} collective-permute-done((bf16[288,512]{1,0:T(8,128)(2,1)S(1)}, bf16[288,512]{1,0:T(8,128)(2,1)S(1)}, u32[]{:S(2)}, u32[]{:S(2)}) %collective-permute-start.14) | collective-permute-done | bytes 294944 | tf_op jit(solution)/shard_map/ppermute | solution.py:28
  99.1 3.4 collective-permute-start.4
  104.1 24.7 %collective-permute-done.32 = bf16[144,2,1152]{2,0,1:T(8,128)(2,1)S(1)} collective-permute-done((bf16[144,2,1152]{2,0,1:T(8,128)(2,1)S(1)}, bf16[144,2,1152]{2,0,1:T(8,128)(2,1)S(1)}, u32[]{:S(2)}, u32[]{:S(2)}) %collective-permute-start.32) | collective-permute-done | bytes 663584 | tf_op jit(solution)/shard_map/ppermute | solution.py:28
  133.4 25.6 %collective-permute-done.5 = bf16[576,1024]{1,0:T(8,128)(2,1)S(1)} collective-permute-done((bf16[576,1024]{1,0:T(8,128)(2,1)S(1)}, bf16[576,1024]{1,0:T(8,128)(2,1)S(1)}, u32[]{:S(2)}, u32[]{:S(2)}) %collective-permute-start.5) | collective-permute-done | bytes 1179680 | tf_op jit(solution)/shard_map/ppermute | solution.py:28
  159.9 62.7 %collective-permute-done.30 = bf16[576,1152]{1,0:T(8,128)(2,1)S(1)} collective-permute-done((bf16[576,1152]{1,0:T(8,128)(2,1)S(1)}, bf16[576,1152]{1,0:T(8,128)(2,1)S(1)}, u32[]{:S(2)}, u32[]{:S(2)}) %collective-permute-start.30) | collective-permute-done | bytes 1327136 | tf_op jit(solution)/shard_map/ppermute | solution.py:28
  224.0 26.2 %collective-permute-done.26 = bf16[576,1152]{1,0:T(8,128)(2,1)S(1)} collective-permute-done((bf16[576,1152]{1,0:T(8,128)(2,1)S(1)}, bf16[576,1152]{1,0:T(8,128)(2,1)S(1)}, u32[]{:S(2)}, u32[]{:S(2)}) %collective-permute-start.26) | collective-permute-done | bytes 1327136 | tf_op jit(solution)/shard_map/ppermute | solution.py:28
  253.9 5.0 fusion.85
  263.7 51.1 %collective-permute-done.34 = bf16[576,1152]{1,0:T(8,128)(2,1)S(1)} collective-permute-done((bf16[576,1152]{1,0:T(8,128)(2,1)S(1)}, bf16[576,1152]{1,0:T(8,128)(2,1)S(1)}, u32[]{:S(2)}, u32[]{:S(2)}) %collective-permute-start.34) | collective-permute-done | bytes 1327136 | tf_op jit(solution)/shard_map/ppermute | solution.py:28
  315.4 10.7 collective-permute-done.7
  333.2 46.5 %collective-permute-done.8 = bf16[1024,256]{1,0:T(8,128)(2,1)S(1)} collective-permute-done((bf16[1024,256]{1,0:T(8,128)(2,1)S(1)}, bf16[1024,256]{1,0:T(8,128)(2,1)S(1)}, u32[]{:S(2)}, u32[]{:S(2)}) %collective-permute-start.8) | collective-permute-done | bytes 524320 | tf_op jit(solution)/shard_map/ppermute | solution.py:28
  379.8 66.2 %collective-permute-done.11 = bf16[1024,256]{1,0:T(8,128)(2,1)S(1)} collective-permute-done((bf16[1024,256]{1,0:T(8,128)(2,1)S(1)}, bf16[1024,256]{1,0:T(8,128)(2,1)S(1)}, u32[]{:S(2)}, u32[]{:S(2)}) %collective-permute-start.11) | collective-permute-done | bytes 524320 | tf_op jit(solution)/shard_map/ppermute | solution.py:28
  446.2 4.6 select_bitcast_fusion.5
  455.0 11.6 attend.1
  473.8 22.5 %collective-permute-done.17 = bf16[128,2304]{1,0:T(8,128)(2,1)S(1)} collective-permute-done((bf16[128,2304]{1,0:T(8,128)(2,1)S(1)}, bf16[128,2304]{1,0:T(8,128)(2,1)S(1)}, u32[]{:S(2)}, u32[]{:S(2)}) %collective-permute-start.17) | collective-permute-done | bytes 589856 | tf_op jit(solution)/shard_map/ppermute | solution.py:28
  507.6 10.6 collective-permute-done.22
  518.2 10.8 collective-permute-done.21
  529.4 3.2 pad_maximum_fusion.1
  536.2 3.4 constant_dynamic-update-slice_fusion.3
  539.7 8.5 fusion.188
  548.2 8.3 multiply_convert_fusion.1
  556.5 3.5 convolution_convert_fusion.3
  560.6 4.2 collective-permute-done.36
  564.8 4.9 fusion.186
  579.0 20.5 %collective-permute-done.37 = bf16[128,2304]{1,0:T(8,128)(2,1)} collective-permute-done((bf16[128,2304]{1,0:T(8,128)(2,1)}, bf16[128,2304]{1,0:T(8,128)(2,1)}, u32[]{:S(2)}, u32[]{:S(2)}) %collective-permute-start.37) | collective-permute-done | bytes 589856 | tf_op jit(solution)/shard_map/ppermute | solution.py:28
  608.6 13.4 %collective-permute-done.42 = bf16[128,2304]{1,0:T(8,128)(2,1)S(1)} collective-permute-done((bf16[128,2304]{1,0:T(8,128)(2,1)S(1)}, bf16[128,2304]{1,0:T(8,128)(2,1)S(1)}, u32[]{:S(2)}, u32[]{:S(2)}) %collective-permute-start.42) | collective-permute-done | bytes 589856 | tf_op jit(solution)/shard_map/ppermute | solution.py:28
  622.0 10.7 collective-permute-done.41
  645.1 3.4 constant_dynamic-update-slice_fusion.8
  648.5 15.8 %fusion.7 = (bf16[1024,1152]{1,0:T(8,128)(2,1)}, bf16[1024,1152]{1,0:T(8,128)(2,1)S(1)}) fusion(f32[1024,1152]{1,0:T(8,128)} %copy-done.85, f32[1024,1152]{1,0:T(8,128)} %get-tuple-element.214, bf16[1024,2304]{1,0:T(8,128)(2,1)} %constant_dynamic-update-slice_fusion.8, bf16[2304,1152]{1,0:T(8,128)(2,1)} %bitcast.563), kind=kOutput, calls=%fused_computation.20 | convolution fusion | flops 5464129536 | bytes 24182784 | tf_op jit(solution)/shard_map/dot_general | solution.py:100
  664.4 4.9 fusion.30
  669.3 6.4 fusion.8
  676.3 4.8 convolution_convert_fusion
  682.8 6.5 convolution_convert_fusion.2
  689.3 4.9 convolution_convert_fusion.1
  696.2 4.9 fusion.33
  701.1 6.4 fusion.187
  710.8 31.1 %collective-permute-done.73 = bf16[1152,1152]{1,0:T(8,128)(2,1)} collective-permute-done((bf16[1152,1152]{1,0:T(8,128)(2,1)}, bf16[1152,1152]{1,0:T(8,128)(2,1)}, u32[]{:S(2)}, u32[]{:S(2)}) %collective-permute-start.73) | collective-permute-done | bytes 2654240 | tf_op jit(solution)/shard_map/ppermute | solution.py:28
  744.1 5.1 convolution_add_fusion
  750.5 48.2 %collective-permute-done.69 = bf16[1152,1152]{1,0:T(8,128)(2,1)} collective-permute-done((bf16[1152,1152]{1,0:T(8,128)(2,1)}, bf16[1152,1152]{1,0:T(8,128)(2,1)}, u32[]{:S(2)}, u32[]{:S(2)}) %collective-permute-start.69) | collective-permute-done | bytes 2654240 | tf_op jit(solution)/shard_map/ppermute | solution.py:28
  801.3 5.8 convolution_add_fusion.1
  815.0 39.6 %collective-permute-done.65 = bf16[1152,1152]{1,0:T(8,128)(2,1)S(1)} collective-permute-done((bf16[1152,1152]{1,0:T(8,128)(2,1)}, bf16[1152,1152]{1,0:T(8,128)(2,1)S(1)}, u32[]{:S(2)}, u32[]{:S(2)}) %collective-permute-start.65) | collective-permute-done | bytes 2654240 | tf_op jit(solution)/shard_map/ppermute | solution.py:28
  855.9 3.4 convolution_add_fusion.2
  861.7 10.5 collective-permute-done.50
  872.2 3.8 collective-permute-start.66
  876.0 8.8 collective-permute-done.49
  896.1 20.5 %attend_back.1 = (f32[512,512]{1,0:T(8,128)S(1)}, f32[4096,512]{1,0:T(8,128)}) custom-call(s32[32]{0:T(128)S(1)} %copy-done.7, s32[1,512]{1,0:T(1,128)S(1)} %copy-done.5, f32[2,512]{1,0:T(2,128)S(1)} %get-tuple-element.19.lse_ref, f32[2,512]{1,0:T(2,128)S(1)} %bitcast.525, bf16[512,512]{1,0:T(8,128)(2,1)S(1)} %copy-done.3, ...), custom_call_target="tpu_custom_call" | custom-call | flops 10737418240 | bytes 16777216 | tf_op jit(solution)/shard_map/attend_back/pallas_call | solution.py:234
  928.1 16.9 %collective-permute-done.70 = bf16[576,1152]{1,0:T(8,128)(2,1)} collective-permute-done((bf16[576,1152]{1,0:T(8,128)(2,1)}, bf16[576,1152]{1,0:T(8,128)(2,1)}, u32[]{:S(2)}, u32[]{:S(2)}) %collective-permute-start.70) | collective-permute-done | bytes 1327136 | tf_op jit(solution)/shard_map/ppermute | solution.py:28
  947.6 24.1 %collective-permute-done.66 = bf16[576,1152]{1,0:T(8,128)(2,1)} collective-permute-done((bf16[576,1152]{1,0:T(8,128)(2,1)}, bf16[576,1152]{1,0:T(8,128)(2,1)}, u32[]{:S(2)}, u32[]{:S(2)}) %collective-permute-start.66) | collective-permute-done | bytes 1327136 | tf_op jit(solution)/shard_map/ppermute | solution.py:28
  973.4 12.3 %collective-permute-done.75 = bf16[2,144,1152]{2,1,0:T(8,128)(2,1)S(1)} collective-permute-done((bf16[2,144,1152]{2,1,0:T(8,128)(2,1)S(1)}, bf16[2,144,1152]{2,1,0:T(8,128)(2,1)S(1)}, u32[]{:S(2)}, u32[]{:S(2)}) %collective-permute-start.75) | collective-permute-done | bytes 663584 | tf_op jit(solution)/shard_map/ppermute | solution.py:28
  986.0 13.8 %collective-permute-done.71 = bf16[2,144,1152]{2,1,0:T(8,128)(2,1)S(1)} collective-permute-done((bf16[2,144,1152]{2,1,0:T(8,128)(2,1)S(1)}, bf16[2,144,1152]{2,1,0:T(8,128)(2,1)S(1)}, u32[]{:S(2)}, u32[]{:S(2)}) %collective-permute-start.71) | collective-permute-done | bytes 663584 | tf_op jit(solution)/shard_map/ppermute | solution.py:28
  1000.2 13.8 %collective-permute-done.67 = bf16[2,144,1152]{2,1,0:T(8,128)(2,1)S(1)} collective-permute-done((bf16[2,144,1152]{2,1,0:T(8,128)(2,1)S(1)}, bf16[2,144,1152]{2,1,0:T(8,128)(2,1)S(1)}, u32[]{:S(2)}, u32[]{:S(2)}) %collective-permute-start.67) | collective-permute-done | bytes 663584 | tf_op jit(solution)/shard_map/ppermute | solution.py:28
  1017.3 13.5 %collective-permute-done.62 = bf16[576,512]{1,0:T(8,128)(2,1)S(1)} collective-permute-done((bf16[576,512]{1,0:T(8,128)(2,1)S(1)}, bf16[576,512]{1,0:T(8,128)(2,1)S(1)}, u32[]{:S(2)}, u32[]{:S(2)}) %collective-permute-start.62) | collective-permute-done | bytes 589856 | tf_op jit(solution)/shard_map/ppermute | solution.py:28
  1038.7 21.2 %collective-permute-done.52 = bf16[1024,512]{1,0:T(8,128)(2,1)S(1)} collective-permute-done((bf16[1024,512]{1,0:T(8,128)(2,1)S(1)}, bf16[1024,512]{1,0:T(8,128)(2,1)S(1)}, u32[]{:S(2)}, u32[]{:S(2)}) %collective-permute-start.52) | collective-permute-done | bytes 1048608 | tf_op jit(solution)/shard_map/ppermute | solution.py:28
  1063.2 21.8 %collective-permute-done.53 = bf16[512,512]{1,0:T(8,128)(2,1)S(1)} collective-permute-done((bf16[512,512]{1,0:T(8,128)(2,1)S(1)}, bf16[512,512]{1,0:T(8,128)(2,1)S(1)}, u32[]{:S(2)}, u32[]{:S(2)}) %collective-permute-start.53) | collective-permute-done | bytes 524320 | tf_op jit(solution)/shard_map/ppermute | solution.py:28
  1089.9 4.1 fusion.84
  1100.7 22.4 %collective-permute-done.54 = bf16[128,2304]{1,0:T(8,128)(2,1)S(1)} collective-permute-done((bf16[128,2304]{1,0:T(8,128)(2,1)S(1)}, bf16[128,2304]{1,0:T(8,128)(2,1)S(1)}, u32[]{:S(2)}, u32[]{:S(2)}) %collective-permute-start.54) | collective-permute-done | bytes 589856 | tf_op jit(solution)/shard_map/ppermute | solution.py:28
  1132.1 3.9 bitcast_add_fusion
  1148.1 17.3 %collective-permute-done.58 = bf16[576,1024]{1,0:T(8,128)(2,1)} collective-permute-done((bf16[576,1024]{1,0:T(8,128)(2,1)S(1)}, bf16[576,1024]{1,0:T(8,128)(2,1)}, u32[]{:S(2)}, u32[]{:S(2)}) %collective-permute-start.58) | collective-permute-done | bytes 1179680 | tf_op jit(solution)/shard_map/ppermute | solution.py:28
  1178.0 18.0 %collective-permute-done.59 = bf16[288,1024]{1,0:T(8,128)(2,1)} collective-permute-done((bf16[288,1024]{1,0:T(8,128)(2,1)}, bf16[288,1024]{1,0:T(8,128)(2,1)}, u32[]{:S(2)}, u32[]{:S(2)}) %collective-permute-start.59) | collective-permute-done | bytes 589856 | tf_op jit(solution)/shard_map/ppermute | solution.py:28
  1198.0 8.3 collective-permute-done.60
  (602 shorter events, 231.0 us)
Async XLA Ops:
  28.4 224.6 %collective-permute-start.2 = (bf16[128,2304]{1,0:T(8,128)(2,1)}, bf16[128,2304]{1,0:T(8,128)(2,1)}, u32[]{:S(2)}, u32[]{:S(2)}) collective-permute-start(bf16[128,2304]{1,0:T(8,128)(2,1)} %multiply_convert_fusion.3), channel_id=1, source_target_pairs={{0,9},{1,8},{2,11},{3,10},{4,13},{5,12},{6,15},{7,14},{8,1},{9,0},... | collective-permute-start | bytes 1769480 | tf_op jit(solution)/shard_map/ppermute | solution.py:28
  28.4 225.5 %collective-permute-start.1 = (bf16[128,2304]{1,0:T(8,128)(2,1)}, bf16[128,2304]{1,0:T(8,128)(2,1)}, u32[]{:S(2)}, u32[]{:S(2)}) collective-permute-start(bf16[128,2304]{1,0:T(8,128)(2,1)} %multiply_convert_fusion.3), channel_id=1, source_target_pairs={{0,8},{1,9},{2,10},{3,11},{4,12},{5,13},{6,14},{7,15},{8,0},{9,1},... | collective-permute-start | bytes 1769480 | tf_op jit(solution)/shard_map/ppermute | solution.py:28
  33.6 34.0 %collective-permute-start.13 = (bf16[144,512]{1,0:T(8,128)(2,1)}, bf16[144,512]{1,0:T(8,128)(2,1)}, u32[]{:S(2)}, u32[]{:S(2)}) collective-permute-start(bf16[144,512]{1,0:T(8,128)(2,1)} %bitcast.519), channel_id=1, source_target_pairs={{0,8},{1,9},{2,10},{3,11},{4,12},{5,13},{6,14},{7,15},{8,0},{9,1},... | collective-permute-start | bytes 442376 | tf_op jit(solution)/shard_map/ppermute | solution.py:28
  37.4 33.3 %collective-permute-start.3 = (bf16[144,1024]{1,0:T(8,128)(2,1)}, bf16[144,1024]{1,0:T(8,128)(2,1)}, u32[]{:S(2)}, u32[]{:S(2)}) collective-permute-start(bf16[144,1024]{1,0:T(8,128)(2,1)} %bitcast.518), channel_id=1, source_target_pairs={{0,8},{1,9},{2,10},{3,11},{4,12},{5,13},{6,14},{7,15},{8,0},{9,1},... | collective-permute-start | bytes 884744 | tf_op jit(solution)/shard_map/ppermute | solution.py:28
  45.6 53.5 %collective-permute-start.24 = (bf16[144,2,1152]{2,0,1:T(8,128)(2,1)}, bf16[144,2,1152]{2,0,1:T(8,128)(2,1)}, u32[]{:S(2)}, u32[]{:S(2)}) collective-permute-start(bf16[144,2,1152]{2,0,1:T(8,128)(2,1)} %bitcast.517), channel_id=1, source_target_pairs={{0,8},{1,9},{2,10},{3,11},{4,12},{5,13},{6,14},{7,15},{8,0},{9,1},... | collective-permute-start | bytes 1990664 | tf_op jit(solution)/shard_map/ppermute | solution.py:28
  67.6 36.2 %collective-permute-start.28 = (bf16[144,2,1152]{2,0,1:T(8,128)(2,1)}, bf16[144,2,1152]{2,0,1:T(8,128)(2,1)S(1)}, u32[]{:S(2)}, u32[]{:S(2)}) collective-permute-start(bf16[144,2,1152]{2,0,1:T(8,128)(2,1)} %bitcast.610), channel_id=1, source_target_pairs={{0,8},{1,9},{2,10},{3,11},{4,12},{5,13},{6,14},{7,15},{8,0},{9,1},... | collective-permute-start | bytes 1990664 | tf_op jit(solution)/shard_map/ppermute | solution.py:28
  70.7 28.1 %collective-permute-start.14 = (bf16[288,512]{1,0:T(8,128)(2,1)S(1)}, bf16[288,512]{1,0:T(8,128)(2,1)S(1)}, u32[]{:S(2)}, u32[]{:S(2)}) collective-permute-start(bf16[288,512]{1,0:T(8,128)(2,1)S(1)} %bitcast.606), channel_id=1, source_target_pairs={{0,16},{1,17},{2,18},{3,19},{4,20},{5,21},{6,22},{7,23},{8,24},{9,... | collective-permute-start | bytes 884744 | tf_op jit(solution)/shard_map/ppermute | solution.py:28
  98.8 30.0 %collective-permute-start.32 = (bf16[144,2,1152]{2,0,1:T(8,128)(2,1)S(1)}, bf16[144,2,1152]{2,0,1:T(8,128)(2,1)S(1)}, u32[]{:S(2)}, u32[]{:S(2)}) collective-permute-start(bf16[144,2,1152]{2,0,1:T(8,128)(2,1)S(1)} %bitcast.609), channel_id=1, source_target_pairs={{0,8},{1,9},{2,10},{3,11},{4,12},{5,13},{6,14},{7,15},{8,0},{9,1},... | collective-permute-start | bytes 1990664 | tf_op jit(solution)/shard_map/ppermute | solution.py:28
  99.1 30.1 %collective-permute-start.4 = (bf16[288,1024]{1,0:T(8,128)(2,1)S(1)}, bf16[288,1024]{1,0:T(8,128)(2,1)S(1)}, u32[]{:S(2)}, u32[]{:S(2)}) collective-permute-start(bf16[288,1024]{1,0:T(8,128)(2,1)S(1)} %bitcast.599), channel_id=1, source_target_pairs={{0,16},{1,17},{2,18},{3,19},{4,20},{5,21},{6,22},{7,23},{8,24},{9,... | collective-permute-start | bytes 1769480 | tf_op jit(solution)/shard_map/ppermute | solution.py:28
  103.8 26.2 %collective-permute-start.15 = (bf16[576,512]{1,0:T(8,128)(2,1)S(1)}, bf16[576,512]{1,0:T(8,128)(2,1)S(1)}, u32[]{:S(2)}, u32[]{:S(2)}) collective-permute-start(bf16[576,512]{1,0:T(8,128)(2,1)S(1)} %bitcast.600), channel_id=1, source_target_pairs={{0,4},{1,5},{2,6},{3,7},{4,0},{5,1},{6,2},{7,3},{8,12},{9,13},{10,... | collective-permute-start | bytes 1769480 | tf_op jit(solution)/shard_map/ppermute | solution.py:28
  130.9 28.0 %collective-permute-start.5 = (bf16[576,1024]{1,0:T(8,128)(2,1)S(1)}, bf16[576,1024]{1,0:T(8,128)(2,1)S(1)}, u32[]{:S(2)}, u32[]{:S(2)}) collective-permute-start(bf16[576,1024]{1,0:T(8,128)(2,1)S(1)} %bitcast.573), channel_id=1, source_target_pairs={{0,4},{1,5},{2,6},{3,7},{4,0},{5,1},{6,2},{7,3},{8,12},{9,13},{10,... | collective-permute-start | bytes 3538952 | tf_op jit(solution)/shard_map/ppermute | solution.py:28
  131.9 27.5 %collective-permute-start.16 = (bf16[8,144,512]{2,1,0:T(8,128)(2,1)S(1)}, bf16[8,144,512]{2,1,0:T(8,128)(2,1)S(1)}, u32[]{:S(2)}, u32[]{:S(2)}) collective-permute-start(bf16[8,144,512]{2,1,0:T(8,128)(2,1)S(1)} %bitcast.574), channel_id=1, source_target_pairs={{0,2},{1,3},{2,0},{3,1},{4,6},{5,7},{6,4},{7,5},{8,10},{9,11},{10,... | collective-permute-start | bytes 3538952 | tf_op jit(solution)/shard_map/ppermute | solution.py:28
  132.8 89.7 %collective-permute-start.30 = (bf16[576,1152]{1,0:T(8,128)(2,1)S(1)}, bf16[576,1152]{1,0:T(8,128)(2,1)S(1)}, u32[]{:S(2)}, u32[]{:S(2)}) collective-permute-start(bf16[576,1152]{1,0:T(8,128)(2,1)S(1)} %bitcast.565), channel_id=1, source_target_pairs={{0,16},{1,17},{2,18},{3,19},{4,20},{5,21},{6,22},{7,23},{8,24},{9,... | collective-permute-start | bytes 3981320 | tf_op jit(solution)/shard_map/ppermute | solution.py:28
  158.9 91.3 %collective-permute-start.26 = (bf16[576,1152]{1,0:T(8,128)(2,1)S(1)}, bf16[576,1152]{1,0:T(8,128)(2,1)S(1)}, u32[]{:S(2)}, u32[]{:S(2)}) collective-permute-start(bf16[576,1152]{1,0:T(8,128)(2,1)S(1)} %bitcast.566), channel_id=1, source_target_pairs={{0,16},{1,17},{2,18},{3,19},{4,20},{5,21},{6,22},{7,23},{8,24},{9,... | collective-permute-start | bytes 3981320 | tf_op jit(solution)/shard_map/ppermute | solution.py:28
  159.4 91.5 %collective-permute-start.6 = (bf16[8,144,1024]{2,1,0:T(8,128)(2,1)S(1)}, bf16[8,144,1024]{2,1,0:T(8,128)(2,1)S(1)}, u32[]{:S(2)}, u32[]{:S(2)}) collective-permute-start(bf16[8,144,1024]{2,1,0:T(8,128)(2,1)S(1)} %bitcast.539), channel_id=1, source_target_pairs={{0,2},{1,3},{2,0},{3,1},{4,6},{5,7},{6,4},{7,5},{8,10},{9,11},{10,... | collective-permute-start | bytes 7077896 | tf_op jit(solution)/shard_map/ppermute | solution.py:28
  222.6 31.3 %collective-permute-start = (bf16[128,2304]{1,0:T(8,128)(2,1)}, bf16[128,2304]{1,0:T(8,128)(2,1)S(1)}, u32[]{:S(2)}, u32[]{:S(2)}) collective-permute-start(bf16[128,2304]{1,0:T(8,128)(2,1)} %multiply_convert_fusion.3), channel_id=1, source_target_pairs={{0,1},{1,0},{2,3},{3,2},{4,5},{5,4},{6,7},{7,6},{8,9},{9,8},{10,11... | collective-permute-start | bytes 1769480 | tf_op jit(solution)/shard_map/ppermute | solution.py:28
  250.2 64.7 %collective-permute-start.34 = (bf16[576,1152]{1,0:T(8,128)(2,1)S(1)}, bf16[576,1152]{1,0:T(8,128)(2,1)S(1)}, u32[]{:S(2)}, u32[]{:S(2)}) collective-permute-start(bf16[576,1152]{1,0:T(8,128)(2,1)S(1)} %bitcast.564), channel_id=1, source_target_pairs={{0,16},{1,17},{2,18},{3,19},{4,20},{5,21},{6,22},{7,23},{8,24},{9,... | collective-permute-start | bytes 3981320 | tf_op jit(solution)/shard_map/ppermute | solution.py:28
  250.9 195.2 %collective-permute-start.27 = (bf16[1152,1152]{1,0:T(8,128)(2,1)S(1)}, bf16[1152,1152]{1,0:T(8,128)(2,1)}, u32[]{:S(2)}, u32[]{:S(2)}) collective-permute-start(bf16[1152,1152]{1,0:T(8,128)(2,1)S(1)} %bitcast.534), channel_id=1, source_target_pairs={{0,4},{1,5},{2,6},{3,7},{4,0},{5,1},{6,2},{7,3},{8,12},{9,13},{10,... | collective-permute-start | bytes 7962632 | tf_op jit(solution)/shard_map/ppermute | solution.py:28
  253.0 197.8 %collective-permute-start.31 = (bf16[1152,1152]{1,0:T(8,128)(2,1)S(1)}, bf16[1152,1152]{1,0:T(8,128)(2,1)}, u32[]{:S(2)}, u32[]{:S(2)}) collective-permute-start(bf16[1152,1152]{1,0:T(8,128)(2,1)S(1)} %bitcast.533), channel_id=1, source_target_pairs={{0,4},{1,5},{2,6},{3,7},{4,0},{5,1},{6,2},{7,3},{8,12},{9,13},{10,... | collective-permute-start | bytes 7962632 | tf_op jit(solution)/shard_map/ppermute | solution.py:28
  260.8 65.3 %collective-permute-start.7 = (bf16[512,256]{1,0:T(8,128)(2,1)S(1)}, bf16[512,256]{1,0:T(8,128)(2,1)S(1)}, u32[]{:S(2)}, u32[]{:S(2)}) collective-permute-start(bf16[512,256]{1,0:T(8,128)(2,1)S(1)} %pad_maximum_fusion.32), channel_id=1, source_target_pairs={{0,16},{1,17},{2,18},{3,19},{4,20},{5,21},{6,22},{7,23},{8,24},{9,... | collective-permute-start | bytes 786440 | tf_op jit(solution)/shard_map/ppermute | solution.py:28
  326.1 53.5 %collective-permute-start.8 = (bf16[1024,256]{1,0:T(8,128)(2,1)S(1)}, bf16[1024,256]{1,0:T(8,128)(2,1)S(1)}, u32[]{:S(2)}, u32[]{:S(2)}) collective-permute-start(bf16[1024,256]{1,0:T(8,128)(2,1)S(1)} %pad_maximum_fusion.25), channel_id=1, source_target_pairs={{0,4},{1,5},{2,6},{3,7},{4,0},{5,1},{6,2},{7,3},{8,12},{9,13},{10,... | collective-permute-start | bytes 1572872 | tf_op jit(solution)/shard_map/ppermute | solution.py:28
  327.7 143.8 %collective-permute-start.35 = (bf16[1152,1152]{1,0:T(8,128)(2,1)S(1)}, bf16[1152,1152]{1,0:T(8,128)(2,1)}, u32[]{:S(2)}, u32[]{:S(2)}) collective-permute-start(bf16[1152,1152]{1,0:T(8,128)(2,1)S(1)} %bitcast.535), channel_id=1, source_target_pairs={{0,4},{1,5},{2,6},{3,7},{4,0},{5,1},{6,2},{7,3},{8,12},{9,13},{10,... | collective-permute-start | bytes 7962632 | tf_op jit(solution)/shard_map/ppermute | solution.py:28
  331.7 114.4 %collective-permute-start.11 = (bf16[1024,256]{1,0:T(8,128)(2,1)S(1)}, bf16[1024,256]{1,0:T(8,128)(2,1)S(1)}, u32[]{:S(2)}, u32[]{:S(2)}) collective-permute-start(bf16[1024,256]{1,0:T(8,128)(2,1)S(1)} %pad_maximum_fusion.26), channel_id=1, source_target_pairs={{0,4},{1,5},{2,6},{3,7},{4,0},{5,1},{6,2},{7,3},{8,12},{9,13},{10,... | collective-permute-start | bytes 1572872 | tf_op jit(solution)/shard_map/ppermute | solution.py:28
  379.7 73.3 %collective-permute-start.9 = (bf16[2048,256]{1,0:T(8,128)(2,1)S(1)}, bf16[2048,256]{1,0:T(8,128)(2,1)S(1)}, u32[]{:S(2)}, u32[]{:S(2)}) collective-permute-start(bf16[2048,256]{1,0:T(8,128)(2,1)S(1)} %pad_maximum_fusion.20), channel_id=1, source_target_pairs={{0,2},{1,3},{2,0},{3,1},{4,6},{5,7},{6,4},{7,5},{8,10},{9,11},{10,... | collective-permute-start | bytes 3145736 | tf_op jit(solution)/shard_map/ppermute | solution.py:28
  467.9 28.4 %collective-permute-start.17 = (bf16[128,2304]{1,0:T(8,128)(2,1)S(1)}, bf16[128,2304]{1,0:T(8,128)(2,1)S(1)}, u32[]{:S(2)}, u32[]{:S(2)}) collective-permute-start(bf16[128,2304]{1,0:T(8,128)(2,1)S(1)} %get-tuple-element.147), channel_id=1, source_target_pairs={{0,1},{1,0},{2,3},{3,2},{4,5},{5,4},{6,7},{7,6},{8,9},{9,8},{10,11... | collective-permute-start | bytes 1769480 | tf_op jit(solution)/shard_map/ppermute | solution.py:28
  468.7 27.5 %collective-permute-start.19 = (bf16[128,2304]{1,0:T(8,128)(2,1)S(1)}, bf16[128,2304]{1,0:T(8,128)(2,1)S(1)}, u32[]{:S(2)}, u32[]{:S(2)}) collective-permute-start(bf16[128,2304]{1,0:T(8,128)(2,1)S(1)} %get-tuple-element.148), channel_id=1, source_target_pairs={{0,9},{1,8},{2,11},{3,10},{4,13},{5,12},{6,15},{7,14},{8,1},{9,0},... | collective-permute-start | bytes 1769480 | tf_op jit(solution)/shard_map/ppermute | solution.py:28
  471.5 26.0 %collective-permute-start.18 = (bf16[128,2304]{1,0:T(8,128)(2,1)S(1)}, bf16[128,2304]{1,0:T(8,128)(2,1)S(1)}, u32[]{:S(2)}, u32[]{:S(2)}) collective-permute-start(bf16[128,2304]{1,0:T(8,128)(2,1)S(1)} %get-tuple-element.149), channel_id=1, source_target_pairs={{0,8},{1,9},{2,10},{3,11},{4,12},{5,13},{6,14},{7,15},{8,0},{9,1},... | collective-permute-start | bytes 1769480 | tf_op jit(solution)/shard_map/ppermute | solution.py:28
  503.5 25.5 %collective-permute-start.21 = (bf16[128,2304]{1,0:T(8,128)(2,1)S(1)}, bf16[128,2304]{1,0:T(8,128)(2,1)S(1)}, u32[]{:S(2)}, u32[]{:S(2)}) collective-permute-start(bf16[128,2304]{1,0:T(8,128)(2,1)S(1)} %get-tuple-element.91), channel_id=1, source_target_pairs={{0,8},{1,9},{2,10},{3,11},{4,12},{5,13},{6,14},{7,15},{8,0},{9,1},... | collective-permute-start | bytes 1769480 | tf_op jit(solution)/shard_map/ppermute | solution.py:28
  503.5 25.6 %collective-permute-start.20 = (bf16[128,2304]{1,0:T(8,128)(2,1)S(1)}, bf16[128,2304]{1,0:T(8,128)(2,1)S(1)}, u32[]{:S(2)}, u32[]{:S(2)}) collective-permute-start(bf16[128,2304]{1,0:T(8,128)(2,1)S(1)} %get-tuple-element.91), channel_id=1, source_target_pairs={{0,1},{1,0},{2,3},{3,2},{4,5},{5,4},{6,7},{7,6},{8,9},{9,8},{10,11... | collective-permute-start | bytes 1769480 | tf_op jit(solution)/shard_map/ppermute | solution.py:28
  570.9 28.6 %collective-permute-start.37 = (bf16[128,2304]{1,0:T(8,128)(2,1)}, bf16[128,2304]{1,0:T(8,128)(2,1)}, u32[]{:S(2)}, u32[]{:S(2)}) collective-permute-start(bf16[128,2304]{1,0:T(8,128)(2,1)} %get-tuple-element.113), channel_id=1, source_target_pairs={{0,1},{1,0},{2,3},{3,2},{4,5},{5,4},{6,7},{7,6},{8,9},{9,8},{10,11... | collective-permute-start | bytes 1769480 | tf_op jit(solution)/shard_map/ppermute | solution.py:28
  572.2 27.2 %collective-permute-start.39 = (bf16[128,2304]{1,0:T(8,128)(2,1)}, bf16[128,2304]{1,0:T(8,128)(2,1)}, u32[]{:S(2)}, u32[]{:S(2)}) collective-permute-start(bf16[128,2304]{1,0:T(8,128)(2,1)} %get-tuple-element.114), channel_id=1, source_target_pairs={{0,9},{1,8},{2,11},{3,10},{4,13},{5,12},{6,15},{7,14},{8,1},{9,0},... | collective-permute-start | bytes 1769480 | tf_op jit(solution)/shard_map/ppermute | solution.py:28
  574.7 26.0 %collective-permute-start.38 = (bf16[128,2304]{1,0:T(8,128)(2,1)}, bf16[128,2304]{1,0:T(8,128)(2,1)}, u32[]{:S(2)}, u32[]{:S(2)}) collective-permute-start(bf16[128,2304]{1,0:T(8,128)(2,1)} %get-tuple-element.115), channel_id=1, source_target_pairs={{0,8},{1,9},{2,10},{3,11},{4,12},{5,13},{6,14},{7,15},{8,0},{9,1},... | collective-permute-start | bytes 1769480 | tf_op jit(solution)/shard_map/ppermute | solution.py:28
  607.5 25.3 %collective-permute-start.41 = (bf16[128,2304]{1,0:T(8,128)(2,1)S(1)}, bf16[128,2304]{1,0:T(8,128)(2,1)S(1)}, u32[]{:S(2)}, u32[]{:S(2)}) collective-permute-start(bf16[128,2304]{1,0:T(8,128)(2,1)S(1)} %get-tuple-element.87), channel_id=1, source_target_pairs={{0,8},{1,9},{2,10},{3,11},{4,12},{5,13},{6,14},{7,15},{8,0},{9,1},... | collective-permute-start | bytes 1769480 | tf_op jit(solution)/shard_map/ppermute | solution.py:28
  607.6 25.2 %collective-permute-start.40 = (bf16[128,2304]{1,0:T(8,128)(2,1)S(1)}, bf16[128,2304]{1,0:T(8,128)(2,1)S(1)}, u32[]{:S(2)}, u32[]{:S(2)}) collective-permute-start(bf16[128,2304]{1,0:T(8,128)(2,1)S(1)} %get-tuple-element.87), channel_id=1, source_target_pairs={{0,1},{1,0},{2,3},{3,2},{4,5},{5,4},{6,7},{7,6},{8,9},{9,8},{10,11... | collective-permute-start | bytes 1769480 | tf_op jit(solution)/shard_map/ppermute | solution.py:28
  675.8 25.3 %collective-permute-start.44 = (bf16[512,2304]{1,0:T(8,128)(2,1)S(1)}, bf16[512,2304]{1,0:T(8,128)(2,1)}, u32[]{:S(2)}, u32[]{:S(2)}) collective-permute-start(bf16[512,2304]{1,0:T(8,128)(2,1)S(1)} %fusion.8), channel_id=1, source_target_pairs={{0,2},{1,3},{2,0},{3,1},{4,6},{5,7},{6,4},{7,5},{8,10},{9,11},{10,... | collective-permute-start | bytes 7077896 | tf_op jit(solution)/shard_map/ppermute | solution.py:28
  681.1 60.7 %collective-permute-start.73 = (bf16[1152,1152]{1,0:T(8,128)(2,1)}, bf16[1152,1152]{1,0:T(8,128)(2,1)}, u32[]{:S(2)}, u32[]{:S(2)}) collective-permute-start(bf16[1152,1152]{1,0:T(8,128)(2,1)} %convolution_convert_fusion), channel_id=1, source_target_pairs={{0,4},{1,5},{2,6},{3,7},{4,0},{5,1},{6,2},{7,3},{8,12},{9,13},{10,... | collective-permute-start | bytes 7962632 | tf_op jit(solution)/shard_map/ppermute | solution.py:28
  694.2 104.6 %collective-permute-start.69 = (bf16[1152,1152]{1,0:T(8,128)(2,1)}, bf16[1152,1152]{1,0:T(8,128)(2,1)}, u32[]{:S(2)}, u32[]{:S(2)}) collective-permute-start(bf16[1152,1152]{1,0:T(8,128)(2,1)} %convolution_convert_fusion.1), channel_id=1, source_target_pairs={{0,4},{1,5},{2,6},{3,7},{4,0},{5,1},{6,2},{7,3},{8,12},{9,13},{10,... | collective-permute-start | bytes 7962632 | tf_op jit(solution)/shard_map/ppermute | solution.py:28
  694.7 160.0 %collective-permute-start.65 = (bf16[1152,1152]{1,0:T(8,128)(2,1)}, bf16[1152,1152]{1,0:T(8,128)(2,1)S(1)}, u32[]{:S(2)}, u32[]{:S(2)}) collective-permute-start(bf16[1152,1152]{1,0:T(8,128)(2,1)} %convolution_convert_fusion.2), channel_id=1, source_target_pairs={{0,4},{1,5},{2,6},{3,7},{4,0},{5,1},{6,2},{7,3},{8,12},{9,13},{10,... | collective-permute-start | bytes 7962632 | tf_op jit(solution)/shard_map/ppermute | solution.py:28
  707.6 100.9 %collective-permute-start.45 = (bf16[128,2304]{1,0:T(8,128)(2,1)S(1)}, bf16[128,2304]{1,0:T(8,128)(2,1)S(1)}, u32[]{:S(2)}, u32[]{:S(2)}) collective-permute-start(bf16[128,2304]{1,0:T(8,128)(2,1)S(1)} %get-tuple-element.110), channel_id=1, source_target_pairs={{0,1},{1,0},{2,3},{3,2},{4,5},{5,4},{6,7},{7,6},{8,9},{9,8},{10,11... | collective-permute-start | bytes 1769480 | tf_op jit(solution)/shard_map/ppermute | solution.py:28
  708.5 100.4 %collective-permute-start.47 = (bf16[128,2304]{1,0:T(8,128)(2,1)S(1)}, bf16[128,2304]{1,0:T(8,128)(2,1)S(1)}, u32[]{:S(2)}, u32[]{:S(2)}) collective-permute-start(bf16[128,2304]{1,0:T(8,128)(2,1)S(1)} %get-tuple-element.111), channel_id=1, source_target_pairs={{0,9},{1,8},{2,11},{3,10},{4,13},{5,12},{6,15},{7,14},{8,1},{9,0},... | collective-permute-start | bytes 1769480 | tf_op jit(solution)/shard_map/ppermute | solution.py:28
  741.9 67.1 %collective-permute-start.46 = (bf16[128,2304]{1,0:T(8,128)(2,1)S(1)}, bf16[128,2304]{1,0:T(8,128)(2,1)S(1)}, u32[]{:S(2)}, u32[]{:S(2)}) collective-permute-start(bf16[128,2304]{1,0:T(8,128)(2,1)S(1)} %get-tuple-element.112), channel_id=1, source_target_pairs={{0,8},{1,9},{2,10},{3,11},{4,12},{5,13},{6,14},{7,15},{8,0},{9,1},... | collective-permute-start | bytes 1769480 | tf_op jit(solution)/shard_map/ppermute | solution.py:28
  798.7 125.1 %collective-permute-start.74 = (bf16[576,1152]{1,0:T(8,128)(2,1)}, bf16[576,1152]{1,0:T(8,128)(2,1)}, u32[]{:S(2)}, u32[]{:S(2)}) collective-permute-start(bf16[576,1152]{1,0:T(8,128)(2,1)} %fusion.21), channel_id=1, source_target_pairs={{0,16},{1,17},{2,18},{3,19},{4,20},{5,21},{6,22},{7,23},{8,24},{9,... | collective-permute-start | bytes 3981320 | tf_op jit(solution)/shard_map/ppermute | solution.py:28
  808.5 136.5 %collective-permute-start.70 = (bf16[576,1152]{1,0:T(8,128)(2,1)}, bf16[576,1152]{1,0:T(8,128)(2,1)}, u32[]{:S(2)}, u32[]{:S(2)}) collective-permute-start(bf16[576,1152]{1,0:T(8,128)(2,1)} %fusion.20), channel_id=1, source_target_pairs={{0,16},{1,17},{2,18},{3,19},{4,20},{5,21},{6,22},{7,23},{8,24},{9,... | collective-permute-start | bytes 3981320 | tf_op jit(solution)/shard_map/ppermute | solution.py:28
  812.7 59.5 %collective-permute-start.50 = (bf16[128,2304]{1,0:T(8,128)(2,1)S(1)}, bf16[128,2304]{1,0:T(8,128)(2,1)S(1)}, u32[]{:S(2)}, u32[]{:S(2)}) collective-permute-start(bf16[128,2304]{1,0:T(8,128)(2,1)S(1)} %fusion.24), channel_id=1, source_target_pairs={{0,9},{1,8},{2,11},{3,10},{4,13},{5,12},{6,15},{7,14},{8,1},{9,0},... | collective-permute-start | bytes 1769480 | tf_op jit(solution)/shard_map/ppermute | solution.py:28
  814.9 70.0 %collective-permute-start.49 = (bf16[128,2304]{1,0:T(8,128)(2,1)S(1)}, bf16[128,2304]{1,0:T(8,128)(2,1)S(1)}, u32[]{:S(2)}, u32[]{:S(2)}) collective-permute-start(bf16[128,2304]{1,0:T(8,128)(2,1)S(1)} %fusion.24), channel_id=1, source_target_pairs={{0,8},{1,9},{2,10},{3,11},{4,12},{5,13},{6,14},{7,15},{8,0},{9,1},... | collective-permute-start | bytes 1769480 | tf_op jit(solution)/shard_map/ppermute | solution.py:28
  854.6 30.2 %collective-permute-start.48 = (bf16[128,2304]{1,0:T(8,128)(2,1)S(1)}, bf16[128,2304]{1,0:T(8,128)(2,1)S(1)}, u32[]{:S(2)}, u32[]{:S(2)}) collective-permute-start(bf16[128,2304]{1,0:T(8,128)(2,1)S(1)} %fusion.24), channel_id=1, source_target_pairs={{0,1},{1,0},{2,3},{3,2},{4,5},{5,4},{6,7},{7,6},{8,9},{9,8},{10,11... | collective-permute-start | bytes 1769480 | tf_op jit(solution)/shard_map/ppermute | solution.py:28
  872.2 99.5 %collective-permute-start.66 = (bf16[576,1152]{1,0:T(8,128)(2,1)}, bf16[576,1152]{1,0:T(8,128)(2,1)}, u32[]{:S(2)}, u32[]{:S(2)}) collective-permute-start(bf16[576,1152]{1,0:T(8,128)(2,1)} %fusion.19), channel_id=1, source_target_pairs={{0,16},{1,17},{2,18},{3,19},{4,20},{5,21},{6,22},{7,23},{8,24},{9,... | collective-permute-start | bytes 3981320 | tf_op jit(solution)/shard_map/ppermute | solution.py:28
  893.2 121.3 %collective-permute-start.61 = (bf16[8,144,512]{2,1,0:T(8,128)(2,1)S(1)}, bf16[8,144,512]{2,1,0:T(8,128)(2,1)S(1)}, u32[]{:S(2)}, u32[]{:S(2)}) collective-permute-start(bf16[8,144,512]{2,1,0:T(8,128)(2,1)S(1)} %fusion.27), channel_id=1, source_target_pairs={{0,2},{1,3},{2,0},{3,1},{4,6},{5,7},{6,4},{7,5},{8,10},{9,11},{10,... | collective-permute-start | bytes 3538952 | tf_op jit(solution)/shard_map/ppermute | solution.py:28
  921.4 111.8 %collective-permute-start.51 = (bf16[2048,512]{1,0:T(8,128)(2,1)S(1)}, bf16[2048,512]{1,0:T(8,128)(2,1)S(1)}, u32[]{:S(2)}, u32[]{:S(2)}) collective-permute-start(bf16[2048,512]{1,0:T(8,128)(2,1)S(1)} %slice.484), channel_id=1, source_target_pairs={{0,2},{1,3},{2,0},{3,1},{4,6},{5,7},{6,4},{7,5},{8,10},{9,11},{10,... | collective-permute-start | bytes 6291464 | tf_op jit(solution)/shard_map/ppermute | solution.py:28
  925.5 60.1 %collective-permute-start.75 = (bf16[2,144,1152]{2,1,0:T(8,128)(2,1)S(1)}, bf16[2,144,1152]{2,1,0:T(8,128)(2,1)S(1)}, u32[]{:S(2)}, u32[]{:S(2)}) collective-permute-start(bf16[2,144,1152]{2,1,0:T(8,128)(2,1)S(1)} %dynamic-slice_bitcast_fusion), channel_id=1, source_target_pairs={{0,8},{1,9},{2,10},{3,11},{4,12},{5,13},{6,14},{7,15},{8,0},{9,1},... | collective-permute-start | bytes 1990664 | tf_op jit(solution)/shard_map/ppermute | solution.py:28
  947.5 52.4 %collective-permute-start.71 = (bf16[2,144,1152]{2,1,0:T(8,128)(2,1)S(1)}, bf16[2,144,1152]{2,1,0:T(8,128)(2,1)S(1)}, u32[]{:S(2)}, u32[]{:S(2)}) collective-permute-start(bf16[2,144,1152]{2,1,0:T(8,128)(2,1)S(1)} %dynamic-slice_bitcast_fusion.1), channel_id=1, source_target_pairs={{0,8},{1,9},{2,10},{3,11},{4,12},{5,13},{6,14},{7,15},{8,0},{9,1},... | collective-permute-start | bytes 1990664 | tf_op jit(solution)/shard_map/ppermute | solution.py:28
  973.3 40.8 %collective-permute-start.67 = (bf16[2,144,1152]{2,1,0:T(8,128)(2,1)S(1)}, bf16[2,144,1152]{2,1,0:T(8,128)(2,1)S(1)}, u32[]{:S(2)}, u32[]{:S(2)}) collective-permute-start(bf16[2,144,1152]{2,1,0:T(8,128)(2,1)S(1)} %dynamic-slice_bitcast_fusion.2), channel_id=1, source_target_pairs={{0,8},{1,9},{2,10},{3,11},{4,12},{5,13},{6,14},{7,15},{8,0},{9,1},... | collective-permute-start | bytes 1990664 | tf_op jit(solution)/shard_map/ppermute | solution.py:28
  985.9 30.9 %collective-permute-start.76 = (bf16[2,144,1152]{2,1,0:T(8,128)(2,1)S(1)}, bf16[2,144,1152]{2,1,0:T(8,128)(2,1)S(1)}, u32[]{:S(2)}, u32[]{:S(2)}) collective-permute-start(bf16[2,144,1152]{2,1,0:T(8,128)(2,1)S(1)} %fusion.46), channel_id=1, source_target_pairs={{0,2},{1,3},{2,0},{3,1},{4,6},{5,7},{6,4},{7,5},{8,10},{9,11},{10,... | collective-permute-start | bytes 1990664 | tf_op jit(solution)/shard_map/ppermute | solution.py:28
  1031.1 31.0 %collective-permute-start.63 = (bf16[288,512]{1,0:T(8,128)(2,1)S(1)}, bf16[288,512]{1,0:T(8,128)(2,1)S(1)}, u32[]{:S(2)}, u32[]{:S(2)}) collective-permute-start(bf16[288,512]{1,0:T(8,128)(2,1)S(1)} %fusion.113), channel_id=1, source_target_pairs={{0,16},{1,17},{2,18},{3,19},{4,20},{5,21},{6,22},{7,23},{8,24},{9,... | collective-permute-start | bytes 884744 | tf_op jit(solution)/shard_map/ppermute | solution.py:28
  1035.1 24.8 %collective-permute-start.52 = (bf16[1024,512]{1,0:T(8,128)(2,1)S(1)}, bf16[1024,512]{1,0:T(8,128)(2,1)S(1)}, u32[]{:S(2)}, u32[]{:S(2)}) collective-permute-start(bf16[1024,512]{1,0:T(8,128)(2,1)S(1)} %slice.485), channel_id=1, source_target_pairs={{0,4},{1,5},{2,6},{3,7},{4,0},{5,1},{6,2},{7,3},{8,12},{9,13},{10,... | collective-permute-start | bytes 3145736 | tf_op jit(solution)/shard_map/ppermute | solution.py:28
  1060.3 24.8 %collective-permute-start.53 = (bf16[512,512]{1,0:T(8,128)(2,1)S(1)}, bf16[512,512]{1,0:T(8,128)(2,1)S(1)}, u32[]{:S(2)}, u32[]{:S(2)}) collective-permute-start(bf16[512,512]{1,0:T(8,128)(2,1)S(1)} %slice.486), channel_id=1, source_target_pairs={{0,16},{1,17},{2,18},{3,19},{4,20},{5,21},{6,22},{7,23},{8,24},{9,... | collective-permute-start | bytes 1572872 | tf_op jit(solution)/shard_map/ppermute | solution.py:28
  1062.2 37.7 %collective-permute-start.64 = (bf16[144,512]{1,0:T(8,128)(2,1)S(1)}, bf16[144,512]{1,0:T(8,128)(2,1)S(1)}, u32[]{:S(2)}, u32[]{:S(2)}) collective-permute-start(bf16[144,512]{1,0:T(8,128)(2,1)S(1)} %dynamic-slice_bitcast_fusion.4), channel_id=1, source_target_pairs={{0,8},{1,9},{2,10},{3,11},{4,12},{5,13},{6,14},{7,15},{8,0},{9,1},... | collective-permute-start | bytes 442376 | tf_op jit(solution)/shard_map/ppermute | solution.py:28
  1094.4 37.7 %collective-permute-start.57 = (bf16[8,144,1024]{2,1,0:T(8,128)(2,1)S(1)}, bf16[8,144,1024]{2,1,0:T(8,128)(2,1)}, u32[]{:S(2)}, u32[]{:S(2)}) collective-permute-start(bf16[8,144,1024]{2,1,0:T(8,128)(2,1)S(1)} %fusion.12), channel_id=1, source_target_pairs={{0,2},{1,3},{2,0},{3,1},{4,6},{5,7},{6,4},{7,5},{8,10},{9,11},{10,... | collective-permute-start | bytes 7077896 | tf_op jit(solution)/shard_map/ppermute | solution.py:28
  1094.6 28.4 %collective-permute-start.54 = (bf16[128,2304]{1,0:T(8,128)(2,1)S(1)}, bf16[128,2304]{1,0:T(8,128)(2,1)S(1)}, u32[]{:S(2)}, u32[]{:S(2)}) collective-permute-start(bf16[128,2304]{1,0:T(8,128)(2,1)S(1)} %get-tuple-element.144), channel_id=1, source_target_pairs={{0,1},{1,0},{2,3},{3,2},{4,5},{5,4},{6,7},{7,6},{8,9},{9,8},{10,11... | collective-permute-start | bytes 1769480 | tf_op jit(solution)/shard_map/ppermute | solution.py:28
  1095.9 27.1 %collective-permute-start.56 = (bf16[128,2304]{1,0:T(8,128)(2,1)S(1)}, bf16[128,2304]{1,0:T(8,128)(2,1)S(1)}, u32[]{:S(2)}, u32[]{:S(2)}) collective-permute-start(bf16[128,2304]{1,0:T(8,128)(2,1)S(1)} %get-tuple-element.145), channel_id=1, source_target_pairs={{0,9},{1,8},{2,11},{3,10},{4,13},{5,12},{6,15},{7,14},{8,1},{9,0},... | collective-permute-start | bytes 1769480 | tf_op jit(solution)/shard_map/ppermute | solution.py:28
  1095.9 28.4 %collective-permute-start.55 = (bf16[128,2304]{1,0:T(8,128)(2,1)S(1)}, bf16[128,2304]{1,0:T(8,128)(2,1)S(1)}, u32[]{:S(2)}, u32[]{:S(2)}) collective-permute-start(bf16[128,2304]{1,0:T(8,128)(2,1)S(1)} %get-tuple-element.146), channel_id=1, source_target_pairs={{0,8},{1,9},{2,10},{3,11},{4,12},{5,13},{6,14},{7,15},{8,0},{9,1},... | collective-permute-start | bytes 1769480 | tf_op jit(solution)/shard_map/ppermute | solution.py:28
  1138.3 27.1 %collective-permute-start.58 = (bf16[576,1024]{1,0:T(8,128)(2,1)S(1)}, bf16[576,1024]{1,0:T(8,128)(2,1)}, u32[]{:S(2)}, u32[]{:S(2)}) collective-permute-start(bf16[576,1024]{1,0:T(8,128)(2,1)S(1)} %fusion.26), channel_id=1, source_target_pairs={{0,4},{1,5},{2,6},{3,7},{4,0},{5,1},{6,2},{7,3},{8,12},{9,13},{10,... | collective-permute-start | bytes 3538952 | tf_op jit(solution)/shard_map/ppermute | solution.py:28
  1148.1 28.2 %collective-permute-start.80 = (f32[144,4]{0,1:T(4,128)}, f32[144,4]{0,1:T(4,128)}, u32[]{:S(2)}, u32[]{:S(2)}) collective-permute-start(f32[144,4]{0,1:T(4,128)} %bitcast.524), channel_id=1, source_target_pairs={{0,2},{1,3},{2,0},{3,1},{4,6},{5,7},{6,4},{7,5},{8,10},{9,11},{10,... | collective-permute-start | bytes 6920 | tf_op jit(solution)/shard_map/ppermute | solution.py:28
  1168.8 27.3 %collective-permute-start.59 = (bf16[288,1024]{1,0:T(8,128)(2,1)}, bf16[288,1024]{1,0:T(8,128)(2,1)}, u32[]{:S(2)}, u32[]{:S(2)}) collective-permute-start(bf16[288,1024]{1,0:T(8,128)(2,1)} %fusion.81), channel_id=1, source_target_pairs={{0,16},{1,17},{2,18},{3,19},{4,20},{5,21},{6,22},{7,23},{8,24},{9,... | collective-permute-start | bytes 1769480 | tf_op jit(solution)/shard_map/ppermute | solution.py:28
  (128 other events, 3850.4 us)

commit v2 on v1

--- a/solution.py
+++ b/solution.py
@@ -6,7 +6,7 @@
 from jax import lax
 from jax.experimental import pallas as pl
 from jax.experimental.pallas import tpu as pltpu
-from jax.sharding import PartitionSpec as P
+from jax.sharding import Mesh, PartitionSpec as P
 
 HEAD_DIM = 256
 SEQ_LEN = 4096
@@ -23,29 +23,51 @@
 KEY_CHUNK = 512
 
 
+DP = ("outer", "zh", "zl", "y", "c")
+AXES = DP + ("x",)
+
+
 def swap(value, mask):
-    count = lax.axis_size("dp") * lax.axis_size("tensor")
-    return lax.ppermute(value, ("dp", "tensor"), [(i, i ^ mask) for i in range(count)])
+    count = lax.axis_size(AXES)
+    return lax.ppermute(value, AXES, [(i, i ^ mask) for i in range(count)])
 
 
 def device_index():
-    return lax.axis_index("dp") * lax.axis_size("tensor") + lax.axis_index("tensor")
+    return lax.axis_index(AXES)
 
 
 def bit(mask):
     return (device_index() // mask) % 2
 
 
-def outer_masks():
-    masks, mask = [], 2 * ZH
-    while mask < lax.axis_size("dp") * lax.axis_size("tensor"):
-        masks.append(mask)
-        mask *= 2
-    return masks
+def after(value, *others):
+    out = pl.pallas_call(
+        lambda *refs: None,
+        in_specs=[pl.BlockSpec(memory_space=pl.ANY)] * (1 + len(others)),
+        out_specs=pl.BlockSpec(memory_space=pl.ANY),
+        out_shape=jax.ShapeDtypeStruct(value.shape, value.dtype),
+        input_output_aliases={0: 0},
+        compiler_params=pltpu.CompilerParams(vmem_limit_bytes=2**16),
+        cost_estimate=pl.CostEstimate(flops=0, bytes_accessed=0, transcendentals=0),
+        name="after",
+    )(value, *others)
+    return out
 
 
 def pick(value, index, axis):
     return lax.dynamic_index_in_dim(value, index, axis, keepdims=False)
+
+
+def split_axis(value, mask, axis):
+    here = bit(mask)
+    return pick(value, 1 - here, axis), pick(value, here, axis)
+
+
+def split_columns(value, mask):
+    half = value.shape[-1] // 2
+    low, high = value[..., :half], value[..., half:]
+    first = bit(mask) == 0
+    return jnp.where(first, high, low), jnp.where(first, low, high)
 
 
 def ordered_stack(own, other, mask, axis):
@@ -58,11 +80,9 @@
     return stacked.reshape((2 * own.shape[0],) + own.shape[1:])
 
 
-def halve(value, mask):
-    half = value.reshape((2, value.shape[0] // 2) + value.shape[1:])
-    here = bit(mask)
-    sent = pick(half, 1 - here, 0).astype(bf16)
-    return pick(half, here, 0).astype(f32) + swap(sent, mask).astype(f32)
+def fold(value, mask, axis):
+    sent, kept = split_axis(value, mask, axis)
+    return kept.astype(f32) + swap(sent.astype(bf16), mask).astype(f32)
 
 
 def spread_rows(rows):
@@ -184,7 +204,7 @@
 
 
 def attend_back_kernel(
-    base_ref, limit_ref, lse_ref, delta_ref, q_ref, do_ref, k_ref, v_ref, dq_ref, dkv_ref, acc
+    base_ref, limit_ref, lse_ref, delta_ref, q_ref, do_ref, k_ref, v_ref, dq_ref, near_ref, far_ref, acc
 ):
     step = pl.program_id(0)
 
@@ -216,8 +236,16 @@
         else:
             key_grad, value_grad = key_grad + key_part, value_grad + value_part
         acc[head] += contract_rows(k_ref[...], raw_grad)
-    dkv_ref[:, :HEAD_DIM] = key_grad
-    dkv_ref[:, HEAD_DIM:] = value_grad
+
+    @pl.when(step < pl.num_programs(0) // 2)
+    def _():
+        near_ref[:, :HEAD_DIM] = key_grad
+        near_ref[:, HEAD_DIM:] = value_grad
+
+    @pl.when(step >= pl.num_programs(0) // 2)
+    def _():
+        far_ref[:, :HEAD_DIM] = key_grad.astype(bf16)
+        far_ref[:, HEAD_DIM:] = value_grad.astype(bf16)
 
     @pl.when(step == pl.num_programs(0) - 1)
     def _():
@@ -246,105 +274,82 @@
         ],
         out_specs=[
             whole((tokens, width)),
-            pl.BlockSpec((KEY_CHUNK, 2 * HEAD_DIM), lambda i: (i, 0)),
+            pl.BlockSpec((KEY_CHUNK, 2 * HEAD_DIM), lambda i: (jnp.minimum(i, steps // 2 - 1), 0)),
+            pl.BlockSpec((KEY_CHUNK, 2 * HEAD_DIM), lambda i: (jnp.maximum(i - steps // 2, 0), 0)),
         ],
         out_shape=[
             jax.ShapeDtypeStruct((tokens, width), f32),
-            jax.ShapeDtypeStruct((keys.shape[0], 2 * HEAD_DIM), f32),
+            jax.ShapeDtypeStruct((keys.shape[0] // 2, 2 * HEAD_DIM), f32),
+            jax.ShapeDtypeStruct((keys.shape[0] // 2, 2 * HEAD_DIM), bf16),
         ],
         scratch_shapes=[pltpu.VMEM((2, HEAD_DIM, tokens), f32)],
         compiler_params=pltpu.CompilerParams(
             dimension_semantics=("arbitrary",), vmem_limit_bytes=48 * 2**20
         ),
         cost_estimate=pl.CostEstimate(
-            flops=10 * area * HEAD_DIM, bytes_accessed=16 * 2**20, transcendentals=2 * area
+            flops=0, bytes_accessed=0, transcendentals=0
         ),
         name="attend_back",
     )(base, limit, lse, delta, query, mixed_grad, keys, values)
 
 
-def gather_attention_weight(piece):
+def gather_attention_weight(piece, first=None):
     rows = piece.shape[0]
-    here = bit(ZL)
-    own = pick(piece, here, 1)
-    got = swap(pick(piece, 1 - here, 1), ZL)
+    sent, own = split_axis(piece, ZL, 1)
+    if first is not None:
+        sent = after(sent, first)
+    got = swap(sent, ZL)
     full = ordered_stack(own, got, ZL, 0).reshape(2 * rows, -1)
-    full = join(full, ZH)
-    full = join(full, Y)
+    full = join(join(full, ZH), Y)
     block = full.reshape(8, rows, -1)
     full = ordered_stack(block, swap(block, C), C, 1).reshape(16 * rows, -1)
-    for mask in outer_masks():
-        full = join(full, mask)
-    return full
+    if lax.axis_size("outer") > 1:
+        full = lax.all_gather(full, "outer", axis=0, tiled=True)
+    return full, got
 
 
 def reduce_attention_grad(value):
-    for mask in reversed(outer_masks()):
-        value = halve(value, mask)
+    if lax.axis_size("outer") > 1:
+        value = lax.psum_scatter(value.astype(bf16), "outer", scatter_dimension=0, tiled=True)
     rows = value.shape[0] // 16
-    here = bit(C)
-    split = value.reshape(8, 2, rows, -1)
-    sent = pick(split, 1 - here, 1).astype(bf16)
-    value = (pick(split, here, 1).astype(f32) + swap(sent, C).astype(f32)).reshape(8 * rows, -1)
-    value = halve(value, Y)
-    value = halve(value, ZH)
-    half = value.astype(bf16).reshape(2, rows, -1)
-    here = bit(ZL)
-    own = pick(half, here, 0)
-    got = swap(pick(half, 1 - here, 0), ZL)
-    return ordered_stack(own, got, ZL, 1).astype(f32)
-
-
-def gather_ffn_weight(piece):
+    value = fold(value.reshape(8, 2, rows, -1), C, 1)
+    value = fold(value.reshape(2, 4 * rows, -1), Y, 0)
+    value = fold(value.reshape(2, 2 * rows, -1), ZH, 0)
+    sent, own = split_axis(value.astype(bf16).reshape(2, rows, -1), ZL, 0)
+    return ordered_stack(own, swap(sent, ZL), ZL, 1).astype(f32)
+
+
+def gather_ffn_weight(piece, first):
     rows = piece.shape[0]
-    split = piece.reshape(rows, 2, 2, -1)
-    here = bit(ZL)
-    own = pick(split, here, 1)
-    got = swap(pick(split, 1 - here, 1), ZL)
-    split = ordered_stack(own, got, ZL, 0)
-    here = bit(C)
-    own = pick(split, here, 2)
-    got = swap(pick(split, 1 - here, 2), C)
-    full = ordered_stack(own, got, C, 1).reshape(4 * rows, -1)
-    full = join(full, ZH)
-    full = join(full, Y)
-    for mask in outer_masks():
-        full = join(full, mask)
-    return full
-
-
-def reduce_ffn_grad(left, right):
-    masks = list(reversed(outer_masks())) + [Y, ZH]
-    half_width = left.shape[1] // 2
-    here = bit(masks[0])
-    sent = contract_rows(lax.dynamic_slice_in_dim(left, (1 - here) * half_width, half_width, 1), right)
-    got = swap(sent.astype(bf16), masks[0])
-    kept = contract_rows(lax.dynamic_slice_in_dim(left, here * half_width, half_width, 1), right)
-    value = kept + got.astype(f32)
-    for mask in masks[1:]:
-        value = halve(value, mask)
-    rows = value.shape[0] // 4
-    split = value.astype(bf16).reshape(2, 2, rows, -1)
-    here = bit(ZL)
-    own = pick(split, here, 0)
-    got = swap(pick(split, 1 - here, 0), ZL)
-    split = ordered_stack(own, got, ZL, 0)
-    here = bit(C)
-    own = pick(split, here, 1)
-    got = swap(pick(split, 1 - here, 1), C)
-    split = ordered_stack(own, got, C, 1)
+    sent, own = split_columns(piece, ZL)
+    got = swap(after(sent, first), ZL)
+    sent, own = split_columns(ordered_stack(own, got, ZL, 0), C)
+    block = ordered_stack(own, swap(sent, C), C, 1).reshape(4 * rows, -1)
+    return lax.all_gather(block, ("outer", "y", "zh"), axis=0, tiled=True), got
+
+
+def scatter_ffn_grad(terms):
+    return lax.psum_scatter(terms, ("outer", "y", "zh"), scatter_dimension=0, tiled=True)
+
+
+def return_ffn_grad(value):
+    split = value.reshape(2, 2, value.shape[0] // 4, -1)
+    sent, own = split_axis(split, ZL, 0)
+    sent, own = split_axis(ordered_stack(own, swap(sent, ZL), ZL, 0), C, 1)
+    split = ordered_stack(own, swap(sent, C), C, 1)
     return jnp.concatenate(
         [split[a, b].astype(f32) for a in range(2) for b in range(2)], axis=1
     )
 
 
 def reduce_gains(value):
-    value = value.T
-    for mask in list(reversed(outer_masks())) + [Y, ZH, ZL, C]:
-        half = value.reshape((2, value.shape[0] // 2) + value.shape[1:])
-        here = bit(mask)
-        value = pick(half, here, 0) + swap(pick(half, 1 - here, 0), mask)
-    return (value + swap(value, X)).T
+    value = value.reshape(4, 16 * lax.axis_size("outer"), -1).transpose(1, 0, 2)
+    if lax.axis_size("outer") > 1:
+        value = lax.psum_scatter(value, "outer", scatter_dimension=0, tiled=True)
+    for mask in (Y, ZH, ZL, C):
+        sent, kept = split_axis(value.reshape((2, value.shape[0] // 2) + value.shape[1:]), mask, 0)
+        value = kept + swap(sent, mask)
+    return (value + swap(value, X))[0]
 
 
 def body(
@@ -365,7 +370,7 @@
 ):
     own_rows, width = tokens.shape
     rows = q_weight.shape[0]
-    outer = lax.axis_size("dp") // 16
+    outer = lax.axis_size("outer")
     me = device_index()
 
     def permuted(value):
@@ -378,18 +383,21 @@
         split = value.reshape(lead, outer, 2, 4, 2 * rows)
         return split.swapaxes(2, 3).reshape(lead, width)
 
-    gains_own = jnp.stack([attn_gain, post_attn_gain, ffn_gain, post_ffn_gain]).astype(bf16)
-    gains = permuted(lax.all_gather(gains_own, "dp", axis=1, tiled=True)).astype(f32)
-    gain_one, gain_two, gain_three, gain_four = (gains[i] for i in range(4))
-
+    gains_own = jnp.stack([attn_gain, post_attn_gain, ffn_gain, post_ffn_gain], axis=1)
+    gains_own = jnp.pad(gains_own.astype(bf16), ((0, 0), (0, 124)))[:, None]
     q_split = q_weight.astype(bf16).reshape(rows, 2, -1)
     k_split = k_weight.astype(bf16).reshape(rows, 2, -1)
     v_split = v_weight.astype(bf16).reshape(rows, 2, -1)
-    qkv_full = gather_attention_weight(jnp.concatenate([q_split, k_split, v_split], axis=2))
-    out_full = gather_attention_weight(out_weight.T.astype(bf16).reshape(rows, 2, -1))
-    gate_full = gather_ffn_weight(gate_weight.astype(bf16))
-    up_full = gather_ffn_weight(up_weight.astype(bf16))
-    down_full = gather_ffn_weight(down_weight.T.astype(bf16))
+    qkv_full, got = gather_attention_weight(
+        jnp.concatenate([q_split, k_split, v_split, jnp.tile(gains_own, (1, 2, 1))], axis=2)
+    )
+    gains = qkv_full[:, 4 * HEAD_DIM : 4 * HEAD_DIM + 4].astype(f32).T
+    qkv_full = qkv_full[:, : 4 * HEAD_DIM]
+    gain_one, gain_two, gain_three, gain_four = (gains[i] for i in range(4))
+    gate_full, got = gather_ffn_weight(gate_weight.astype(bf16), got)
+    up_full, got_up = gather_ffn_weight(up_weight.astype(bf16), got)
+    out_full, got = gather_attention_weight(out_weight.T.astype(bf16).reshape(rows, 2, -1), got)
+    down_full, got = gather_ffn_weight(down_weight.T.astype(bf16), got_up)
 
     row_bases = [((me ^ mask) * own_rows) % SEQ_LEN for mask in (0, X, ZL, X | ZL)]
     lane = jnp.arange(own_rows, dtype=jnp.int32)
@@ -407,10 +415,11 @@
     angles = query_pos.astype(f32)[:, None] * frequency[None, :]
     cosine, sine = jnp.cos(angles), jnp.sin(angles)
 
-    resid = permuted(tokens).astype(f32)
+    own_tokens = permuted(tokens)
+    resid = own_tokens.astype(f32)
     upstream = permuted(cotangent).astype(f32)
 
-    hidden_one = spread_rows(rms_scale(resid, gain_one).astype(bf16))
+    hidden_one = rms_scale(spread_rows(own_tokens).astype(f32), gain_one).astype(bf16)
     projected = mm(hidden_one, qkv_full)
     scale = HEAD_DIM ** (-0.5)
     query_rot = jnp.concatenate(
@@ -457,15 +466,20 @@
     ffn_grad, gain_four_grad = post_ffn_pull(upstream)
     ffn_grad_rows = spread_rows(ffn_grad.astype(bf16))
     ffn_grad_rows = jnp.concatenate([ffn_grad_rows, swap(ffn_grad_rows, C)], axis=0)
+    down_terms = contract_rows(ffn_grad_rows, inner).astype(bf16)
+    down_sums = scatter_ffn_grad(down_terms)
+    gate_part = after(gate_part, down_terms)
     inner_grad = mm(ffn_grad_rows, down_full)
     unused_inner, gelu_pull = jax.vjp(gelu_times, gate_part, up_part)
     gate_grad_part, up_grad_part = gelu_pull(inner_grad)
     gate_grad_part = gate_grad_part.astype(bf16)
     up_grad_part = up_grad_part.astype(bf16)
     normed_three_grad = share_out([(gate_grad_part, gate_full), (up_grad_part, up_full)])
-    down_block = reduce_ffn_grad(ffn_grad_rows, inner)
-    gate_block = reduce_ffn_grad(hidden_two, gate_grad_part)
-    up_block = reduce_ffn_grad(hidden_two, up_grad_part)
+    gate_sums = scatter_ffn_grad(contract_rows(hidden_two, gate_grad_part).astype(bf16))
+    up_sums = scatter_ffn_grad(contract_rows(hidden_two, up_grad_part).astype(bf16))
+    down_block = return_ffn_grad(down_sums)
+    gate_block = return_ffn_grad(gate_sums)
+    up_block = return_ffn_grad(up_sums)
     unused_three, ffn_norm_pull = jax.vjp(rms_scale, resid_two, gain_three)
     resid_two_extra, gain_three_grad = ffn_norm_pull(normed_three_grad)
     resid_two_grad = upstream + resid_two_extra
@@ -477,13 +491,15 @@
     delta = jnp.sum(
         (mixed_grad.astype(f32) * mixed).reshape(-1, 2, HEAD_DIM), axis=-1
     ).T
-    query_grad, key_value_grad = attend_back(
+    query_grad, key_value_grad, sent = attend_back(
         key_bases, limit, lse, delta, query_rot, mixed_grad, keys, values
     )
     for mask in (C, Y, ZH):
-        count = key_value_grad.shape[0] // 2
-        got = swap(key_value_grad[count:].astype(bf16), mask)
-        key_value_grad = key_value_grad[:count].astype(f32) + got.astype(f32)
+        key_value_grad = key_value_grad + swap(sent, mask).astype(f32)
+        if mask != ZH:
+            count = key_value_grad.shape[0] // 2
+            sent = key_value_grad[count:].astype(bf16)
+            key_value_grad = key_value_grad[:count]
     out_block = reduce_attention_grad(contract_rows(attn_grad_rows, mixed_low))
     qkv_grad = jnp.concatenate(
         [
@@ -522,24 +538,15 @@
 
 
 def solution(mesh):
-    weight_specs = (
-        P("dp", "tensor"),
-        P("dp", "tensor"),
-        P("dp", "tensor"),
-        P("tensor", "dp"),
-        P("dp", "tensor"),
-        P("dp", "tensor"),
-        P("tensor", "dp"),
-        P("dp"),
-        P("dp"),
-        P("dp"),
-        P("dp"),
-    )
-    rows_spec = P(("dp", "tensor"), None)
+    outer = mesh.shape["dp"] // 16
+    parts = Mesh(mesh.devices.reshape(outer, 2, 2, 2, 2, 2), AXES)
+    by_rows, by_columns = P(DP, "x"), P("x", DP)
+    weight_specs = (by_rows,) * 3 + (by_columns,) + (by_rows,) * 2 + (by_columns,) + (P(DP),) * 4
+    tokens_spec = P(AXES, None)
     return jax.shard_map(
         body,
-        mesh=mesh,
-        in_specs=(rows_spec, rows_spec, P()) + weight_specs,
-        out_specs=(rows_spec, rows_spec) + weight_specs,
+        mesh=parts,
+        in_specs=(tokens_spec, tokens_spec, P()) + weight_specs,
+        out_specs=(tokens_spec, tokens_spec) + weight_specs,
         check_vma=False,
     )

time: 1220 us -> 998 us (0.82)
  waiting for transfers between devices: 790 us -> 609 us
  local copies, waits for them, and re-layouts: 88.1 us -> 63.7 us
  blocking collectives: 23.2 us -> 0 us
  between operations: 4.45 us -> 17.3 us
    ppermute x82 -> x70, waiting for transfers between devices: 790 us -> 608 us  [swap(): return lax.ppermute(value, AXES, [(i, i ^ mask) for i in range(count)])]
    all_gather x1 -> x0, blocking collectives: 23.2 us -> none  [body(): lax.all_gather(gains_own, 'dp', axis=1, tiled=True)]
    ppermute x82 -> x70, starting transfers between devices: 75.1 us -> 62.8 us  [swap(): return lax.ppermute(value, AXES, [(i, i ^ mask) for i in range(count)])]
    another operation x42 -> x30, other arithmetic: 25.6 us -> 18.7 us  [ordered_stack(): jnp.stack([jnp.where(first, own, other), jnp.where(first, other, own)], a...]
    dot_general x8 -> x5, matrix products: 37.5 us -> 35.5 us  [contract_rows(): lax.dot_general(left, right, (((0,), (0,)), ((), ())), preferred_element_...]
    unnamed x239 -> x131, local copies, waits for them, and re-layouts: 26.3 us -> 27.7 us
  transfers between devices with their start and end apart: 82 -> 76, of which waited for: 44 -> 43; matrix products, arithmetic and copies ran while one was open for 17% -> 21% of each run, Pallas kernels for 3% -> 3%
where the time goes in v2:
time: 998 us; the launch traced here: 990 us
  waiting for transfers between devices  609 us (61%)
  matrix products  124 us (12%)
  other arithmetic  79.6 us (8%)
  local copies, waits for them, and re-layouts  63.7 us (6%)
  starting transfers between devices  63.6 us (6%)
  Pallas kernels  32.8 us (3%)
  between operations  17.3 us (2%)
    ppermute x70, waiting for transfers between devices, swap(): return lax.ppermute(value, AXES, [(i, i ^ mask) for i in range(count)])  608 us
    ppermute x70, starting transfers between devices, swap(): return lax.ppermute(value, AXES, [(i, i ^ mask) for i in range(count)])  62.8 us
    dot_general x5, matrix products, mm(): return jnp.dot(left, right, preferred_element_type=f32)  44.8 us
    dot_general x10, matrix products, contract_cols(): lax.dot_general(left, right, (((1,), (1,)), ((), ())), preferred_element_...  43.5 us
    dot_general x5, matrix products, contract_rows(): lax.dot_general(left, right, (((0,), (0,)), ((), ())), preferred_element_...  35.5 us
    unnamed x131, local copies, waits for them, and re-layouts  27.7 us
    pallas_call x1, Pallas kernels, attend_back(): pl.pallas_call(attend_back_kernel, grid=(steps,), in_specs=[pl.BlockSpec(...  21.2 us
  transfers between devices with their start and end apart: 76, of which 43 were waited for; matrix products, arithmetic and copies ran while one was open for 21% of the time, Pallas kernels for 3%

profile of v2, /device:TPU:0, one launch (start us, length us, event | category | flops | bytes accessed | tf_op | source)
XLA Modules:
  0.0 990.0 jit_solution(15694123586862001788)
XLA Ops:
  13.5 3.1 collective-permute-start.3
  18.5 5.8 collective-permute-done.3.refs_1_
  33.6 8.6 collective-permute-done.13.refs_1_
  46.6 2.9 convert_element_type.309
  54.3 2.8 collective-permute-start.4
  57.2 50.7 %collective-permute-done.4 = bf16[288,1152]{1,0:T(8,128)(2,1)S(1)} collective-permute-done((bf16[288,1152]{1,0:T(8,128)(2,1)S(1)}, bf16[288,1152]{1,0:T(8,128)(2,1)S(1)}, u32[]{:S(2)}, u32[]{:S(2)}) %collective-permute-start.4) | collective-permute-done | bytes 663584 | tf_op jit(solution)/shard_map/ppermute | solution.py:32
  111.2 3.1 collective-permute-start.14
  120.6 36.8 %collective-permute-done.5 = bf16[576,1152]{1,0:T(8,128)(2,1)} collective-permute-done((bf16[576,1152]{1,0:T(8,128)(2,1)}, bf16[576,1152]{1,0:T(8,128)(2,1)}, u32[]{:S(2)}, u32[]{:S(2)}) %collective-permute-start.5) | collective-permute-done | bytes 1327136 | tf_op jit(solution)/shard_map/ppermute | solution.py:32
  164.3 19.0 %collective-permute-done.15 = bf16[288,512]{1,0:T(8,128)(2,1)S(1)} collective-permute-done((bf16[288,512]{1,0:T(8,128)(2,1)S(1)}, bf16[288,512]{1,0:T(8,128)(2,1)S(1)}, u32[]{:S(2)}, u32[]{:S(2)}) %collective-permute-start.15) | collective-permute-done | bytes 294944 | tf_op jit(solution)/shard_map/ppermute | solution.py:32
  183.4 2.6 collective-permute-start.16
  187.9 3.0 select_bitcast_fusion.1
  193.8 4.4 fusion.23
  204.1 36.5 %collective-permute-done.7 = bf16[512,256]{1,0:T(8,128)(2,1)S(1)} collective-permute-done((bf16[512,256]{1,0:T(8,128)(2,1)S(1)}, bf16[512,256]{1,0:T(8,128)(2,1)S(1)}, u32[]{:S(2)}, u32[]{:S(2)}) %collective-permute-start.7) | collective-permute-done | bytes 262176 | tf_op jit(solution)/shard_map/ppermute | solution.py:32
  240.7 10.1 %collective-permute-done.10 = bf16[512,256]{1,0:T(8,128)(2,1)S(1)} collective-permute-done((bf16[512,256]{1,0:T(8,128)(2,1)S(1)}, bf16[512,256]{1,0:T(8,128)(2,1)S(1)}, u32[]{:S(2)}, u32[]{:S(2)}) %collective-permute-start.10) | collective-permute-done | bytes 262176 | tf_op jit(solution)/shard_map/ppermute | solution.py:32
  253.9 12.5 %collective-permute-done.11 = bf16[1024,256]{1,0:T(8,128)(2,1)S(1)} collective-permute-done((bf16[1024,256]{1,0:T(8,128)(2,1)S(1)}, bf16[1024,256]{1,0:T(8,128)(2,1)S(1)}, u32[]{:S(2)}, u32[]{:S(2)}) %collective-permute-start.11) | collective-permute-done | bytes 524320 | tf_op jit(solution)/shard_map/ppermute | solution.py:32
  270.7 11.6 %attend.1 = (f32[512,512]{1,0:T(8,128)S(1)}, bf16[512,512]{1,0:T(8,128)(2,1)S(1)}, f32[2,512]{1,0:T(2,128)S(1)}) custom-call(s32[32]{0:T(128)S(1)} %stack.343.base_ref, s32[1,512]{1,0:T(1,128)S(1)} %add_maximum_fusion.limit_ref, bf16[512,512]{1,0:T(8,128)(2,1)S(1)} %pad_maximum_fusion.22.q_ref, bf16[4096,256]{1,0:T(8,128)(2,1)S(1)} %pad_maximum_fusion.7.k_ref, ...), custom_call_target="tpu_custom_call" | custom-call | flops 4294967296 | bytes 8388608 | tf_op jit(solution)/shard_map/attend/pallas_call | solution.py:176
  291.3 10.6 %collective-permute-done.18 = bf16[128,2304]{1,0:T(8,128)(2,1)} collective-permute-done((bf16[128,2304]{1,0:T(8,128)(2,1)}, bf16[128,2304]{1,0:T(8,128)(2,1)}, u32[]{:S(2)}, u32[]{:S(2)}) %collective-permute-start.18) | collective-permute-done | bytes 589856 | tf_op jit(solution)/shard_map/ppermute | solution.py:32
  301.8 28.9 %collective-permute-done.20 = bf16[128,2304]{1,0:T(8,128)(2,1)} collective-permute-done((bf16[128,2304]{1,0:T(8,128)(2,1)}, bf16[128,2304]{1,0:T(8,128)(2,1)}, u32[]{:S(2)}, u32[]{:S(2)}) %collective-permute-start.20) | collective-permute-done | bytes 589856 | tf_op jit(solution)/shard_map/ppermute | solution.py:32
  330.8 12.0 %collective-permute-done.19 = bf16[128,2304]{1,0:T(8,128)(2,1)} collective-permute-done((bf16[128,2304]{1,0:T(8,128)(2,1)}, bf16[128,2304]{1,0:T(8,128)(2,1)}, u32[]{:S(2)}, u32[]{:S(2)}) %collective-permute-start.19) | collective-permute-done | bytes 589856 | tf_op jit(solution)/shard_map/ppermute | solution.py:32
  342.7 3.2 multiply_reduce_fusion.9
  351.9 28.0 %collective-permute-done.23 = bf16[128,2304]{1,0:T(8,128)(2,1)S(1)} collective-permute-done((bf16[128,2304]{1,0:T(8,128)(2,1)S(1)}, bf16[128,2304]{1,0:T(8,128)(2,1)S(1)}, u32[]{:S(2)}, u32[]{:S(2)}) %collective-permute-start.23) | collective-permute-done | bytes 589856 | tf_op jit(solution)/shard_map/ppermute | solution.py:32
  379.9 14.2 %collective-permute-done.22 = bf16[128,2304]{1,0:T(8,128)(2,1)S(1)} collective-permute-done((bf16[128,2304]{1,0:T(8,128)(2,1)S(1)}, bf16[128,2304]{1,0:T(8,128)(2,1)S(1)}, u32[]{:S(2)}, u32[]{:S(2)}) %collective-permute-start.22) | collective-permute-done | bytes 589856 | tf_op jit(solution)/shard_map/ppermute | solution.py:32
  400.5 11.1 %fusion.189.refs_0_ = f32[1024,1152]{1,0:T(8,128)} fusion(bf16[1024,2304]{1,0:T(8,128)(2,1)} %constant_dynamic-update-slice_fusion, bf16[2304,1152]{1,0:T(8,128)(2,1)} %all-gather.4.cloned.1.call-done), kind=kOutput, calls=%fused_computation.413 | convolution fusion | flops 5435817984 | bytes 14745600 | tf_op jit(solution)/shard_map/dot_general | solution.py:120
  411.6 12.5 %fusion.18 = (bf16[1024,1152]{1,0:T(8,128)(2,1)}, f32[1024,1152]{1,0:T(8,128)}) fusion(f32[1024,1152]{1,0:T(8,128)} %fusion.189.refs_0_, bf16[1024,2304]{1,0:T(8,128)(2,1)} %constant_dynamic-update-slice_fusion, bf16[2304,1152]{1,0:T(8,128)(2,1)} %all-gather.6.cloned.1.call-done), kind=kOutput, calls=%fused_computation.29 | convolution fusion | flops 5447614464 | bytes 21823488 | tf_op jit(solution)/shard_map/dot_general | solution.py:120
  425.1 6.3 convolution_convert_fusion.3
  431.5 4.5 collective-permute-done.30
  436.0 4.9 fusion.187
  448.2 2.7 copy.122
  450.8 19.6 %collective-permute-done.31 = bf16[128,2304]{1,0:T(8,128)(2,1)} collective-permute-done((bf16[128,2304]{1,0:T(8,128)(2,1)}, bf16[128,2304]{1,0:T(8,128)(2,1)}, u32[]{:S(2)}, u32[]{:S(2)}) %collective-permute-start.31) | collective-permute-done | bytes 589856 | tf_op jit(solution)/shard_map/ppermute | solution.py:32
  479.4 13.7 %collective-permute-done.36 = bf16[128,2304]{1,0:T(8,128)(2,1)S(1)} collective-permute-done((bf16[128,2304]{1,0:T(8,128)(2,1)S(1)}, bf16[128,2304]{1,0:T(8,128)(2,1)S(1)}, u32[]{:S(2)}, u32[]{:S(2)}) %collective-permute-start.36) | collective-permute-done | bytes 589856 | tf_op jit(solution)/shard_map/ppermute | solution.py:32
  493.1 10.6 %collective-permute-done.35 = bf16[128,2304]{1,0:T(8,128)(2,1)S(1)} collective-permute-done((bf16[128,2304]{1,0:T(8,128)(2,1)S(1)}, bf16[128,2304]{1,0:T(8,128)(2,1)S(1)}, u32[]{:S(2)}, u32[]{:S(2)}) %collective-permute-start.35) | collective-permute-done | bytes 589856 | tf_op jit(solution)/shard_map/ppermute | solution.py:32
  504.1 4.4 collective-permute-done.37
  510.8 8.4 convolution_convert_fusion.2.refs_1_
  528.3 13.1 %multiply_convert_fusion = (bf16[1024,1152]{1,0:T(8,128)(2,1)S(1)}, bf16[1024,1152]{1,0:T(8,128)(2,1)S(1)}) fusion(f32[1024,1152]{1,0:T(8,128)} %copy-done.3, f32[1024,1152]{1,0:T(8,128)} %get-tuple-element.174, bf16[1024,2304]{1,0:T(8,128)(2,1)S(1)} %copy-done.39, bf16[2304,1152]{1,0:T(8,128)(2,1)} %all-gather.8.cloned.1.call-done), kind=kOutput, calls=%fused_computation.33 | convolution fusion | flops 5464129536 | bytes 24182784 | tf_op jit(solution)/shard_map/dot_general | solution.py:120
  541.4 3.2 fusion.47
  544.7 4.5 fusion.19
  549.3 9.8 convolution_convert_fusion.1
  559.4 6.3 fusion.52
  565.7 6.7 fusion.188
  576.0 23.0 %collective-permute-done.39 = bf16[128,2304]{1,0:T(8,128)(2,1)S(1)} collective-permute-done((bf16[128,2304]{1,0:T(8,128)(2,1)S(1)}, bf16[128,2304]{1,0:T(8,128)(2,1)S(1)}, u32[]{:S(2)}, u32[]{:S(2)}) %collective-permute-start.39) | collective-permute-done | bytes 589856 | tf_op jit(solution)/shard_map/ppermute | solution.py:32
  599.1 4.1 collective-permute-done.41
  603.1 21.1 %collective-permute-done.40 = bf16[128,2304]{1,0:T(8,128)(2,1)S(1)} collective-permute-done((bf16[128,2304]{1,0:T(8,128)(2,1)S(1)}, bf16[128,2304]{1,0:T(8,128)(2,1)S(1)}, u32[]{:S(2)}, u32[]{:S(2)}) %collective-permute-start.40) | collective-permute-done | bytes 589856 | tf_op jit(solution)/shard_map/ppermute | solution.py:32
  631.5 23.6 %collective-permute-done.44 = bf16[128,2304]{1,0:T(8,128)(2,1)} collective-permute-done((bf16[128,2304]{1,0:T(8,128)(2,1)}, bf16[128,2304]{1,0:T(8,128)(2,1)}, u32[]{:S(2)}, u32[]{:S(2)}) %collective-permute-start.44) | collective-permute-done | bytes 589856 | tf_op jit(solution)/shard_map/ppermute | solution.py:32
  655.2 21.5 %collective-permute-done.43 = bf16[128,2304]{1,0:T(8,128)(2,1)} collective-permute-done((bf16[128,2304]{1,0:T(8,128)(2,1)}, bf16[128,2304]{1,0:T(8,128)(2,1)}, u32[]{:S(2)}, u32[]{:S(2)}) %collective-permute-start.43) | collective-permute-done | bytes 589856 | tf_op jit(solution)/shard_map/ppermute | solution.py:32
  676.7 3.8 convolution_convert_fusion.6.do_ref
  684.2 3.0 fusion.94
  689.7 21.2 %attend_back.1 = (f32[512,512]{1,0:T(8,128)S(1)}, f32[2048,512]{1,0:T(8,128)}, bf16[2048,512]{1,0:T(8,128)(2,1)}) custom-call(s32[32]{0:T(128)S(1)} %stack.343.base_ref, s32[1,512]{1,0:T(1,128)S(1)} %add_maximum_fusion.limit_ref, f32[2,512]{1,0:T(2,128)S(1)} %get-tuple-element.20.lse_ref, f32[2,512]{1,0:T(2,128)S(1)} %bitcast.392, ...), custom_call_target="tpu_custom_call" | custom-call | tf_op jit(solution)/shard_map/attend_back/pallas_call | solution.py:262
  710.9 9.8 convolution_convert_fusion
  720.7 2.6 bitcast_add_fusion.1
  735.9 4.8 collective-permute-done.56
  742.5 38.0 %collective-permute-done.46 = bf16[1024,512]{1,0:T(8,128)(2,1)S(1)} collective-permute-done((bf16[1024,512]{1,0:T(8,128)(2,1)}, bf16[1024,512]{1,0:T(8,128)(2,1)S(1)}, u32[]{:S(2)}, u32[]{:S(2)}) %collective-permute-start.46) | collective-permute-done | bytes 1048608 | tf_op jit(solution)/shard_map/ppermute | solution.py:32
  784.0 43.2 %collective-permute-done.47 = bf16[512,512]{1,0:T(8,128)(2,1)S(1)} collective-permute-done((bf16[512,512]{1,0:T(8,128)(2,1)S(1)}, bf16[512,512]{1,0:T(8,128)(2,1)S(1)}, u32[]{:S(2)}, u32[]{:S(2)}) %collective-permute-start.47) | collective-permute-done | bytes 524320 | tf_op jit(solution)/shard_map/ppermute | solution.py:32
  830.1 4.5 convolution_convert_fusion.4
  838.3 4.5 fusion.67
  844.6 18.1 %collective-permute-done.48 = bf16[128,2304]{1,0:T(8,128)(2,1)S(1)} collective-permute-done((bf16[128,2304]{1,0:T(8,128)(2,1)S(1)}, bf16[128,2304]{1,0:T(8,128)(2,1)S(1)}, u32[]{:S(2)}, u32[]{:S(2)}) %collective-permute-start.48) | collective-permute-done | bytes 589856 | tf_op jit(solution)/shard_map/ppermute | solution.py:32
  863.9 14.5 %collective-permute-done.49 = bf16[128,2304]{1,0:T(8,128)(2,1)S(1)} collective-permute-done((bf16[128,2304]{1,0:T(8,128)(2,1)S(1)}, bf16[128,2304]{1,0:T(8,128)(2,1)S(1)}, u32[]{:S(2)}, u32[]{:S(2)}) %collective-permute-start.49) | collective-permute-done | bytes 589856 | tf_op jit(solution)/shard_map/ppermute | solution.py:32
  878.4 2.8 fusion.41
  885.7 2.9 collective-permute-done.58
  891.3 2.6 collective-permute-done.67
  896.5 3.9 bitcast_add_fusion
  914.3 17.8 %collective-permute-done.52 = bf16[576,1024]{1,0:T(8,128)(2,1)} collective-permute-done((bf16[576,1024]{1,0:T(8,128)(2,1)}, bf16[576,1024]{1,0:T(8,128)(2,1)}, u32[]{:S(2)}, u32[]{:S(2)}) %collective-permute-start.52) | collective-permute-done | bytes 1179680 | tf_op jit(solution)/shard_map/ppermute | solution.py:32
  936.2 18.3 %collective-permute-done.59 = bf16[2,144,1152]{2,1,0:T(8,128)(2,1)S(1)} collective-permute-done((bf16[2,144,1152]{2,1,0:T(8,128)(2,1)S(1)}, bf16[2,144,1152]{2,1,0:T(8,128)(2,1)S(1)}, u32[]{:S(2)}, u32[]{:S(2)}) %collective-permute-start.59) | collective-permute-done | bytes 663584 | tf_op jit(solution)/shard_map/ppermute | solution.py:32
  954.9 10.3 %collective-permute-done.53 = bf16[288,1024]{1,0:T(8,128)(2,1)S(1)} collective-permute-done((bf16[288,1024]{1,0:T(8,128)(2,1)S(1)}, bf16[288,1024]{1,0:T(8,128)(2,1)S(1)}, u32[]{:S(2)}, u32[]{:S(2)}) %collective-permute-start.53) | collective-permute-done | bytes 589856 | tf_op jit(solution)/shard_map/ppermute | solution.py:32
  968.2 5.8 collective-permute-done.54
  (449 shorter events, 194.6 us)
Async XLA Ops:
  7.2 393.3 %all-gather.4.cloned.1.call-start = ((), (), s32[]{:S(2)}) async-start(), calls=%async_computation.3 | async-start | bytes 6635520 | tf_op jit(solution)/shard_map/all_gather | solution.py:328
  13.5 10.9 %collective-permute-start.3 = (bf16[144,1152]{1,0:T(8,128)(2,1)S(1)}, bf16[144,1152]{1,0:T(8,128)(2,1)S(1)}, u32[]{:S(2)}, u32[]{:S(2)}) collective-permute-start(bf16[144,1152]{1,0:T(8,128)(2,1)S(1)} %dynamic-slice_bitcast_fusion.3), channel_id=1, source_target_pairs={{0,8},{1,9},{2,10},{3,11},{4,12},{5,13},{6,14},{7,15},{8,0},{9,1},... | collective-permute-start | bytes 995336 | tf_op jit(solution)/shard_map/ppermute | solution.py:32
  24.4 17.8 %collective-permute-start.13 = (bf16[144,2304]{1,0:T(8,128)(2,1)S(1)}, bf16[144,2304]{1,0:T(8,128)(2,1)S(1)}, u32[]{:S(2)}, u32[]{:S(2)}) collective-permute-start(bf16[144,2304]{1,0:T(8,128)(2,1)S(1)} %after.5), channel_id=1, source_target_pairs={{0,8},{1,9},{2,10},{3,11},{4,12},{5,13},{6,14},{7,15},{8,0},{9,1},... | collective-permute-start | bytes 1990664 | tf_op jit(solution)/shard_map/ppermute | solution.py:32
  30.1 131.3 %collective-permute-start.2 = (bf16[128,2304]{0,1:T(8,128)(2,1)}, bf16[128,2304]{0,1:T(8,128)(2,1)}, u32[]{:S(2)}, u32[]{:S(2)}) collective-permute-start(bf16[128,2304]{0,1:T(8,128)(2,1)} %bitcast.2), channel_id=1, source_target_pairs={{0,9},{1,8},{2,11},{3,10},{4,13},{5,12},{6,15},{7,14},{8,1},{9,0},... | collective-permute-start | bytes 1769480 | tf_op jit(solution)/shard_map/ppermute | solution.py:32
  31.5 130.5 %collective-permute-start.1 = (bf16[128,2304]{0,1:T(8,128)(2,1)}, bf16[128,2304]{0,1:T(8,128)(2,1)}, u32[]{:S(2)}, u32[]{:S(2)}) collective-permute-start(bf16[128,2304]{0,1:T(8,128)(2,1)} %bitcast.2), channel_id=1, source_target_pairs={{0,8},{1,9},{2,10},{3,11},{4,12},{5,13},{6,14},{7,15},{8,0},{9,1},... | collective-permute-start | bytes 1769480 | tf_op jit(solution)/shard_map/ppermute | solution.py:32
  33.1 129.0 %collective-permute-start = (bf16[128,2304]{0,1:T(8,128)(2,1)}, bf16[128,2304]{0,1:T(8,128)(2,1)}, u32[]{:S(2)}, u32[]{:S(2)}) collective-permute-start(bf16[128,2304]{0,1:T(8,128)(2,1)} %bitcast.2), channel_id=1, source_target_pairs={{0,1},{1,0},{2,3},{3,2},{4,5},{5,4},{6,7},{7,6},{8,9},{9,8},{10,11... | collective-permute-start | bytes 1769480 | tf_op jit(solution)/shard_map/ppermute | solution.py:32
  52.7 358.9 %all-gather.6.cloned.1.call-start = ((), (), s32[]{:S(2)}) async-start(), calls=%async_computation.4 | async-start | bytes 6635520 | tf_op jit(solution)/shard_map/all_gather | solution.py:328
  54.3 53.6 %collective-permute-start.4 = (bf16[288,1152]{1,0:T(8,128)(2,1)S(1)}, bf16[288,1152]{1,0:T(8,128)(2,1)S(1)}, u32[]{:S(2)}, u32[]{:S(2)}) collective-permute-start(bf16[288,1152]{1,0:T(8,128)(2,1)S(1)} %bitcast.424), channel_id=1, source_target_pairs={{0,16},{1,17},{2,18},{3,19},{4,20},{5,21},{6,22},{7,23},{8,24},{9,... | collective-permute-start | bytes 1990664 | tf_op jit(solution)/shard_map/ppermute | solution.py:32
  109.3 48.1 %collective-permute-start.5 = (bf16[576,1152]{1,0:T(8,128)(2,1)}, bf16[576,1152]{1,0:T(8,128)(2,1)}, u32[]{:S(2)}, u32[]{:S(2)}) collective-permute-start(bf16[576,1152]{1,0:T(8,128)(2,1)} %bitcast.47), channel_id=1, source_target_pairs={{0,4},{1,5},{2,6},{3,7},{4,0},{5,1},{6,2},{7,3},{8,12},{9,13},{10,... | collective-permute-start | bytes 3981320 | tf_op jit(solution)/shard_map/ppermute | solution.py:32
  118.6 42.5 %collective-permute-start.26 = (bf16[144,2304]{1,0:T(8,128)(2,1)S(1)}, bf16[144,2304]{1,0:T(8,128)(2,1)S(1)}, u32[]{:S(2)}, u32[]{:S(2)}) collective-permute-start(bf16[144,2304]{1,0:T(8,128)(2,1)S(1)} %after.7), channel_id=1, source_target_pairs={{0,8},{1,9},{2,10},{3,11},{4,12},{5,13},{6,14},{7,15},{8,0},{9,1},... | collective-permute-start | bytes 1990664 | tf_op jit(solution)/shard_map/ppermute | solution.py:32
  157.4 25.9 %collective-permute-start.15 = (bf16[288,512]{1,0:T(8,128)(2,1)S(1)}, bf16[288,512]{1,0:T(8,128)(2,1)S(1)}, u32[]{:S(2)}, u32[]{:S(2)}) collective-permute-start(bf16[288,512]{1,0:T(8,128)(2,1)S(1)} %bitcast.438), channel_id=1, source_target_pairs={{0,16},{1,17},{2,18},{3,19},{4,20},{5,21},{6,22},{7,23},{8,24},{9,... | collective-permute-start | bytes 884744 | tf_op jit(solution)/shard_map/ppermute | solution.py:32
  161.1 26.8 %collective-permute-start.6 = (bf16[8,144,1152]{2,1,0:T(8,128)(2,1)}, bf16[8,144,1152]{2,1,0:T(8,128)(2,1)}, u32[]{:S(2)}, u32[]{:S(2)}) collective-permute-start(bf16[8,144,1152]{2,1,0:T(8,128)(2,1)} %bitcast.50), channel_id=1, source_target_pairs={{0,2},{1,3},{2,0},{3,1},{4,6},{5,7},{6,4},{7,5},{8,10},{9,11},{10,... | collective-permute-start | bytes 7962632 | tf_op jit(solution)/shard_map/ppermute | solution.py:32
  161.5 24.5 %collective-permute-start.27 = (bf16[2,144,1152]{2,1,0:T(8,128)(2,1)S(1)}, bf16[2,144,1152]{2,1,0:T(8,128)(2,1)S(1)}, u32[]{:S(2)}, u32[]{:S(2)}) collective-permute-start(bf16[2,144,1152]{2,1,0:T(8,128)(2,1)S(1)} %broadcast_select_fusion.8), channel_id=1, source_target_pairs={{0,2},{1,3},{2,0},{3,1},{4,6},{5,7},{6,4},{7,5},{8,10},{9,11},{10,... | collective-permute-start | bytes 1990664 | tf_op jit(solution)/shard_map/ppermute | solution.py:32
  183.4 17.5 %collective-permute-start.16 = (bf16[576,512]{1,0:T(8,128)(2,1)S(1)}, bf16[576,512]{1,0:T(8,128)(2,1)}, u32[]{:S(2)}, u32[]{:S(2)}) collective-permute-start(bf16[576,512]{1,0:T(8,128)(2,1)S(1)} %bitcast.425), channel_id=1, source_target_pairs={{0,4},{1,5},{2,6},{3,7},{4,0},{5,1},{6,2},{7,3},{8,12},{9,13},{10,... | collective-permute-start | bytes 1769480 | tf_op jit(solution)/shard_map/ppermute | solution.py:32
  186.0 65.1 %collective-permute-start.28 = (bf16[144,2304]{1,0:T(8,128)(2,1)S(1)}, bf16[144,2304]{1,0:T(8,128)(2,1)}, u32[]{:S(2)}, u32[]{:S(2)}) collective-permute-start(bf16[144,2304]{1,0:T(8,128)(2,1)S(1)} %after.8), channel_id=1, source_target_pairs={{0,8},{1,9},{2,10},{3,11},{4,12},{5,13},{6,14},{7,15},{8,0},{9,1},... | collective-permute-start | bytes 1990664 | tf_op jit(solution)/shard_map/ppermute | solution.py:32
  187.7 237.4 %all-gather.8.cloned.1.call-start = ((), (), s32[]{:S(2)}) async-start(), calls=%async_computation.5 | async-start | bytes 6635520 | tf_op jit(solution)/shard_map/all_gather | solution.py:328
  199.6 41.0 %collective-permute-start.7 = (bf16[512,256]{1,0:T(8,128)(2,1)S(1)}, bf16[512,256]{1,0:T(8,128)(2,1)S(1)}, u32[]{:S(2)}, u32[]{:S(2)}) collective-permute-start(bf16[512,256]{1,0:T(8,128)(2,1)S(1)} %pad_maximum_fusion.28), channel_id=1, source_target_pairs={{0,16},{1,17},{2,18},{3,19},{4,20},{5,21},{6,22},{7,23},{8,24},{9,... | collective-permute-start | bytes 786440 | tf_op jit(solution)/shard_map/ppermute | solution.py:32
  202.1 48.7 %collective-permute-start.10 = (bf16[512,256]{1,0:T(8,128)(2,1)S(1)}, bf16[512,256]{1,0:T(8,128)(2,1)S(1)}, u32[]{:S(2)}, u32[]{:S(2)}) collective-permute-start(bf16[512,256]{1,0:T(8,128)(2,1)S(1)} %slice.657), channel_id=1, source_target_pairs={{0,16},{1,17},{2,18},{3,19},{4,20},{5,21},{6,22},{7,23},{8,24},{9,... | collective-permute-start | bytes 786440 | tf_op jit(solution)/shard_map/ppermute | solution.py:32
  204.0 62.6 %collective-permute-start.17 = (bf16[8,144,512]{2,1,0:T(8,128)(2,1)S(1)}, bf16[8,144,512]{2,1,0:T(8,128)(2,1)S(1)}, u32[]{:S(2)}, u32[]{:S(2)}) collective-permute-start(bf16[8,144,512]{2,1,0:T(8,128)(2,1)S(1)} %bitcast.415), channel_id=1, source_target_pairs={{0,2},{1,3},{2,0},{3,1},{4,6},{5,7},{6,4},{7,5},{8,10},{9,11},{10,... | collective-permute-start | bytes 3538952 | tf_op jit(solution)/shard_map/ppermute | solution.py:32
  240.6 12.7 %collective-permute-start.8 = (bf16[1024,256]{1,0:T(8,128)(2,1)S(1)}, bf16[1024,256]{1,0:T(8,128)(2,1)S(1)}, u32[]{:S(2)}, u32[]{:S(2)}) collective-permute-start(bf16[1024,256]{1,0:T(8,128)(2,1)S(1)} %pad_maximum_fusion.23), channel_id=1, source_target_pairs={{0,4},{1,5},{2,6},{3,7},{4,0},{5,1},{6,2},{7,3},{8,12},{9,13},{10,... | collective-permute-start | bytes 1572872 | tf_op jit(solution)/shard_map/ppermute | solution.py:32
  250.9 15.6 %collective-permute-start.11 = (bf16[1024,256]{1,0:T(8,128)(2,1)S(1)}, bf16[1024,256]{1,0:T(8,128)(2,1)S(1)}, u32[]{:S(2)}, u32[]{:S(2)}) collective-permute-start(bf16[1024,256]{1,0:T(8,128)(2,1)S(1)} %pad_maximum_fusion.24), channel_id=1, source_target_pairs={{0,4},{1,5},{2,6},{3,7},{4,0},{5,1},{6,2},{7,3},{8,12},{9,13},{10,... | collective-permute-start | bytes 1572872 | tf_op jit(solution)/shard_map/ppermute | solution.py:32
  253.3 35.0 %collective-permute-start.29 = (bf16[2,144,1152]{2,1,0:T(8,128)(2,1)}, bf16[2,144,1152]{2,1,0:T(8,128)(2,1)}, u32[]{:S(2)}, u32[]{:S(2)}) collective-permute-start(bf16[2,144,1152]{2,1,0:T(8,128)(2,1)} %broadcast_select_fusion.6), channel_id=1, source_target_pairs={{0,2},{1,3},{2,0},{3,1},{4,6},{5,7},{6,4},{7,5},{8,10},{9,11},{10,... | collective-permute-start | bytes 1990664 | tf_op jit(solution)/shard_map/ppermute | solution.py:32
  253.4 13.8 %collective-permute-start.9 = (bf16[2048,256]{1,0:T(8,128)(2,1)S(1)}, bf16[2048,256]{1,0:T(8,128)(2,1)S(1)}, u32[]{:S(2)}, u32[]{:S(2)}) collective-permute-start(bf16[2048,256]{1,0:T(8,128)(2,1)S(1)} %pad_maximum_fusion.14), channel_id=1, source_target_pairs={{0,2},{1,3},{2,0},{3,1},{4,6},{5,7},{6,4},{7,5},{8,10},{9,11},{10,... | collective-permute-start | bytes 3145736 | tf_op jit(solution)/shard_map/ppermute | solution.py:32
  284.8 17.1 %collective-permute-start.18 = (bf16[128,2304]{1,0:T(8,128)(2,1)}, bf16[128,2304]{1,0:T(8,128)(2,1)}, u32[]{:S(2)}, u32[]{:S(2)}) collective-permute-start(bf16[128,2304]{1,0:T(8,128)(2,1)} %get-tuple-element.133), channel_id=1, source_target_pairs={{0,1},{1,0},{2,3},{3,2},{4,5},{5,4},{6,7},{7,6},{8,9},{9,8},{10,11... | collective-permute-start | bytes 1769480 | tf_op jit(solution)/shard_map/ppermute | solution.py:32
  286.2 44.5 %collective-permute-start.20 = (bf16[128,2304]{1,0:T(8,128)(2,1)}, bf16[128,2304]{1,0:T(8,128)(2,1)}, u32[]{:S(2)}, u32[]{:S(2)}) collective-permute-start(bf16[128,2304]{1,0:T(8,128)(2,1)} %get-tuple-element.134), channel_id=1, source_target_pairs={{0,9},{1,8},{2,11},{3,10},{4,13},{5,12},{6,15},{7,14},{8,1},{9,0},... | collective-permute-start | bytes 1769480 | tf_op jit(solution)/shard_map/ppermute | solution.py:32
  286.2 56.5 %collective-permute-start.19 = (bf16[128,2304]{1,0:T(8,128)(2,1)}, bf16[128,2304]{1,0:T(8,128)(2,1)}, u32[]{:S(2)}, u32[]{:S(2)}) collective-permute-start(bf16[128,2304]{1,0:T(8,128)(2,1)} %get-tuple-element.135), channel_id=1, source_target_pairs={{0,8},{1,9},{2,10},{3,11},{4,12},{5,13},{6,14},{7,15},{8,0},{9,1},... | collective-permute-start | bytes 1769480 | tf_op jit(solution)/shard_map/ppermute | solution.py:32
  291.0 617.6 %reduce-scatter.8.cloned.1.call-start = ((), (), s32[]{:S(2)}) async-start(), calls=%async_computation.8 | async-start | bytes 6635520 | tf_op jit(solution)/shard_map/reduce_scatter | solution.py:332
  348.4 31.5 %collective-permute-start.23 = (bf16[128,2304]{1,0:T(8,128)(2,1)S(1)}, bf16[128,2304]{1,0:T(8,128)(2,1)S(1)}, u32[]{:S(2)}, u32[]{:S(2)}) collective-permute-start(bf16[128,2304]{1,0:T(8,128)(2,1)S(1)} %get-tuple-element.83), channel_id=1, source_target_pairs={{0,9},{1,8},{2,11},{3,10},{4,13},{5,12},{6,15},{7,14},{8,1},{9,0},... | collective-permute-start | bytes 1769480 | tf_op jit(solution)/shard_map/ppermute | solution.py:32
  348.7 45.4 %collective-permute-start.22 = (bf16[128,2304]{1,0:T(8,128)(2,1)S(1)}, bf16[128,2304]{1,0:T(8,128)(2,1)S(1)}, u32[]{:S(2)}, u32[]{:S(2)}) collective-permute-start(bf16[128,2304]{1,0:T(8,128)(2,1)S(1)} %get-tuple-element.83), channel_id=1, source_target_pairs={{0,8},{1,9},{2,10},{3,11},{4,12},{5,13},{6,14},{7,15},{8,0},{9,1},... | collective-permute-start | bytes 1769480 | tf_op jit(solution)/shard_map/ppermute | solution.py:32
  351.2 42.9 %collective-permute-start.21 = (bf16[128,2304]{1,0:T(8,128)(2,1)S(1)}, bf16[128,2304]{1,0:T(8,128)(2,1)S(1)}, u32[]{:S(2)}, u32[]{:S(2)}) collective-permute-start(bf16[128,2304]{1,0:T(8,128)(2,1)S(1)} %get-tuple-element.83), channel_id=1, source_target_pairs={{0,1},{1,0},{2,3},{3,2},{4,5},{5,4},{6,7},{7,6},{8,9},{9,8},{10,11... | collective-permute-start | bytes 1769480 | tf_op jit(solution)/shard_map/ppermute | solution.py:32
  442.1 28.3 %collective-permute-start.31 = (bf16[128,2304]{1,0:T(8,128)(2,1)}, bf16[128,2304]{1,0:T(8,128)(2,1)}, u32[]{:S(2)}, u32[]{:S(2)}) collective-permute-start(bf16[128,2304]{1,0:T(8,128)(2,1)} %get-tuple-element.95), channel_id=1, source_target_pairs={{0,1},{1,0},{2,3},{3,2},{4,5},{5,4},{6,7},{7,6},{8,9},{9,8},{10,11... | collective-permute-start | bytes 1769480 | tf_op jit(solution)/shard_map/ppermute | solution.py:32
  443.6 26.9 %collective-permute-start.33 = (bf16[128,2304]{1,0:T(8,128)(2,1)}, bf16[128,2304]{1,0:T(8,128)(2,1)}, u32[]{:S(2)}, u32[]{:S(2)}) collective-permute-start(bf16[128,2304]{1,0:T(8,128)(2,1)} %get-tuple-element.96), channel_id=1, source_target_pairs={{0,9},{1,8},{2,11},{3,10},{4,13},{5,12},{6,15},{7,14},{8,1},{9,0},... | collective-permute-start | bytes 1769480 | tf_op jit(solution)/shard_map/ppermute | solution.py:32
  443.6 28.1 %collective-permute-start.32 = (bf16[128,2304]{1,0:T(8,128)(2,1)}, bf16[128,2304]{1,0:T(8,128)(2,1)}, u32[]{:S(2)}, u32[]{:S(2)}) collective-permute-start(bf16[128,2304]{1,0:T(8,128)(2,1)} %get-tuple-element.97), channel_id=1, source_target_pairs={{0,8},{1,9},{2,10},{3,11},{4,12},{5,13},{6,14},{7,15},{8,0},{9,1},... | collective-permute-start | bytes 1769480 | tf_op jit(solution)/shard_map/ppermute | solution.py:32
  475.8 17.3 %collective-permute-start.36 = (bf16[128,2304]{1,0:T(8,128)(2,1)S(1)}, bf16[128,2304]{1,0:T(8,128)(2,1)S(1)}, u32[]{:S(2)}, u32[]{:S(2)}) collective-permute-start(bf16[128,2304]{1,0:T(8,128)(2,1)S(1)} %get-tuple-element.79), channel_id=1, source_target_pairs={{0,9},{1,8},{2,11},{3,10},{4,13},{5,12},{6,15},{7,14},{8,1},{9,0},... | collective-permute-start | bytes 1769480 | tf_op jit(solution)/shard_map/ppermute | solution.py:32
  476.3 27.4 %collective-permute-start.35 = (bf16[128,2304]{1,0:T(8,128)(2,1)S(1)}, bf16[128,2304]{1,0:T(8,128)(2,1)S(1)}, u32[]{:S(2)}, u32[]{:S(2)}) collective-permute-start(bf16[128,2304]{1,0:T(8,128)(2,1)S(1)} %get-tuple-element.79), channel_id=1, source_target_pairs={{0,8},{1,9},{2,10},{3,11},{4,12},{5,13},{6,14},{7,15},{8,0},{9,1},... | collective-permute-start | bytes 1769480 | tf_op jit(solution)/shard_map/ppermute | solution.py:32
  478.8 24.9 %collective-permute-start.34 = (bf16[128,2304]{1,0:T(8,128)(2,1)S(1)}, bf16[128,2304]{1,0:T(8,128)(2,1)S(1)}, u32[]{:S(2)}, u32[]{:S(2)}) collective-permute-start(bf16[128,2304]{1,0:T(8,128)(2,1)S(1)} %get-tuple-element.79), channel_id=1, source_target_pairs={{0,1},{1,0},{2,3},{3,2},{4,5},{5,4},{6,7},{7,6},{8,9},{9,8},{10,11... | collective-permute-start | bytes 1769480 | tf_op jit(solution)/shard_map/ppermute | solution.py:32
  519.2 390.6 %reduce-scatter.4.cloned.1.call-start = ((), (), s32[]{:S(2)}) async-start(), calls=%async_computation.6 | async-start | bytes 6635520 | tf_op jit(solution)/shard_map/reduce_scatter | solution.py:332
  549.2 16.5 %collective-permute-start.38 = (bf16[512,2304]{1,0:T(8,128)(2,1)}, bf16[512,2304]{1,0:T(8,128)(2,1)}, u32[]{:S(2)}, u32[]{:S(2)}) collective-permute-start(bf16[512,2304]{1,0:T(8,128)(2,1)} %fusion.19), channel_id=1, source_target_pairs={{0,2},{1,3},{2,0},{3,1},{4,6},{5,7},{6,4},{7,5},{8,10},{9,11},{10,... | collective-permute-start | bytes 7077896 | tf_op jit(solution)/shard_map/ppermute | solution.py:32
  559.2 353.9 %reduce-scatter.6.cloned.1.call-start = ((), (), s32[]{:S(2)}) async-start(), calls=%async_computation.7 | async-start | bytes 6635520 | tf_op jit(solution)/shard_map/reduce_scatter | solution.py:332
  572.5 26.6 %collective-permute-start.39 = (bf16[128,2304]{1,0:T(8,128)(2,1)S(1)}, bf16[128,2304]{1,0:T(8,128)(2,1)S(1)}, u32[]{:S(2)}, u32[]{:S(2)}) collective-permute-start(bf16[128,2304]{1,0:T(8,128)(2,1)S(1)} %get-tuple-element.92), channel_id=1, source_target_pairs={{0,1},{1,0},{2,3},{3,2},{4,5},{5,4},{6,7},{7,6},{8,9},{9,8},{10,11... | collective-permute-start | bytes 1769480 | tf_op jit(solution)/shard_map/ppermute | solution.py:32
  573.9 29.2 %collective-permute-start.41 = (bf16[128,2304]{1,0:T(8,128)(2,1)S(1)}, bf16[128,2304]{1,0:T(8,128)(2,1)S(1)}, u32[]{:S(2)}, u32[]{:S(2)}) collective-permute-start(bf16[128,2304]{1,0:T(8,128)(2,1)S(1)} %get-tuple-element.93), channel_id=1, source_target_pairs={{0,9},{1,8},{2,11},{3,10},{4,13},{5,12},{6,15},{7,14},{8,1},{9,0},... | collective-permute-start | bytes 1769480 | tf_op jit(solution)/shard_map/ppermute | solution.py:32
  574.7 49.5 %collective-permute-start.40 = (bf16[128,2304]{1,0:T(8,128)(2,1)S(1)}, bf16[128,2304]{1,0:T(8,128)(2,1)S(1)}, u32[]{:S(2)}, u32[]{:S(2)}) collective-permute-start(bf16[128,2304]{1,0:T(8,128)(2,1)S(1)} %get-tuple-element.94), channel_id=1, source_target_pairs={{0,8},{1,9},{2,10},{3,11},{4,12},{5,13},{6,14},{7,15},{8,0},{9,1},... | collective-permute-start | bytes 1769480 | tf_op jit(solution)/shard_map/ppermute | solution.py:32
  627.7 27.4 %collective-permute-start.44 = (bf16[128,2304]{1,0:T(8,128)(2,1)}, bf16[128,2304]{1,0:T(8,128)(2,1)}, u32[]{:S(2)}, u32[]{:S(2)}) collective-permute-start(bf16[128,2304]{1,0:T(8,128)(2,1)} %fusion.37), channel_id=1, source_target_pairs={{0,9},{1,8},{2,11},{3,10},{4,13},{5,12},{6,15},{7,14},{8,1},{9,0},... | collective-permute-start | bytes 1769480 | tf_op jit(solution)/shard_map/ppermute | solution.py:32
  628.2 48.5 %collective-permute-start.43 = (bf16[128,2304]{1,0:T(8,128)(2,1)}, bf16[128,2304]{1,0:T(8,128)(2,1)}, u32[]{:S(2)}, u32[]{:S(2)}) collective-permute-start(bf16[128,2304]{1,0:T(8,128)(2,1)} %fusion.37), channel_id=1, source_target_pairs={{0,8},{1,9},{2,10},{3,11},{4,12},{5,13},{6,14},{7,15},{8,0},{9,1},... | collective-permute-start | bytes 1769480 | tf_op jit(solution)/shard_map/ppermute | solution.py:32
  630.6 46.0 %collective-permute-start.42 = (bf16[128,2304]{1,0:T(8,128)(2,1)}, bf16[128,2304]{1,0:T(8,128)(2,1)}, u32[]{:S(2)}, u32[]{:S(2)}) collective-permute-start(bf16[128,2304]{1,0:T(8,128)(2,1)} %fusion.37), channel_id=1, source_target_pairs={{0,1},{1,0},{2,3},{3,2},{4,5},{5,4},{6,7},{7,6},{8,9},{9,8},{10,11... | collective-permute-start | bytes 1769480 | tf_op jit(solution)/shard_map/ppermute | solution.py:32
  688.5 32.1 %collective-permute-start.55 = (bf16[8,144,512]{2,1,0:T(8,128)(2,1)}, bf16[8,144,512]{2,1,0:T(8,128)(2,1)}, u32[]{:S(2)}, u32[]{:S(2)}) collective-permute-start(bf16[8,144,512]{2,1,0:T(8,128)(2,1)} %fusion.43), channel_id=1, source_target_pairs={{0,2},{1,3},{2,0},{3,1},{4,6},{5,7},{6,4},{7,5},{8,10},{9,11},{10,... | collective-permute-start | bytes 3538952 | tf_op jit(solution)/shard_map/ppermute | solution.py:32
  710.9 14.9 %collective-permute-start.45 = (bf16[2048,512]{1,0:T(8,128)(2,1)}, bf16[2048,512]{1,0:T(8,128)(2,1)}, u32[]{:S(2)}, u32[]{:S(2)}) collective-permute-start(bf16[2048,512]{1,0:T(8,128)(2,1)} %get-tuple-element.24), channel_id=1, source_target_pairs={{0,2},{1,3},{2,0},{3,1},{4,6},{5,7},{6,4},{7,5},{8,10},{9,11},{10,... | collective-permute-start | bytes 6291464 | tf_op jit(solution)/shard_map/ppermute | solution.py:32
  724.3 16.4 %collective-permute-start.56 = (bf16[576,512]{1,0:T(8,128)(2,1)}, bf16[576,512]{1,0:T(8,128)(2,1)}, u32[]{:S(2)}, u32[]{:S(2)}) collective-permute-start(bf16[576,512]{1,0:T(8,128)(2,1)} %fusion.92), channel_id=1, source_target_pairs={{0,4},{1,5},{2,6},{3,7},{4,0},{5,1},{6,2},{7,3},{8,12},{9,13},{10,... | collective-permute-start | bytes 1769480 | tf_op jit(solution)/shard_map/ppermute | solution.py:32
  731.3 49.2 %collective-permute-start.46 = (bf16[1024,512]{1,0:T(8,128)(2,1)}, bf16[1024,512]{1,0:T(8,128)(2,1)S(1)}, u32[]{:S(2)}, u32[]{:S(2)}) collective-permute-start(bf16[1024,512]{1,0:T(8,128)(2,1)} %slice.655), channel_id=1, source_target_pairs={{0,4},{1,5},{2,6},{3,7},{4,0},{5,1},{6,2},{7,3},{8,12},{9,13},{10,... | collective-permute-start | bytes 3145736 | tf_op jit(solution)/shard_map/ppermute | solution.py:32
  742.4 41.5 %collective-permute-start.57 = (bf16[288,512]{1,0:T(8,128)(2,1)S(1)}, bf16[288,512]{1,0:T(8,128)(2,1)S(1)}, u32[]{:S(2)}, u32[]{:S(2)}) collective-permute-start(bf16[288,512]{1,0:T(8,128)(2,1)S(1)} %fusion.123), channel_id=1, source_target_pairs={{0,16},{1,17},{2,18},{3,19},{4,20},{5,21},{6,22},{7,23},{8,24},{9,... | collective-permute-start | bytes 884744 | tf_op jit(solution)/shard_map/ppermute | solution.py:32
  780.9 46.4 %collective-permute-start.47 = (bf16[512,512]{1,0:T(8,128)(2,1)S(1)}, bf16[512,512]{1,0:T(8,128)(2,1)S(1)}, u32[]{:S(2)}, u32[]{:S(2)}) collective-permute-start(bf16[512,512]{1,0:T(8,128)(2,1)S(1)} %slice.656), channel_id=1, source_target_pairs={{0,16},{1,17},{2,18},{3,19},{4,20},{5,21},{6,22},{7,23},{8,24},{9,... | collective-permute-start | bytes 1572872 | tf_op jit(solution)/shard_map/ppermute | solution.py:32
  834.7 27.9 %collective-permute-start.48 = (bf16[128,2304]{1,0:T(8,128)(2,1)S(1)}, bf16[128,2304]{1,0:T(8,128)(2,1)S(1)}, u32[]{:S(2)}, u32[]{:S(2)}) collective-permute-start(bf16[128,2304]{1,0:T(8,128)(2,1)S(1)} %get-tuple-element.130), channel_id=1, source_target_pairs={{0,1},{1,0},{2,3},{3,2},{4,5},{5,4},{6,7},{7,6},{8,9},{9,8},{10,11... | collective-permute-start | bytes 1769480 | tf_op jit(solution)/shard_map/ppermute | solution.py:32
  836.4 27.5 %collective-permute-start.50 = (bf16[128,2304]{1,0:T(8,128)(2,1)S(1)}, bf16[128,2304]{1,0:T(8,128)(2,1)S(1)}, u32[]{:S(2)}, u32[]{:S(2)}) collective-permute-start(bf16[128,2304]{1,0:T(8,128)(2,1)S(1)} %get-tuple-element.131), channel_id=1, source_target_pairs={{0,9},{1,8},{2,11},{3,10},{4,13},{5,12},{6,15},{7,14},{8,1},{9,0},... | collective-permute-start | bytes 1769480 | tf_op jit(solution)/shard_map/ppermute | solution.py:32
  836.4 42.0 %collective-permute-start.49 = (bf16[128,2304]{1,0:T(8,128)(2,1)S(1)}, bf16[128,2304]{1,0:T(8,128)(2,1)S(1)}, u32[]{:S(2)}, u32[]{:S(2)}) collective-permute-start(bf16[128,2304]{1,0:T(8,128)(2,1)S(1)} %get-tuple-element.132), channel_id=1, source_target_pairs={{0,8},{1,9},{2,10},{3,11},{4,12},{5,13},{6,14},{7,15},{8,0},{9,1},... | collective-permute-start | bytes 1769480 | tf_op jit(solution)/shard_map/ppermute | solution.py:32
  844.6 52.0 %collective-permute-start.51 = (bf16[8,144,1024]{2,1,0:T(8,128)(2,1)}, bf16[8,144,1024]{2,1,0:T(8,128)(2,1)}, u32[]{:S(2)}, u32[]{:S(2)}) collective-permute-start(bf16[8,144,1024]{2,1,0:T(8,128)(2,1)} %fusion.34), channel_id=1, source_target_pairs={{0,2},{1,3},{2,0},{3,1},{4,6},{5,7},{6,4},{7,5},{8,10},{9,11},{10,... | collective-permute-start | bytes 7077896 | tf_op jit(solution)/shard_map/ppermute | solution.py:32
  895.1 12.9 %collective-permute-start.69 = (f32[1,4,144]{2,0,1:T(1,128)S(1)}, f32[1,4,144]{2,0,1:T(1,128)S(1)}, u32[]{:S(2)}, u32[]{:S(2)}) collective-permute-start(f32[1,4,144]{2,0,1:T(1,128)S(1)} %fusion.167), channel_id=1, source_target_pairs={{0,1},{1,0},{2,3},{3,2},{4,5},{5,4},{6,7},{7,6},{8,9},{9,8},{10,11... | collective-permute-start | bytes 6920 | tf_op jit(solution)/shard_map/ppermute | solution.py:32
  904.0 28.2 %collective-permute-start.52 = (bf16[576,1024]{1,0:T(8,128)(2,1)}, bf16[576,1024]{1,0:T(8,128)(2,1)}, u32[]{:S(2)}, u32[]{:S(2)}) collective-permute-start(bf16[576,1024]{1,0:T(8,128)(2,1)} %fusion.42), channel_id=1, source_target_pairs={{0,4},{1,5},{2,6},{3,7},{4,0},{5,1},{6,2},{7,3},{8,12},{9,13},{10,... | collective-permute-start | bytes 3538952 | tf_op jit(solution)/shard_map/ppermute | solution.py:32
  909.8 25.0 %collective-permute-start.63 = (bf16[2,144,1152]{2,1,0:T(8,128)(2,1)S(1)}, bf16[2,144,1152]{2,1,0:T(8,128)(2,1)}, u32[]{:S(2)}, u32[]{:S(2)}) collective-permute-start(bf16[2,144,1152]{2,1,0:T(8,128)(2,1)S(1)} %dynamic-slice_bitcast_fusion), channel_id=1, source_target_pairs={{0,8},{1,9},{2,10},{3,11},{4,12},{5,13},{6,14},{7,15},{8,0},{9,1},... | collective-permute-start | bytes 1990664 | tf_op jit(solution)/shard_map/ppermute | solution.py:32
  911.0 43.5 %collective-permute-start.59 = (bf16[2,144,1152]{2,1,0:T(8,128)(2,1)S(1)}, bf16[2,144,1152]{2,1,0:T(8,128)(2,1)S(1)}, u32[]{:S(2)}, u32[]{:S(2)}) collective-permute-start(bf16[2,144,1152]{2,1,0:T(8,128)(2,1)S(1)} %dynamic-slice_bitcast_fusion.2), channel_id=1, source_target_pairs={{0,8},{1,9},{2,10},{3,11},{4,12},{5,13},{6,14},{7,15},{8,0},{9,1},... | collective-permute-start | bytes 1990664 | tf_op jit(solution)/shard_map/ppermute | solution.py:32
  914.2 53.6 %collective-permute-start.61 = (bf16[2,144,1152]{2,1,0:T(8,128)(2,1)S(1)}, bf16[2,144,1152]{2,1,0:T(8,128)(2,1)S(1)}, u32[]{:S(2)}, u32[]{:S(2)}) collective-permute-start(bf16[2,144,1152]{2,1,0:T(8,128)(2,1)S(1)} %dynamic-slice_bitcast_fusion.1), channel_id=1, source_target_pairs={{0,8},{1,9},{2,10},{3,11},{4,12},{5,13},{6,14},{7,15},{8,0},{9,1},... | collective-permute-start | bytes 1990664 | tf_op jit(solution)/shard_map/ppermute | solution.py:32
  934.7 30.5 %collective-permute-start.53 = (bf16[288,1024]{1,0:T(8,128)(2,1)S(1)}, bf16[288,1024]{1,0:T(8,128)(2,1)S(1)}, u32[]{:S(2)}, u32[]{:S(2)}) collective-permute-start(bf16[288,1024]{1,0:T(8,128)(2,1)S(1)} %fusion.91), channel_id=1, source_target_pairs={{0,16},{1,17},{2,18},{3,19},{4,20},{5,21},{6,22},{7,23},{8,24},{9,... | collective-permute-start | bytes 1769480 | tf_op jit(solution)/shard_map/ppermute | solution.py:32
  936.2 40.4 %collective-permute-start.64 = (bf16[2,144,1152]{2,1,0:T(8,128)(2,1)S(1)}, bf16[2,144,1152]{2,1,0:T(8,128)(2,1)S(1)}, u32[]{:S(2)}, u32[]{:S(2)}) collective-permute-start(bf16[2,144,1152]{2,1,0:T(8,128)(2,1)S(1)} %fusion.74), channel_id=1, source_target_pairs={{0,2},{1,3},{2,0},{3,1},{4,6},{5,7},{6,4},{7,5},{8,10},{9,11},{10,... | collective-permute-start | bytes 1990664 | tf_op jit(solution)/shard_map/ppermute | solution.py:32
  954.8 22.0 %collective-permute-start.60 = (bf16[2,144,1152]{2,1,0:T(8,128)(2,1)S(1)}, bf16[2,144,1152]{2,1,0:T(8,128)(2,1)S(1)}, u32[]{:S(2)}, u32[]{:S(2)}) collective-permute-start(bf16[2,144,1152]{2,1,0:T(8,128)(2,1)S(1)} %fusion.82), channel_id=1, source_target_pairs={{0,2},{1,3},{2,0},{3,1},{4,6},{5,7},{6,4},{7,5},{8,10},{9,11},{10,... | collective-permute-start | bytes 1990664 | tf_op jit(solution)/shard_map/ppermute | solution.py:32
  968.1 9.1 collective-permute-start.62
  (71 other events, 996.3 us)
Sparse Core Ops, SparseCore 0:
  52.8 142.5 all-gather.3
  197.8 120.1 all-gather.5
  320.3 104.7 all-gather.7
  519.3 104.3 reduce-scatter.7
  626.6 104.3 reduce-scatter.3
  733.8 138.4 reduce-scatter.5

commit v3 on v2

--- a/solution.py
+++ b/solution.py
@@ -86,15 +86,18 @@
 
 
 def spread_rows(rows):
-    return jnp.concatenate([rows, swap(rows, X), swap(rows, ZL), swap(rows, X | ZL)], axis=0)
-
-
-def return_rows(own, others):
+    return jnp.concatenate([rows, swap(rows, X), swap(rows, Y), swap(rows, X | Y)], axis=0)
+
+
+def return_rows(own, others, first=None):
     count = own.shape[0]
     total = own
-    for place, mask in enumerate((X, ZL, X | ZL)):
+    for place, mask in enumerate((X, Y, X | Y)):
         part = others[place * count : (place + 1) * count]
-        total = total + swap(part, mask).astype(f32)
+        got = swap(part, mask)
+        if first is not None:
+            got = after(got, first)
+        total = total + got.astype(f32)
     return total
 
 
@@ -293,49 +296,49 @@
     )(base, limit, lse, delta, query, mixed_grad, keys, values)
 
 
-def gather_attention_weight(piece, first=None):
+def gather_attention_weight(piece):
     rows = piece.shape[0]
-    sent, own = split_axis(piece, ZL, 1)
-    if first is not None:
-        sent = after(sent, first)
-    got = swap(sent, ZL)
-    full = ordered_stack(own, got, ZL, 0).reshape(2 * rows, -1)
-    full = join(join(full, ZH), Y)
-    block = full.reshape(8, rows, -1)
-    full = ordered_stack(block, swap(block, C), C, 1).reshape(16 * rows, -1)
-    if lax.axis_size("outer") > 1:
-        full = lax.all_gather(full, "outer", axis=0, tiled=True)
-    return full, got
-
-
-def reduce_attention_grad(value):
+    sent, own = split_axis(piece, Y, 1)
+    got = swap(sent, Y)
+    full = ordered_stack(own, got, Y, 0).reshape(2 * rows, -1)
+    full = lax.all_gather(full, ("outer", "zh", "zl", "c"), axis=0, tiled=True)
+    full = full.reshape(-1, 2, 2, rows, full.shape[1]).swapaxes(1, 2)
+    return full.reshape(-1, full.shape[-1]), got
+
+
+def fold_cores(value):
     if lax.axis_size("outer") > 1:
         value = lax.psum_scatter(value.astype(bf16), "outer", scatter_dimension=0, tiled=True)
-    rows = value.shape[0] // 16
-    value = fold(value.reshape(8, 2, rows, -1), C, 1)
-    value = fold(value.reshape(2, 4 * rows, -1), Y, 0)
-    value = fold(value.reshape(2, 2 * rows, -1), ZH, 0)
-    sent, own = split_axis(value.astype(bf16).reshape(2, rows, -1), ZL, 0)
-    return ordered_stack(own, swap(sent, ZL), ZL, 1).astype(f32)
-
-
-def gather_ffn_weight(piece, first):
+    return fold(value.reshape(8, 2, value.shape[0] // 16, -1), C, 1)
+
+
+def fold_rest(value):
+    rows = value.shape[1]
+    value = fold(value.reshape(2, 2, 2 * rows, -1), ZL, 1)
+    value = fold(value, ZH, 0)
+    sent, own = split_axis(value.astype(bf16).reshape(2, rows, -1), Y, 0)
+    return ordered_stack(own, swap(sent, Y), Y, 1).astype(f32)
+
+
+def gather_ffn_weight(piece, first, begin=None):
     rows = piece.shape[0]
-    sent, own = split_columns(piece, ZL)
-    got = swap(after(sent, first), ZL)
-    sent, own = split_columns(ordered_stack(own, got, ZL, 0), C)
+    sent, own = split_columns(piece, Y)
+    got = swap(after(sent, first), Y)
+    sent, own = split_columns(ordered_stack(own, got, Y, 0), C)
     block = ordered_stack(own, swap(sent, C), C, 1).reshape(4 * rows, -1)
-    return lax.all_gather(block, ("outer", "y", "zh"), axis=0, tiled=True), got
+    if begin is not None:
+        block = after(block, begin)
+    return lax.all_gather(block, ("outer", "zh", "zl"), axis=0, tiled=True), got
 
 
 def scatter_ffn_grad(terms):
-    return lax.psum_scatter(terms, ("outer", "y", "zh"), scatter_dimension=0, tiled=True)
+    return lax.psum_scatter(terms, ("outer", "zh", "zl"), scatter_dimension=0, tiled=True)
 
 
 def return_ffn_grad(value):
     split = value.reshape(2, 2, value.shape[0] // 4, -1)
-    sent, own = split_axis(split, ZL, 0)
-    sent, own = split_axis(ordered_stack(own, swap(sent, ZL), ZL, 0), C, 1)
+    sent, own = split_axis(split, Y, 0)
+    sent, own = split_axis(ordered_stack(own, swap(sent, Y), Y, 0), C, 1)
     split = ordered_stack(own, swap(sent, C), C, 1)
     return jnp.concatenate(
         [split[a, b].astype(f32) for a in range(2) for b in range(2)], axis=1
@@ -346,7 +349,7 @@
     value = value.reshape(4, 16 * lax.axis_size("outer"), -1).transpose(1, 0, 2)
     if lax.axis_size("outer") > 1:
         value = lax.psum_scatter(value, "outer", scatter_dimension=0, tiled=True)
-    for mask in (Y, ZH, ZL, C):
+    for mask in (ZH, ZL, Y, C):
         sent, kept = split_axis(value.reshape((2, value.shape[0] // 2) + value.shape[1:]), mask, 0)
         value = kept + swap(sent, mask)
     return (value + swap(value, X))[0]
@@ -373,39 +376,29 @@
     outer = lax.axis_size("outer")
     me = device_index()
 
-    def permuted(value):
-        lead = value.shape[0]
-        split = value.reshape(lead, outer, 4, 2, 2 * rows)
-        return split.swapaxes(2, 3).reshape(lead, width)
-
-    def restored(value):
-        lead = value.shape[0]
-        split = value.reshape(lead, outer, 2, 4, 2 * rows)
-        return split.swapaxes(2, 3).reshape(lead, width)
-
     gains_own = jnp.stack([attn_gain, post_attn_gain, ffn_gain, post_ffn_gain], axis=1)
     gains_own = jnp.pad(gains_own.astype(bf16), ((0, 0), (0, 124)))[:, None]
     q_split = q_weight.astype(bf16).reshape(rows, 2, -1)
     k_split = k_weight.astype(bf16).reshape(rows, 2, -1)
     v_split = v_weight.astype(bf16).reshape(rows, 2, -1)
-    qkv_full, got = gather_attention_weight(
-        jnp.concatenate([q_split, k_split, v_split, jnp.tile(gains_own, (1, 2, 1))], axis=2)
-    )
-    gains = qkv_full[:, 4 * HEAD_DIM : 4 * HEAD_DIM + 4].astype(f32).T
-    qkv_full = qkv_full[:, : 4 * HEAD_DIM]
+    out_split = out_weight.T.astype(bf16).reshape(rows, 2, -1)
+    full, got = gather_attention_weight(
+        jnp.concatenate([q_split, k_split, v_split, out_split, jnp.tile(gains_own, (1, 2, 1))], axis=2)
+    )
+    qkv_full, out_full = full[:, : 4 * HEAD_DIM], full[:, 4 * HEAD_DIM : 6 * HEAD_DIM]
+    gains = full[:, 6 * HEAD_DIM : 6 * HEAD_DIM + 4].astype(f32).T
     gain_one, gain_two, gain_three, gain_four = (gains[i] for i in range(4))
-    gate_full, got = gather_ffn_weight(gate_weight.astype(bf16), got)
-    up_full, got_up = gather_ffn_weight(up_weight.astype(bf16), got)
-    out_full, got = gather_attention_weight(out_weight.T.astype(bf16).reshape(rows, 2, -1), got)
-    down_full, got = gather_ffn_weight(down_weight.T.astype(bf16), got_up)
-
-    row_bases = [((me ^ mask) * own_rows) % SEQ_LEN for mask in (0, X, ZL, X | ZL)]
+    gate_full, got = gather_ffn_weight(gate_weight.astype(bf16), got, full)
+    up_full, got = gather_ffn_weight(up_weight.astype(bf16), got)
+    down_full, got = gather_ffn_weight(down_weight.T.astype(bf16), got)
+
+    row_bases = [((me ^ mask) * own_rows) % SEQ_LEN for mask in (0, X, Y, X | Y)]
     lane = jnp.arange(own_rows, dtype=jnp.int32)
     query_pos = jnp.concatenate([base + lane for base in row_bases])
     key_bases = []
     for group in range(8):
-        flips = (ZH if group & 1 else 0) | (Y if group & 2 else 0) | (C if group & 4 else 0)
-        for mask in (0, X, ZL, X | ZL):
+        flips = (ZH if group & 1 else 0) | (ZL if group & 2 else 0) | (C if group & 4 else 0)
+        for mask in (0, X, Y, X | Y):
             key_bases.append(((me ^ (flips | mask)) * own_rows) % SEQ_LEN)
     key_bases = jnp.stack(key_bases).astype(jnp.int32)
     prefix_len = lax.dynamic_index_in_dim(prefix, me // 32, 0, keepdims=False)
@@ -415,11 +408,10 @@
     angles = query_pos.astype(f32)[:, None] * frequency[None, :]
     cosine, sine = jnp.cos(angles), jnp.sin(angles)
 
-    own_tokens = permuted(tokens)
-    resid = own_tokens.astype(f32)
-    upstream = permuted(cotangent).astype(f32)
-
-    hidden_one = rms_scale(spread_rows(own_tokens).astype(f32), gain_one).astype(bf16)
+    resid = tokens.astype(f32)
+    upstream = cotangent.astype(f32)
+
+    hidden_one = rms_scale(spread_rows(tokens).astype(f32), gain_one).astype(bf16)
     projected = mm(hidden_one, qkv_full)
     scale = HEAD_DIM ** (-0.5)
     query_rot = jnp.concatenate(
@@ -431,7 +423,7 @@
     )
     keys = rotate(projected[:, 2 * HEAD_DIM : 3 * HEAD_DIM], cosine, sine).astype(bf16)
     values = projected[:, 3 * HEAD_DIM :].astype(bf16)
-    for mask in (ZH, Y, C):
+    for mask in (ZH, ZL, C):
         keys = jnp.concatenate([keys, swap(keys, mask)], axis=0)
         values = jnp.concatenate([values, swap(values, mask)], axis=0)
     mixed, mixed_low, lse = attend(key_bases, limit, query_rot, keys, values)
@@ -476,31 +468,34 @@
     up_grad_part = up_grad_part.astype(bf16)
     normed_three_grad = share_out([(gate_grad_part, gate_full), (up_grad_part, up_full)])
     gate_sums = scatter_ffn_grad(contract_rows(hidden_two, gate_grad_part).astype(bf16))
-    up_sums = scatter_ffn_grad(contract_rows(hidden_two, up_grad_part).astype(bf16))
-    down_block = return_ffn_grad(down_sums)
-    gate_block = return_ffn_grad(gate_sums)
-    up_block = return_ffn_grad(up_sums)
+    up_terms = contract_rows(hidden_two, up_grad_part).astype(bf16)
     unused_three, ffn_norm_pull = jax.vjp(rms_scale, resid_two, gain_three)
     resid_two_extra, gain_three_grad = ffn_norm_pull(normed_three_grad)
     resid_two_grad = upstream + resid_two_extra
 
     unused_two, post_attn_pull = jax.vjp(rms_scale, attn_sum, gain_two)
     attn_grad, gain_two_grad = post_attn_pull(resid_two_grad)
-    attn_grad_rows = spread_rows(attn_grad.astype(bf16))
-    mixed_grad = mm(attn_grad_rows, out_full).astype(bf16)
+    attn_grad_rows = spread_rows(after(attn_grad.astype(bf16), up_terms))
+    out_terms = fold_cores(contract_rows(attn_grad_rows, mixed_low))
+    mixed_grad = after(mm(attn_grad_rows, out_full).astype(bf16), down_sums, out_terms)
     delta = jnp.sum(
         (mixed_grad.astype(f32) * mixed).reshape(-1, 2, HEAD_DIM), axis=-1
     ).T
     query_grad, key_value_grad, sent = attend_back(
         key_bases, limit, lse, delta, query_rot, mixed_grad, keys, values
     )
-    for mask in (C, Y, ZH):
-        key_value_grad = key_value_grad + swap(sent, mask).astype(f32)
+    for mask in (C, ZL, ZH):
+        got = swap(sent, mask)
+        key_value_grad = key_value_grad + got.astype(f32)
         if mask != ZH:
             count = key_value_grad.shape[0] // 2
             sent = key_value_grad[count:].astype(bf16)
             key_value_grad = key_value_grad[:count]
-    out_block = reduce_attention_grad(contract_rows(attn_grad_rows, mixed_low))
+    out_block = fold_rest(out_terms)
+    up_sums = scatter_ffn_grad(after(up_terms, got))
+    down_block = return_ffn_grad(after(down_sums, got))
+    gate_block = return_ffn_grad(after(gate_sums, got))
+    up_block = return_ffn_grad(up_sums)
     qkv_grad = jnp.concatenate(
         [
             rotate(query_grad[:, :HEAD_DIM], cosine, -sine),
@@ -512,16 +507,17 @@
     ).astype(bf16)
     normed_others = contract_cols(qkv_grad[own_rows:], qkv_full).astype(bf16)
     normed_own = contract_cols(qkv_grad[:own_rows], qkv_full)
-    normed_one_grad = return_rows(normed_own, normed_others)
-    qkv_block = reduce_attention_grad(contract_rows(hidden_one, qkv_grad))
+    qkv_terms = fold_cores(contract_rows(hidden_one, qkv_grad))
+    normed_one_grad = return_rows(normed_own, normed_others, qkv_terms)
+    qkv_block = fold_rest(qkv_terms)
     unused_one, attn_norm_pull = jax.vjp(rms_scale, resid, gain_one)
     resid_extra, gain_one_grad = attn_norm_pull(normed_one_grad)
-    input_grad = restored(resid_two_grad + resid_extra)
+    input_grad = resid_two_grad + resid_extra
     gain_rows = reduce_gains(
         jnp.stack([gain_one_grad, gain_two_grad, gain_three_grad, gain_four_grad])
     )
     return (
-        restored(layer_out.astype(bf16)),
+        layer_out.astype(bf16),
         input_grad,
         qkv_block[:, :, : 2 * HEAD_DIM].reshape(rows, -1),
         qkv_block[:, :, 2 * HEAD_DIM : 3 * HEAD_DIM].reshape(rows, -1),

time: 998 us -> 970 us (0.972)
  waiting for transfers between devices: 609 us -> 593 us
    ppermute x70 -> x63, waiting for transfers between devices: 608 us -> 492 us  [swap(): return lax.ppermute(value, AXES, [(i, i ^ mask) for i in range(count)])]
    all_gather x3 -> x4, waiting for transfers between devices: 1.04 us -> 101 us  [the longest x1 55.4 us: gather_attention_weight(): full = lax.all_gather(full, ('outer', 'zh', 'zl', 'c'), axis=0, tiled=True)]
    another operation x30 -> x16, other arithmetic: 18.7 us -> 5.58 us  [ordered_stack(): jnp.stack([jnp.where(first, own, other), jnp.where(first, other, own)], a...]
    unnamed x131 -> x178, local copies, waits for them, and re-layouts: 27.7 us -> 35.3 us
    ppermute x70 -> x63, starting transfers between devices: 62.8 us -> 64.1 us  [swap(): return lax.ppermute(value, AXES, [(i, i ^ mask) for i in range(count)])]
  transfers between devices with their start and end apart: 76 -> 70, of which waited for: 43 -> 45; matrix products, arithmetic and copies ran while one was open for 21% -> 20% of each run, Pallas kernels for 3% -> 3%
where the time goes in v3:
time: 970 us; the launch traced here: 964 us
  waiting for transfers between devices  593 us (61%)
  matrix products  117 us (12%)
  other arithmetic  75.2 us (8%)
  starting transfers between devices  64.5 us (7%)
  local copies, waits for them, and re-layouts  64.2 us (7%)
  Pallas kernels  32.9 us (3%)
  between operations  17.2 us (2%)
    ppermute x63, waiting for transfers between devices, swap(): return lax.ppermute(value, AXES, [(i, i ^ mask) for i in range(count)])  492 us
    ppermute x63, starting transfers between devices, swap(): return lax.ppermute(value, AXES, [(i, i ^ mask) for i in range(count)])  64.1 us
    all_gather x1, waiting for transfers between devices, gather_attention_weight(): full = lax.all_gather(full, ('outer', 'zh', 'zl', 'c'), axis=0, tiled=True)  55.4 us
    dot_general x5, matrix products, mm(): return jnp.dot(left, right, preferred_element_type=f32)  46.5 us
    all_gather x3, waiting for transfers between devices, gather_ffn_weight(): lax.all_gather(block, ('outer', 'zh', 'zl'), axis=0, tiled=True)  45.5 us
    dot_general x10, matrix products, contract_cols(): lax.dot_general(left, right, (((1,), (1,)), ((), ())), preferred_element_...  36 us
    unnamed x178, local copies, waits for them, and re-layouts  35.3 us
    dot_general x5, matrix products, contract_rows(): lax.dot_general(left, right, (((0,), (0,)), ((), ())), preferred_element_...  34.8 us
  transfers between devices with their start and end apart: 70, of which 45 were waited for; matrix products, arithmetic and copies ran while one was open for 20% of the time, Pallas kernels for 3%

profile of v3, /device:TPU:0, one launch (start us, length us, event | category | flops | bytes accessed | tf_op | source)
XLA Modules:
  0.0 964.5 jit_solution(4107114895096738737)
XLA Ops:
  11.0 3.0 collective-permute-start.3
  14.1 11.0 %collective-permute-done.3.refs_1_ = bf16[144,1664]{1,0:T(8,128)(2,1)S(1)} collective-permute-done((bf16[144,1664]{1,0:T(8,128)(2,1)S(1)}, bf16[144,1664]{1,0:T(8,128)(2,1)S(1)}, u32[]{:S(2)}, u32[]{:S(2)}) %collective-permute-start.3) | collective-permute-done | bytes 479264 | tf_op jit(solution)/shard_map/ppermute | solution.py:32
  30.0 14.4 %collective-permute-done.17.refs_1_ = bf16[144,2304]{1,0:T(8,128)(2,1)S(1)} collective-permute-done((bf16[144,2304]{1,0:T(8,128)(2,1)S(1)}, bf16[144,2304]{1,0:T(8,128)(2,1)S(1)}, u32[]{:S(2)}, u32[]{:S(2)}) %collective-permute-start.17) | collective-permute-done | bytes 663584 | tf_op jit(solution)/shard_map/ppermute | solution.py:32
  48.5 55.4 %all-gather.5.cloned.1.call-done = bf16[2304,1664]{1,0:T(8,128)(2,1)} async-done(((bf16[288,1664]{1,0:T(8,128)(2,1)}), bf16[2304,1664]{1,0:T(8,128)(2,1)}) %all-gather.5.cloned.1.call-update) | async-done | bytes 7667728 | tf_op jit(solution)/shard_map/all_gather | solution.py:304
  103.9 3.7 copy.80
  107.7 3.1 copy-done.2
  117.9 25.4 %collective-permute-done.19.refs_1_ = bf16[144,2304]{1,0:T(8,128)(2,1)S(1)} collective-permute-done((bf16[144,2304]{1,0:T(8,128)(2,1)S(1)}, bf16[144,2304]{1,0:T(8,128)(2,1)S(1)}, u32[]{:S(2)}, u32[]{:S(2)}) %collective-permute-start.19) | collective-permute-done | bytes 663584 | tf_op jit(solution)/shard_map/ppermute | solution.py:32
  143.8 11.6 %collective-permute-done.1 = bf16[128,2304]{1,0:T(8,128)(2,1)} collective-permute-done((bf16[128,2304]{1,0:T(8,128)(2,1)}, bf16[128,2304]{1,0:T(8,128)(2,1)}, u32[]{:S(2)}, u32[]{:S(2)}) %collective-permute-start.1) | collective-permute-done | bytes 589856 | tf_op jit(solution)/shard_map/ppermute | solution.py:32
  162.6 5.7 fusion.23
  171.7 32.2 %collective-permute-done.4 = bf16[512,256]{1,0:T(8,128)(2,1)S(1)} collective-permute-done((bf16[512,256]{1,0:T(8,128)(2,1)S(1)}, bf16[512,256]{1,0:T(8,128)(2,1)S(1)}, u32[]{:S(2)}, u32[]{:S(2)}) %collective-permute-start.4) | collective-permute-done | bytes 262176 | tf_op jit(solution)/shard_map/ppermute | solution.py:32
  208.7 18.3 %collective-permute-done.7 = bf16[512,256]{1,0:T(8,128)(2,1)S(1)} collective-permute-done((bf16[512,256]{1,0:T(8,128)(2,1)S(1)}, bf16[512,256]{1,0:T(8,128)(2,1)S(1)}, u32[]{:S(2)}, u32[]{:S(2)}) %collective-permute-start.7) | collective-permute-done | bytes 262176 | tf_op jit(solution)/shard_map/ppermute | solution.py:32
  227.0 4.6 collective-permute-start.8
  236.0 31.9 %collective-permute-done.8 = bf16[1024,256]{1,0:T(8,128)(2,1)S(1)} collective-permute-done((bf16[1024,256]{1,0:T(8,128)(2,1)S(1)}, bf16[1024,256]{1,0:T(8,128)(2,1)S(1)}, u32[]{:S(2)}, u32[]{:S(2)}) %collective-permute-start.8) | collective-permute-done | bytes 524320 | tf_op jit(solution)/shard_map/ppermute | solution.py:32
  272.4 11.6 %attend.1 = (f32[512,512]{1,0:T(8,128)S(1)}, bf16[512,512]{1,0:T(8,128)(2,1)S(1)}, f32[2,512]{1,0:T(2,128)S(1)}) custom-call(s32[32]{0:T(128)S(1)} %stack.280.base_ref, s32[1,512]{1,0:T(1,128)S(1)} %add_maximum_fusion.limit_ref, bf16[512,512]{1,0:T(8,128)(2,1)S(1)} %pad_maximum_fusion.15.q_ref, bf16[4096,256]{1,0:T(8,128)(2,1)S(1)} %pad_maximum_fusion.4.k_ref, ...), custom_call_target="tpu_custom_call" | custom-call | flops 4294967296 | bytes 8388608 | tf_op jit(solution)/shard_map/attend/pallas_call | solution.py:179
  284.1 3.2 convolution_convert_fusion.5
  288.4 2.9 collective-permute-start.12
  293.6 12.2 %collective-permute-done.12 = bf16[128,2304]{1,0:T(8,128)(2,1)} collective-permute-done((bf16[128,2304]{1,0:T(8,128)(2,1)}, bf16[128,2304]{1,0:T(8,128)(2,1)}, u32[]{:S(2)}, u32[]{:S(2)}) %collective-permute-start.12) | collective-permute-done | bytes 589856 | tf_op jit(solution)/shard_map/ppermute | solution.py:32
  305.8 12.0 %collective-permute-done.11 = bf16[128,2304]{1,0:T(8,128)(2,1)} collective-permute-done((bf16[128,2304]{1,0:T(8,128)(2,1)}, bf16[128,2304]{1,0:T(8,128)(2,1)}, u32[]{:S(2)}, u32[]{:S(2)}) %collective-permute-start.11) | collective-permute-done | bytes 589856 | tf_op jit(solution)/shard_map/ppermute | solution.py:32
  318.1 3.2 multiply_reduce_fusion.6
  328.2 12.7 %collective-permute-done.13 = bf16[128,2304]{1,0:T(8,128)(2,1)S(1)} collective-permute-done((bf16[128,2304]{1,0:T(8,128)(2,1)S(1)}, bf16[128,2304]{1,0:T(8,128)(2,1)S(1)}, u32[]{:S(2)}, u32[]{:S(2)}) %collective-permute-start.13) | collective-permute-done | bytes 589856 | tf_op jit(solution)/shard_map/ppermute | solution.py:32
  341.0 12.8 %collective-permute-done.14 = bf16[128,2304]{1,0:T(8,128)(2,1)S(1)} collective-permute-done((bf16[128,2304]{1,0:T(8,128)(2,1)S(1)}, bf16[128,2304]{1,0:T(8,128)(2,1)S(1)}, u32[]{:S(2)}, u32[]{:S(2)}) %collective-permute-start.14) | collective-permute-done | bytes 589856 | tf_op jit(solution)/shard_map/ppermute | solution.py:32
  360.0 11.5 %fusion.197.refs_0_ = f32[1024,1152]{1,0:T(8,128)} fusion(bf16[1024,2304]{1,0:T(8,128)(2,1)} %constant_dynamic-update-slice_fusion.1, bf16[2304,1152]{1,0:T(8,128)(2,1)} %all-gather.7.cloned.1.call-done), kind=kOutput, calls=%fused_computation.396 | convolution fusion | flops 5435817984 | bytes 14745600 | tf_op jit(solution)/shard_map/dot_general | solution.py:123
  371.5 12.5 %fusion.18 = (bf16[1024,1152]{1,0:T(8,128)(2,1)}, f32[1024,1152]{1,0:T(8,128)}) fusion(f32[1024,1152]{1,0:T(8,128)} %fusion.197.refs_0_, bf16[1024,2304]{1,0:T(8,128)(2,1)} %constant_dynamic-update-slice_fusion.1, bf16[2304,1152]{1,0:T(8,128)(2,1)} %all-gather.9.cloned.1.call-done), kind=kOutput, calls=%fused_computation.28 | convolution fusion | flops 5447614464 | bytes 21823488 | tf_op jit(solution)/shard_map/dot_general | solution.py:123
  384.1 45.5 %all-gather.11.cloned.1.call-done = bf16[2304,1152]{1,0:T(8,128)(2,1)} async-done(((bf16[576,1152]{1,0:T(8,128)(2,1)}), bf16[2304,1152]{1,0:T(8,128)(2,1)}) %all-gather.11.cloned.1.call-update) | async-done | bytes 5308432 | tf_op jit(solution)/shard_map/all_gather | solution.py:331
  429.6 6.3 convolution_convert_fusion.3
  435.9 4.5 collective-permute-done.23
  440.5 3.2 fusion.195
  447.4 13.6 %collective-permute-done.26 = bf16[128,2304]{1,0:T(8,128)(2,1)S(1)} collective-permute-done((bf16[128,2304]{1,0:T(8,128)(2,1)S(1)}, bf16[128,2304]{1,0:T(8,128)(2,1)S(1)}, u32[]{:S(2)}, u32[]{:S(2)}) %collective-permute-start.26) | collective-permute-done | bytes 589856 | tf_op jit(solution)/shard_map/ppermute | solution.py:32
  461.0 11.8 %collective-permute-done.25 = bf16[128,2304]{1,0:T(8,128)(2,1)S(1)} collective-permute-done((bf16[128,2304]{1,0:T(8,128)(2,1)S(1)}, bf16[128,2304]{1,0:T(8,128)(2,1)S(1)}, u32[]{:S(2)}, u32[]{:S(2)}) %collective-permute-start.25) | collective-permute-done | bytes 589856 | tf_op jit(solution)/shard_map/ppermute | solution.py:32
  478.9 12.7 %collective-permute-done.27 = bf16[128,2304]{1,0:T(8,128)(2,1)S(1)} collective-permute-done((bf16[128,2304]{1,0:T(8,128)(2,1)S(1)}, bf16[128,2304]{1,0:T(8,128)(2,1)S(1)}, u32[]{:S(2)}, u32[]{:S(2)}) %collective-permute-start.27) | collective-permute-done | bytes 589856 | tf_op jit(solution)/shard_map/ppermute | solution.py:32
  491.6 12.8 %collective-permute-done.28 = bf16[128,2304]{1,0:T(8,128)(2,1)S(1)} collective-permute-done((bf16[128,2304]{1,0:T(8,128)(2,1)S(1)}, bf16[128,2304]{1,0:T(8,128)(2,1)S(1)}, u32[]{:S(2)}, u32[]{:S(2)}) %collective-permute-start.28) | collective-permute-done | bytes 589856 | tf_op jit(solution)/shard_map/ppermute | solution.py:32
  504.8 4.4 collective-permute-done.30
  511.4 8.1 convolution_convert_fusion.2.refs_1_
  522.1 3.3 copy-done.12
  529.5 13.2 %multiply_convert_fusion = (bf16[1024,1152]{1,0:T(8,128)(2,1)S(1)}, bf16[1024,1152]{1,0:T(8,128)(2,1)S(1)}) fusion(f32[1024,1152]{1,0:T(8,128)} %copy-done.13, f32[1024,1152]{1,0:T(8,128)} %get-tuple-element.121, bf16[1024,2304]{1,0:T(8,128)(2,1)S(1)} %copy-done.49, bf16[2304,1152]{1,0:T(8,128)(2,1)} %all-gather.11.cloned.1.call-done), kind=kOutput, calls=%fused_computation.32 | convolution fusion | flops 5464129536 | bytes 24182784 | tf_op jit(solution)/shard_map/dot_general | solution.py:123
  542.7 3.2 fusion.59
  546.0 3.5 fusion.19
  549.8 4.5 fusion.64
  554.3 9.8 %convolution_convert_fusion.1.refs_1_.refs_0_ = bf16[2304,1152]{1,0:T(8,128)(2,1)} fusion(bf16[1024,2304]{1,0:T(8,128)(2,1)} %constant_dynamic-update-slice_fusion.1, bf16[1024,1152]{1,0:T(8,128)(2,1)S(1)} %get-tuple-element.48), kind=kOutput, calls=%fused_computation.1 | convolution fusion | flops 5438472192 | bytes 12386304 | tf_op jit(solution)/shard_map/dot_general | solution.py:127
  564.1 5.2 fusion.196
  574.1 9.7 %convolution_convert_fusion = bf16[2304,1152]{1,0:T(8,128)(2,1)} fusion(bf16[1024,2304]{1,0:T(8,128)(2,1)} %constant_dynamic-update-slice_fusion.1, bf16[1024,1152]{1,0:T(8,128)(2,1)S(1)} %copy-done.70), kind=kOutput, calls=%fused_computation | convolution fusion | flops 5438472192 | bytes 12386304 | tf_op jit(solution)/shard_map/dot_general | solution.py:127
  583.8 4.0 collective-permute-done.34
  587.9 11.6 %collective-permute-done.33 = bf16[128,2304]{1,0:T(8,128)(2,1)} collective-permute-done((bf16[128,2304]{1,0:T(8,128)(2,1)}, bf16[128,2304]{1,0:T(8,128)(2,1)}, u32[]{:S(2)}, u32[]{:S(2)}) %collective-permute-start.33) | collective-permute-done | bytes 589856 | tf_op jit(solution)/shard_map/ppermute | solution.py:32
  599.5 2.9 multiply_reduce_fusion
  609.8 13.7 %collective-permute-done.37 = bf16[128,2304]{1,0:T(8,128)(2,1)S(1)} collective-permute-done((bf16[128,2304]{1,0:T(8,128)(2,1)S(1)}, bf16[128,2304]{1,0:T(8,128)(2,1)S(1)}, u32[]{:S(2)}, u32[]{:S(2)}) %collective-permute-start.37) | collective-permute-done | bytes 589856 | tf_op jit(solution)/shard_map/ppermute | solution.py:32
  623.5 11.1 %collective-permute-done.36 = bf16[128,2304]{1,0:T(8,128)(2,1)S(1)} collective-permute-done((bf16[128,2304]{1,0:T(8,128)(2,1)S(1)}, bf16[128,2304]{1,0:T(8,128)(2,1)S(1)}, u32[]{:S(2)}, u32[]{:S(2)}) %collective-permute-start.36) | collective-permute-done | bytes 589856 | tf_op jit(solution)/shard_map/ppermute | solution.py:32
  638.6 3.6 fusion.42.refs_0_
  647.7 2.9 reshape.358
  654.2 21.3 %attend_back.1 = (f32[512,512]{1,0:T(8,128)S(1)}, f32[2048,512]{1,0:T(8,128)}, bf16[2048,512]{1,0:T(8,128)(2,1)}) custom-call(s32[32]{0:T(128)S(1)} %copy-done.23, s32[1,512]{1,0:T(1,128)S(1)} %copy-done.21, f32[2,512]{1,0:T(2,128)S(1)} %get-tuple-element.20.lse_ref, f32[2,512]{1,0:T(2,128)S(1)} %bitcast.350, bf16[512,512]{1,0:T(8,128)(2,1)S(1)} %copy-done.17, ...), custom_call_target="tpu_custom_call" | custom-call | tf_op jit(solution)/shard_map/attend_back/pallas_call | solution.py:265
  677.0 43.4 %collective-permute-done.49 = bf16[2,288,512]{2,1,0:T(8,128)(2,1)S(1)} collective-permute-done((bf16[2,288,512]{2,1,0:T(8,128)(2,1)S(1)}, bf16[2,288,512]{2,1,0:T(8,128)(2,1)S(1)}, u32[]{:S(2)}, u32[]{:S(2)}) %collective-permute-start.49) | collective-permute-done | bytes 589856 | tf_op jit(solution)/shard_map/ppermute | solution.py:32
  720.7 3.6 convert_add_fusion.2
  727.4 5.0 collective-permute-done.50
  736.0 3.3 collective-permute-done.51
  742.4 10.0 %collective-permute-done.40 = bf16[1024,512]{1,0:T(8,128)(2,1)} collective-permute-done((bf16[1024,512]{1,0:T(8,128)(2,1)}, bf16[1024,512]{1,0:T(8,128)(2,1)}, u32[]{:S(2)}, u32[]{:S(2)}) %collective-permute-start.40) | collective-permute-done | bytes 1048608 | tf_op jit(solution)/shard_map/ppermute | solution.py:32
  754.7 2.9 collective-permute-start.41
  761.1 18.5 %collective-permute-done.41.refs_1_ = bf16[512,512]{1,0:T(8,128)(2,1)S(1)} collective-permute-done((bf16[512,512]{1,0:T(8,128)(2,1)S(1)}, bf16[512,512]{1,0:T(8,128)(2,1)S(1)}, u32[]{:S(2)}, u32[]{:S(2)}) %collective-permute-start.41) | collective-permute-done | bytes 524320 | tf_op jit(solution)/shard_map/ppermute | solution.py:32
  785.2 3.3 collective-permute-start.45
  796.3 5.7 fusion.79
  805.2 10.2 %collective-permute-done.52 = bf16[2,144,1152]{2,1,0:T(8,128)(2,1)S(1)} collective-permute-done((bf16[2,144,1152]{2,1,0:T(8,128)(2,1)S(1)}, bf16[2,144,1152]{2,1,0:T(8,128)(2,1)S(1)}, u32[]{:S(2)}, u32[]{:S(2)}) %collective-permute-start.52) | collective-permute-done | bytes 663584 | tf_op jit(solution)/shard_map/ppermute | solution.py:32
  817.4 24.8 %collective-permute-done.56 = bf16[2,144,1152]{2,1,0:T(8,128)(2,1)S(1)} collective-permute-done((bf16[2,144,1152]{2,1,0:T(8,128)(2,1)S(1)}, bf16[2,144,1152]{2,1,0:T(8,128)(2,1)S(1)}, u32[]{:S(2)}, u32[]{:S(2)}) %collective-permute-start.56) | collective-permute-done | bytes 663584 | tf_op jit(solution)/shard_map/ppermute | solution.py:32
  854.6 8.8 collective-permute-done.58
  876.5 33.7 %collective-permute-done.46 = bf16[2,288,1024]{2,1,0:T(8,128)(2,1)} collective-permute-done((bf16[2,288,1024]{2,1,0:T(8,128)(2,1)S(1)}, bf16[2,288,1024]{2,1,0:T(8,128)(2,1)}, u32[]{:S(2)}, u32[]{:S(2)}) %collective-permute-start.46) | collective-permute-done | bytes 1179680 | tf_op jit(solution)/shard_map/ppermute | solution.py:32
  923.2 19.3 %collective-permute-done.47 = bf16[288,1024]{1,0:T(8,128)(2,1)} collective-permute-done((bf16[288,1024]{1,0:T(8,128)(2,1)}, bf16[288,1024]{1,0:T(8,128)(2,1)}, u32[]{:S(2)}, u32[]{:S(2)}) %collective-permute-start.47) | collective-permute-done | bytes 589856 | tf_op jit(solution)/shard_map/ppermute | solution.py:32
  945.7 7.1 collective-permute-done.48
  (469 shorter events, 186.3 us)
Async XLA Ops:
  7.2 96.7 %all-gather.5.cloned.1.call-start = ((), (), s32[]{:S(2)}) async-start(), calls=%async_computation.3 | async-start | bytes 8626176 | tf_op jit(solution)/shard_map/all_gather | solution.py:304
  11.0 14.0 %collective-permute-start.3 = (bf16[144,1664]{1,0:T(8,128)(2,1)S(1)}, bf16[144,1664]{1,0:T(8,128)(2,1)S(1)}, u32[]{:S(2)}, u32[]{:S(2)}) collective-permute-start(bf16[144,1664]{1,0:T(8,128)(2,1)S(1)} %dynamic-slice_bitcast_fusion.3), channel_id=1, source_target_pairs={{0,4},{1,5},{2,6},{3,7},{4,0},{5,1},{6,2},{7,3},{8,12},{9,13},{10,... | collective-permute-start | bytes 1437704 | tf_op jit(solution)/shard_map/ppermute | solution.py:32
  26.2 333.8 %all-gather.7.cloned.1.call-start = ((), (), s32[]{:S(2)}) async-start(), calls=%async_computation.4 | async-start | bytes 6635520 | tf_op jit(solution)/shard_map/all_gather | solution.py:331
  28.2 16.2 %collective-permute-start.17 = (bf16[144,2304]{1,0:T(8,128)(2,1)S(1)}, bf16[144,2304]{1,0:T(8,128)(2,1)S(1)}, u32[]{:S(2)}, u32[]{:S(2)}) collective-permute-start(bf16[144,2304]{1,0:T(8,128)(2,1)S(1)} %after.13), channel_id=1, source_target_pairs={{0,4},{1,5},{2,6},{3,7},{4,0},{5,1},{6,2},{7,3},{8,12},{9,13},{10,... | collective-permute-start | bytes 1990664 | tf_op jit(solution)/shard_map/ppermute | solution.py:32
  110.8 260.7 %all-gather.9.cloned.1.call-start = ((), (), s32[]{:S(2)}) async-start(), calls=%async_computation.5 | async-start | bytes 6635520 | tf_op jit(solution)/shard_map/all_gather | solution.py:331
  112.9 30.4 %collective-permute-start.19 = (bf16[144,2304]{1,0:T(8,128)(2,1)S(1)}, bf16[144,2304]{1,0:T(8,128)(2,1)S(1)}, u32[]{:S(2)}, u32[]{:S(2)}) collective-permute-start(bf16[144,2304]{1,0:T(8,128)(2,1)S(1)} %after.15), channel_id=1, source_target_pairs={{0,4},{1,5},{2,6},{3,7},{4,0},{5,1},{6,2},{7,3},{8,12},{9,13},{10,... | collective-permute-start | bytes 1990664 | tf_op jit(solution)/shard_map/ppermute | solution.py:32
  114.4 29.3 %collective-permute-start.2 = (bf16[128,2304]{1,0:T(8,128)(2,1)}, bf16[128,2304]{1,0:T(8,128)(2,1)}, u32[]{:S(2)}, u32[]{:S(2)}) collective-permute-start(bf16[128,2304]{1,0:T(8,128)(2,1)} %param.14), channel_id=1, source_target_pairs={{0,5},{1,4},{2,7},{3,6},{4,1},{5,0},{6,3},{7,2},{8,13},{9,12},{10,... | collective-permute-start | bytes 1769480 | tf_op jit(solution)/shard_map/ppermute | solution.py:32
  115.9 39.5 %collective-permute-start.1 = (bf16[128,2304]{1,0:T(8,128)(2,1)}, bf16[128,2304]{1,0:T(8,128)(2,1)}, u32[]{:S(2)}, u32[]{:S(2)}) collective-permute-start(bf16[128,2304]{1,0:T(8,128)(2,1)} %param.14), channel_id=1, source_target_pairs={{0,4},{1,5},{2,6},{3,7},{4,0},{5,1},{6,2},{7,3},{8,12},{9,13},{10,... | collective-permute-start | bytes 1769480 | tf_op jit(solution)/shard_map/ppermute | solution.py:32
  117.4 38.0 %collective-permute-start = (bf16[128,2304]{1,0:T(8,128)(2,1)}, bf16[128,2304]{1,0:T(8,128)(2,1)}, u32[]{:S(2)}, u32[]{:S(2)}) collective-permute-start(bf16[128,2304]{1,0:T(8,128)(2,1)} %param.14), channel_id=1, source_target_pairs={{0,1},{1,0},{2,3},{3,2},{4,5},{5,4},{6,7},{7,6},{8,9},{9,8},{10,11... | collective-permute-start | bytes 1769480 | tf_op jit(solution)/shard_map/ppermute | solution.py:32
  143.7 13.6 %collective-permute-start.20 = (bf16[2,144,1152]{2,1,0:T(8,128)(2,1)S(1)}, bf16[2,144,1152]{2,1,0:T(8,128)(2,1)S(1)}, u32[]{:S(2)}, u32[]{:S(2)}) collective-permute-start(bf16[2,144,1152]{2,1,0:T(8,128)(2,1)S(1)} %broadcast_select_fusion.14), channel_id=1, source_target_pairs={{0,2},{1,3},{2,0},{3,1},{4,6},{5,7},{6,4},{7,5},{8,10},{9,11},{10,... | collective-permute-start | bytes 1990664 | tf_op jit(solution)/shard_map/ppermute | solution.py:32
  159.0 270.6 %all-gather.11.cloned.1.call-start = ((), (), s32[]{:S(2)}) async-start(), calls=%async_computation.6 | async-start | bytes 6635520 | tf_op jit(solution)/shard_map/all_gather | solution.py:331
  170.4 33.4 %collective-permute-start.4 = (bf16[512,256]{1,0:T(8,128)(2,1)S(1)}, bf16[512,256]{1,0:T(8,128)(2,1)S(1)}, u32[]{:S(2)}, u32[]{:S(2)}) collective-permute-start(bf16[512,256]{1,0:T(8,128)(2,1)S(1)} %pad_maximum_fusion.20), channel_id=1, source_target_pairs={{0,16},{1,17},{2,18},{3,19},{4,20},{5,21},{6,22},{7,23},{8,24},{9,... | collective-permute-start | bytes 786440 | tf_op jit(solution)/shard_map/ppermute | solution.py:32
  204.7 28.7 %collective-permute-start.5 = (bf16[1024,256]{1,0:T(8,128)(2,1)}, bf16[1024,256]{1,0:T(8,128)(2,1)}, u32[]{:S(2)}, u32[]{:S(2)}) collective-permute-start(bf16[1024,256]{1,0:T(8,128)(2,1)} %pad_maximum_fusion.16), channel_id=1, source_target_pairs={{0,8},{1,9},{2,10},{3,11},{4,12},{5,13},{6,14},{7,15},{8,0},{9,1},... | collective-permute-start | bytes 1572872 | tf_op jit(solution)/shard_map/ppermute | solution.py:32
  204.8 29.9 %collective-permute-start.21 = (bf16[144,2304]{1,0:T(8,128)(2,1)S(1)}, bf16[144,2304]{1,0:T(8,128)(2,1)}, u32[]{:S(2)}, u32[]{:S(2)}) collective-permute-start(bf16[144,2304]{1,0:T(8,128)(2,1)S(1)} %after.16), channel_id=1, source_target_pairs={{0,4},{1,5},{2,6},{3,7},{4,0},{5,1},{6,2},{7,3},{8,12},{9,13},{10,... | collective-permute-start | bytes 1990664 | tf_op jit(solution)/shard_map/ppermute | solution.py:32
  206.4 20.6 %collective-permute-start.7 = (bf16[512,256]{1,0:T(8,128)(2,1)S(1)}, bf16[512,256]{1,0:T(8,128)(2,1)S(1)}, u32[]{:S(2)}, u32[]{:S(2)}) collective-permute-start(bf16[512,256]{1,0:T(8,128)(2,1)S(1)} %slice.668), channel_id=1, source_target_pairs={{0,16},{1,17},{2,18},{3,19},{4,20},{5,21},{6,22},{7,23},{8,24},{9,... | collective-permute-start | bytes 786440 | tf_op jit(solution)/shard_map/ppermute | solution.py:32
  227.0 40.9 %collective-permute-start.8 = (bf16[1024,256]{1,0:T(8,128)(2,1)S(1)}, bf16[1024,256]{1,0:T(8,128)(2,1)S(1)}, u32[]{:S(2)}, u32[]{:S(2)}) collective-permute-start(bf16[1024,256]{1,0:T(8,128)(2,1)S(1)} %pad_maximum_fusion.17), channel_id=1, source_target_pairs={{0,8},{1,9},{2,10},{3,11},{4,12},{5,13},{6,14},{7,15},{8,0},{9,1},... | collective-permute-start | bytes 1572872 | tf_op jit(solution)/shard_map/ppermute | solution.py:32
  234.6 34.4 %collective-permute-start.6 = (bf16[2048,256]{1,0:T(8,128)(2,1)S(1)}, bf16[2048,256]{1,0:T(8,128)(2,1)S(1)}, u32[]{:S(2)}, u32[]{:S(2)}) collective-permute-start(bf16[2048,256]{1,0:T(8,128)(2,1)S(1)} %pad_maximum_fusion.9), channel_id=1, source_target_pairs={{0,2},{1,3},{2,0},{3,1},{4,6},{5,7},{6,4},{7,5},{8,10},{9,11},{10,... | collective-permute-start | bytes 3145736 | tf_op jit(solution)/shard_map/ppermute | solution.py:32
  268.3 23.6 %collective-permute-start.22 = (bf16[2,144,1152]{2,1,0:T(8,128)(2,1)S(1)}, bf16[2,144,1152]{2,1,0:T(8,128)(2,1)S(1)}, u32[]{:S(2)}, u32[]{:S(2)}) collective-permute-start(bf16[2,144,1152]{2,1,0:T(8,128)(2,1)S(1)} %broadcast_select_fusion.12), channel_id=1, source_target_pairs={{0,2},{1,3},{2,0},{3,1},{4,6},{5,7},{6,4},{7,5},{8,10},{9,11},{10,... | collective-permute-start | bytes 1990664 | tf_op jit(solution)/shard_map/ppermute | solution.py:32
  288.4 17.4 %collective-permute-start.12 = (bf16[128,2304]{1,0:T(8,128)(2,1)}, bf16[128,2304]{1,0:T(8,128)(2,1)}, u32[]{:S(2)}, u32[]{:S(2)}) collective-permute-start(bf16[128,2304]{1,0:T(8,128)(2,1)} %get-tuple-element.90), channel_id=1, source_target_pairs={{0,5},{1,4},{2,7},{3,6},{4,1},{5,0},{6,3},{7,2},{8,13},{9,12},{10,... | collective-permute-start | bytes 1769480 | tf_op jit(solution)/shard_map/ppermute | solution.py:32
  291.3 26.5 %collective-permute-start.11 = (bf16[128,2304]{1,0:T(8,128)(2,1)}, bf16[128,2304]{1,0:T(8,128)(2,1)}, u32[]{:S(2)}, u32[]{:S(2)}) collective-permute-start(bf16[128,2304]{1,0:T(8,128)(2,1)} %get-tuple-element.91), channel_id=1, source_target_pairs={{0,4},{1,5},{2,6},{3,7},{4,0},{5,1},{6,2},{7,3},{8,12},{9,13},{10,... | collective-permute-start | bytes 1769480 | tf_op jit(solution)/shard_map/ppermute | solution.py:32
  291.8 26.2 %collective-permute-start.10 = (bf16[128,2304]{1,0:T(8,128)(2,1)S(1)}, bf16[128,2304]{1,0:T(8,128)(2,1)}, u32[]{:S(2)}, u32[]{:S(2)}) collective-permute-start(bf16[128,2304]{1,0:T(8,128)(2,1)S(1)} %get-tuple-element.89), channel_id=1, source_target_pairs={{0,1},{1,0},{2,3},{3,2},{4,5},{5,4},{6,7},{7,6},{8,9},{9,8},{10,11... | collective-permute-start | bytes 1769480 | tf_op jit(solution)/shard_map/ppermute | solution.py:32
  293.6 350.4 %reduce-scatter.4.cloned.1.call-start = ((), (), s32[]{:S(2)}) async-start(), calls=%async_computation.7 | async-start | bytes 6635520 | tf_op jit(solution)/shard_map/reduce_scatter | solution.py:335
  324.7 16.2 %collective-permute-start.13 = (bf16[128,2304]{1,0:T(8,128)(2,1)S(1)}, bf16[128,2304]{1,0:T(8,128)(2,1)S(1)}, u32[]{:S(2)}, u32[]{:S(2)}) collective-permute-start(bf16[128,2304]{1,0:T(8,128)(2,1)S(1)} %get-tuple-element.45), channel_id=1, source_target_pairs={{0,1},{1,0},{2,3},{3,2},{4,5},{5,4},{6,7},{7,6},{8,9},{9,8},{10,11... | collective-permute-start | bytes 1769480 | tf_op jit(solution)/shard_map/ppermute | solution.py:32
  326.2 27.5 %collective-permute-start.14 = (bf16[128,2304]{1,0:T(8,128)(2,1)S(1)}, bf16[128,2304]{1,0:T(8,128)(2,1)S(1)}, u32[]{:S(2)}, u32[]{:S(2)}) collective-permute-start(bf16[128,2304]{1,0:T(8,128)(2,1)S(1)} %get-tuple-element.45), channel_id=1, source_target_pairs={{0,4},{1,5},{2,6},{3,7},{4,0},{5,1},{6,2},{7,3},{8,12},{9,13},{10,... | collective-permute-start | bytes 1769480 | tf_op jit(solution)/shard_map/ppermute | solution.py:32
  326.7 27.0 %collective-permute-start.15 = (bf16[128,2304]{1,0:T(8,128)(2,1)S(1)}, bf16[128,2304]{1,0:T(8,128)(2,1)S(1)}, u32[]{:S(2)}, u32[]{:S(2)}) collective-permute-start(bf16[128,2304]{1,0:T(8,128)(2,1)S(1)} %get-tuple-element.45), channel_id=1, source_target_pairs={{0,5},{1,4},{2,7},{3,6},{4,1},{5,0},{6,3},{7,2},{8,13},{9,12},{10,... | collective-permute-start | bytes 1769480 | tf_op jit(solution)/shard_map/ppermute | solution.py:32
  353.9 4.6 collective-permute-start.16
  435.9 4.6 collective-permute-start.23
  443.9 17.2 %collective-permute-start.26 = (bf16[128,2304]{1,0:T(8,128)(2,1)S(1)}, bf16[128,2304]{1,0:T(8,128)(2,1)S(1)}, u32[]{:S(2)}, u32[]{:S(2)}) collective-permute-start(bf16[128,2304]{1,0:T(8,128)(2,1)S(1)} %get-tuple-element.54), channel_id=1, source_target_pairs={{0,5},{1,4},{2,7},{3,6},{4,1},{5,0},{6,3},{7,2},{8,13},{9,12},{10,... | collective-permute-start | bytes 1769480 | tf_op jit(solution)/shard_map/ppermute | solution.py:32
  446.3 26.5 %collective-permute-start.25 = (bf16[128,2304]{1,0:T(8,128)(2,1)S(1)}, bf16[128,2304]{1,0:T(8,128)(2,1)S(1)}, u32[]{:S(2)}, u32[]{:S(2)}) collective-permute-start(bf16[128,2304]{1,0:T(8,128)(2,1)S(1)} %get-tuple-element.55), channel_id=1, source_target_pairs={{0,4},{1,5},{2,6},{3,7},{4,0},{5,1},{6,2},{7,3},{8,12},{9,13},{10,... | collective-permute-start | bytes 1769480 | tf_op jit(solution)/shard_map/ppermute | solution.py:32
  446.9 26.0 %collective-permute-start.24 = (bf16[128,2304]{1,0:T(8,128)(2,1)S(1)}, bf16[128,2304]{1,0:T(8,128)(2,1)S(1)}, u32[]{:S(2)}, u32[]{:S(2)}) collective-permute-start(bf16[128,2304]{1,0:T(8,128)(2,1)S(1)} %get-tuple-element.53), channel_id=1, source_target_pairs={{0,1},{1,0},{2,3},{3,2},{4,5},{5,4},{6,7},{7,6},{8,9},{9,8},{10,11... | collective-permute-start | bytes 1769480 | tf_op jit(solution)/shard_map/ppermute | solution.py:32
  475.3 16.3 %collective-permute-start.27 = (bf16[128,2304]{1,0:T(8,128)(2,1)S(1)}, bf16[128,2304]{1,0:T(8,128)(2,1)S(1)}, u32[]{:S(2)}, u32[]{:S(2)}) collective-permute-start(bf16[128,2304]{1,0:T(8,128)(2,1)S(1)} %get-tuple-element.41), channel_id=1, source_target_pairs={{0,1},{1,0},{2,3},{3,2},{4,5},{5,4},{6,7},{7,6},{8,9},{9,8},{10,11... | collective-permute-start | bytes 1769480 | tf_op jit(solution)/shard_map/ppermute | solution.py:32
  476.9 27.6 %collective-permute-start.28 = (bf16[128,2304]{1,0:T(8,128)(2,1)S(1)}, bf16[128,2304]{1,0:T(8,128)(2,1)S(1)}, u32[]{:S(2)}, u32[]{:S(2)}) collective-permute-start(bf16[128,2304]{1,0:T(8,128)(2,1)S(1)} %get-tuple-element.41), channel_id=1, source_target_pairs={{0,4},{1,5},{2,6},{3,7},{4,0},{5,1},{6,2},{7,3},{8,12},{9,13},{10,... | collective-permute-start | bytes 1769480 | tf_op jit(solution)/shard_map/ppermute | solution.py:32
  477.6 26.8 %collective-permute-start.29 = (bf16[128,2304]{1,0:T(8,128)(2,1)S(1)}, bf16[128,2304]{1,0:T(8,128)(2,1)S(1)}, u32[]{:S(2)}, u32[]{:S(2)}) collective-permute-start(bf16[128,2304]{1,0:T(8,128)(2,1)S(1)} %get-tuple-element.41), channel_id=1, source_target_pairs={{0,5},{1,4},{2,7},{3,6},{4,1},{5,0},{6,3},{7,2},{8,13},{9,12},{10,... | collective-permute-start | bytes 1769480 | tf_op jit(solution)/shard_map/ppermute | solution.py:32
  504.6 4.6 collective-permute-start.30
  519.6 271.5 %reduce-scatter.6.cloned.1.call-start = ((), (), s32[]{:S(2)}) async-start(), calls=%async_computation.8 | async-start | bytes 6635520 | tf_op jit(solution)/shard_map/reduce_scatter | solution.py:335
  549.5 14.5 %collective-permute-start.31 = (bf16[512,2304]{1,0:T(8,128)(2,1)S(1)}, bf16[512,2304]{1,0:T(8,128)(2,1)S(1)}, u32[]{:S(2)}, u32[]{:S(2)}) collective-permute-start(bf16[512,2304]{1,0:T(8,128)(2,1)S(1)} %fusion.19), channel_id=1, source_target_pairs={{0,2},{1,3},{2,0},{3,1},{4,6},{5,7},{6,4},{7,5},{8,10},{9,11},{10,... | collective-permute-start | bytes 7077896 | tf_op jit(solution)/shard_map/ppermute | solution.py:32
  570.6 17.3 %collective-permute-start.34 = (bf16[128,2304]{1,0:T(8,128)(2,1)}, bf16[128,2304]{1,0:T(8,128)(2,1)S(1)}, u32[]{:S(2)}, u32[]{:S(2)}) collective-permute-start(bf16[128,2304]{1,0:T(8,128)(2,1)} %get-tuple-element.51), channel_id=1, source_target_pairs={{0,5},{1,4},{2,7},{3,6},{4,1},{5,0},{6,3},{7,2},{8,13},{9,12},{10,... | collective-permute-start | bytes 1769480 | tf_op jit(solution)/shard_map/ppermute | solution.py:32
  571.2 28.3 %collective-permute-start.33 = (bf16[128,2304]{1,0:T(8,128)(2,1)}, bf16[128,2304]{1,0:T(8,128)(2,1)}, u32[]{:S(2)}, u32[]{:S(2)}) collective-permute-start(bf16[128,2304]{1,0:T(8,128)(2,1)} %get-tuple-element.52), channel_id=1, source_target_pairs={{0,4},{1,5},{2,6},{3,7},{4,0},{5,1},{6,2},{7,3},{8,12},{9,13},{10,... | collective-permute-start | bytes 1769480 | tf_op jit(solution)/shard_map/ppermute | solution.py:32
  571.8 27.7 %collective-permute-start.32 = (bf16[128,2304]{1,0:T(8,128)(2,1)}, bf16[128,2304]{1,0:T(8,128)(2,1)}, u32[]{:S(2)}, u32[]{:S(2)}) collective-permute-start(bf16[128,2304]{1,0:T(8,128)(2,1)} %get-tuple-element.50), channel_id=1, source_target_pairs={{0,1},{1,0},{2,3},{3,2},{4,5},{5,4},{6,7},{7,6},{8,9},{9,8},{10,11... | collective-permute-start | bytes 1769480 | tf_op jit(solution)/shard_map/ppermute | solution.py:32
  583.8 332.6 %reduce-scatter.8.cloned.1.call-start = ((), (), s32[]{:S(2)}) async-start(), calls=%async_computation.9 | async-start | bytes 6635520 | tf_op jit(solution)/shard_map/reduce_scatter | solution.py:335
  606.3 17.2 %collective-permute-start.37 = (bf16[128,2304]{1,0:T(8,128)(2,1)S(1)}, bf16[128,2304]{1,0:T(8,128)(2,1)S(1)}, u32[]{:S(2)}, u32[]{:S(2)}) collective-permute-start(bf16[128,2304]{1,0:T(8,128)(2,1)S(1)} %after.18), channel_id=1, source_target_pairs={{0,5},{1,4},{2,7},{3,6},{4,1},{5,0},{6,3},{7,2},{8,13},{9,12},{10,... | collective-permute-start | bytes 1769480 | tf_op jit(solution)/shard_map/ppermute | solution.py:32
  607.4 27.1 %collective-permute-start.36 = (bf16[128,2304]{1,0:T(8,128)(2,1)S(1)}, bf16[128,2304]{1,0:T(8,128)(2,1)S(1)}, u32[]{:S(2)}, u32[]{:S(2)}) collective-permute-start(bf16[128,2304]{1,0:T(8,128)(2,1)S(1)} %after.18), channel_id=1, source_target_pairs={{0,4},{1,5},{2,6},{3,7},{4,0},{5,1},{6,2},{7,3},{8,12},{9,13},{10,... | collective-permute-start | bytes 1769480 | tf_op jit(solution)/shard_map/ppermute | solution.py:32
  608.0 26.5 %collective-permute-start.35 = (bf16[128,2304]{1,0:T(8,128)(2,1)S(1)}, bf16[128,2304]{1,0:T(8,128)(2,1)S(1)}, u32[]{:S(2)}, u32[]{:S(2)}) collective-permute-start(bf16[128,2304]{1,0:T(8,128)(2,1)S(1)} %after.18), channel_id=1, source_target_pairs={{0,1},{1,0},{2,3},{3,2},{4,5},{5,4},{6,7},{7,6},{8,9},{9,8},{10,11... | collective-permute-start | bytes 1769480 | tf_op jit(solution)/shard_map/ppermute | solution.py:32
  638.5 3.8 collective-permute-start.38
  676.5 44.3 %collective-permute-start.39 = (bf16[2048,512]{1,0:T(8,128)(2,1)}, bf16[2048,512]{1,0:T(8,128)(2,1)}, u32[]{:S(2)}, u32[]{:S(2)}) collective-permute-start(bf16[2048,512]{1,0:T(8,128)(2,1)} %get-tuple-element.24), channel_id=1, source_target_pairs={{0,2},{1,3},{2,0},{3,1},{4,6},{5,7},{6,4},{7,5},{8,10},{9,11},{10,... | collective-permute-start | bytes 6291464 | tf_op jit(solution)/shard_map/ppermute | solution.py:32
  676.9 43.5 %collective-permute-start.49 = (bf16[2,288,512]{2,1,0:T(8,128)(2,1)S(1)}, bf16[2,288,512]{2,1,0:T(8,128)(2,1)S(1)}, u32[]{:S(2)}, u32[]{:S(2)}) collective-permute-start(bf16[2,288,512]{2,1,0:T(8,128)(2,1)S(1)} %fusion.104), channel_id=1, source_target_pairs={{0,8},{1,9},{2,10},{3,11},{4,12},{5,13},{6,14},{7,15},{8,0},{9,1},... | collective-permute-start | bytes 1769480 | tf_op jit(solution)/shard_map/ppermute | solution.py:32
  720.7 11.7 %collective-permute-start.50 = (bf16[288,512]{1,0:T(8,128)(2,1)S(1)}, bf16[288,512]{1,0:T(8,128)(2,1)S(1)}, u32[]{:S(2)}, u32[]{:S(2)}) collective-permute-start(bf16[288,512]{1,0:T(8,128)(2,1)S(1)} %fusion.135), channel_id=1, source_target_pairs={{0,16},{1,17},{2,18},{3,19},{4,20},{5,21},{6,22},{7,23},{8,24},{9,... | collective-permute-start | bytes 884744 | tf_op jit(solution)/shard_map/ppermute | solution.py:32
  727.4 25.0 %collective-permute-start.40 = (bf16[1024,512]{1,0:T(8,128)(2,1)}, bf16[1024,512]{1,0:T(8,128)(2,1)}, u32[]{:S(2)}, u32[]{:S(2)}) collective-permute-start(bf16[1024,512]{1,0:T(8,128)(2,1)} %slice.666), channel_id=1, source_target_pairs={{0,8},{1,9},{2,10},{3,11},{4,12},{5,13},{6,14},{7,15},{8,0},{9,1},... | collective-permute-start | bytes 3145736 | tf_op jit(solution)/shard_map/ppermute | solution.py:32
  733.9 5.5 collective-permute-start.51
  754.7 24.9 %collective-permute-start.41 = (bf16[512,512]{1,0:T(8,128)(2,1)S(1)}, bf16[512,512]{1,0:T(8,128)(2,1)S(1)}, u32[]{:S(2)}, u32[]{:S(2)}) collective-permute-start(bf16[512,512]{1,0:T(8,128)(2,1)S(1)} %slice.667), channel_id=1, source_target_pairs={{0,16},{1,17},{2,18},{3,19},{4,20},{5,21},{6,22},{7,23},{8,24},{9,... | collective-permute-start | bytes 1572872 | tf_op jit(solution)/shard_map/ppermute | solution.py:32
  785.2 64.4 %collective-permute-start.45 = (bf16[128,2304]{1,0:T(8,128)(2,1)}, bf16[128,2304]{1,0:T(8,128)(2,1)S(1)}, u32[]{:S(2)}, u32[]{:S(2)}) collective-permute-start(bf16[128,2304]{1,0:T(8,128)(2,1)} %get-tuple-element.87), channel_id=1, source_target_pairs={{0,5},{1,4},{2,7},{3,6},{4,1},{5,0},{6,3},{7,2},{8,13},{9,12},{10,... | collective-permute-start | bytes 1769480 | tf_op jit(solution)/shard_map/ppermute | solution.py:32
  795.7 19.7 %collective-permute-start.52 = (bf16[2,144,1152]{2,1,0:T(8,128)(2,1)S(1)}, bf16[2,144,1152]{2,1,0:T(8,128)(2,1)S(1)}, u32[]{:S(2)}, u32[]{:S(2)}) collective-permute-start(bf16[2,144,1152]{2,1,0:T(8,128)(2,1)S(1)} %dynamic-slice_bitcast_fusion.2), channel_id=1, source_target_pairs={{0,4},{1,5},{2,6},{3,7},{4,0},{5,1},{6,2},{7,3},{8,12},{9,13},{10,... | collective-permute-start | bytes 1990664 | tf_op jit(solution)/shard_map/ppermute | solution.py:32
  802.5 45.9 %collective-permute-start.43 = (bf16[8,144,1024]{2,1,0:T(8,128)(2,1)S(1)}, bf16[8,144,1024]{2,1,0:T(8,128)(2,1)S(1)}, u32[]{:S(2)}, u32[]{:S(2)}) collective-permute-start(bf16[8,144,1024]{2,1,0:T(8,128)(2,1)S(1)} %fusion.25), channel_id=1, source_target_pairs={{0,2},{1,3},{2,0},{3,1},{4,6},{5,7},{6,4},{7,5},{8,10},{9,11},{10,... | collective-permute-start | bytes 7077896 | tf_op jit(solution)/shard_map/ppermute | solution.py:32
  802.6 47.1 %collective-permute-start.44 = (bf16[128,2304]{1,0:T(8,128)(2,1)S(1)}, bf16[128,2304]{1,0:T(8,128)(2,1)S(1)}, u32[]{:S(2)}, u32[]{:S(2)}) collective-permute-start(bf16[128,2304]{1,0:T(8,128)(2,1)S(1)} %get-tuple-element.88), channel_id=1, source_target_pairs={{0,4},{1,5},{2,6},{3,7},{4,0},{5,1},{6,2},{7,3},{8,12},{9,13},{10,... | collective-permute-start | bytes 1769480 | tf_op jit(solution)/shard_map/ppermute | solution.py:32
  803.2 46.5 %collective-permute-start.42 = (bf16[128,2304]{1,0:T(8,128)(2,1)S(1)}, bf16[128,2304]{1,0:T(8,128)(2,1)S(1)}, u32[]{:S(2)}, u32[]{:S(2)}) collective-permute-start(bf16[128,2304]{1,0:T(8,128)(2,1)S(1)} %get-tuple-element.86), channel_id=1, source_target_pairs={{0,1},{1,0},{2,3},{3,2},{4,5},{5,4},{6,7},{7,6},{8,9},{9,8},{10,11... | collective-permute-start | bytes 1769480 | tf_op jit(solution)/shard_map/ppermute | solution.py:32
  815.4 26.8 %collective-permute-start.56 = (bf16[2,144,1152]{2,1,0:T(8,128)(2,1)S(1)}, bf16[2,144,1152]{2,1,0:T(8,128)(2,1)S(1)}, u32[]{:S(2)}, u32[]{:S(2)}) collective-permute-start(bf16[2,144,1152]{2,1,0:T(8,128)(2,1)S(1)} %dynamic-slice_bitcast_fusion), channel_id=1, source_target_pairs={{0,4},{1,5},{2,6},{3,7},{4,0},{5,1},{6,2},{7,3},{8,12},{9,13},{10,... | collective-permute-start | bytes 1990664 | tf_op jit(solution)/shard_map/ppermute | solution.py:32
  854.4 9.0 collective-permute-start.58
  863.5 6.5 collective-permute-start.59
  866.4 43.8 %collective-permute-start.46 = (bf16[2,288,1024]{2,1,0:T(8,128)(2,1)S(1)}, bf16[2,288,1024]{2,1,0:T(8,128)(2,1)}, u32[]{:S(2)}, u32[]{:S(2)}) collective-permute-start(bf16[2,288,1024]{2,1,0:T(8,128)(2,1)S(1)} %fusion.54), channel_id=1, source_target_pairs={{0,8},{1,9},{2,10},{3,11},{4,12},{5,13},{6,14},{7,15},{8,0},{9,1},... | collective-permute-start | bytes 3538952 | tf_op jit(solution)/shard_map/ppermute | solution.py:32
  875.0 46.8 %collective-permute-start.62 = (f32[1,4,144]{2,0,1:T(1,128)S(1)}, f32[1,4,144]{2,0,1:T(1,128)}, u32[]{:S(2)}, u32[]{:S(2)}) collective-permute-start(f32[1,4,144]{2,0,1:T(1,128)S(1)} %fusion.176), channel_id=1, source_target_pairs={{0,1},{1,0},{2,3},{3,2},{4,5},{5,4},{6,7},{7,6},{8,9},{9,8},{10,11... | collective-permute-start | bytes 6920 | tf_op jit(solution)/shard_map/ppermute | solution.py:32
  913.5 29.0 %collective-permute-start.47 = (bf16[288,1024]{1,0:T(8,128)(2,1)}, bf16[288,1024]{1,0:T(8,128)(2,1)}, u32[]{:S(2)}, u32[]{:S(2)}) collective-permute-start(bf16[288,1024]{1,0:T(8,128)(2,1)} %fusion.103), channel_id=1, source_target_pairs={{0,16},{1,17},{2,18},{3,19},{4,20},{5,21},{6,22},{7,23},{8,24},{9,... | collective-permute-start | bytes 1769480 | tf_op jit(solution)/shard_map/ppermute | solution.py:32
  917.5 27.9 %collective-permute-start.54 = (bf16[2,144,1152]{2,1,0:T(8,128)(2,1)S(1)}, bf16[2,144,1152]{2,1,0:T(8,128)(2,1)S(1)}, u32[]{:S(2)}, u32[]{:S(2)}) collective-permute-start(bf16[2,144,1152]{2,1,0:T(8,128)(2,1)S(1)} %dynamic-slice_bitcast_fusion.1), channel_id=1, source_target_pairs={{0,4},{1,5},{2,6},{3,7},{4,0},{5,1},{6,2},{7,3},{8,12},{9,13},{10,... | collective-permute-start | bytes 1990664 | tf_op jit(solution)/shard_map/ppermute | solution.py:32
  943.8 9.0 collective-permute-start.48
  945.6 9.8 %collective-permute-start.55 = (bf16[2,144,1152]{2,1,0:T(8,128)(2,1)S(1)}, bf16[2,144,1152]{2,1,0:T(8,128)(2,1)S(1)}, u32[]{:S(2)}, u32[]{:S(2)}) collective-permute-start(bf16[2,144,1152]{2,1,0:T(8,128)(2,1)S(1)} %fusion.90), channel_id=1, source_target_pairs={{0,2},{1,3},{2,0},{3,1},{4,6},{5,7},{6,4},{7,5},{8,10},{9,11},{10,... | collective-permute-start | bytes 1990664 | tf_op jit(solution)/shard_map/ppermute | solution.py:32
  (89 other events, 932.6 us)
Sparse Core Ops, SparseCore 0:
  26.3 77.5 all-gather.4
  111.0 114.4 all-gather.6
  227.1 102.7 all-gather.8
  331.3 98.2 all-gather.10
  519.7 92.2 reduce-scatter.3
  614.3 109.4 reduce-scatter.5
  791.1 108.5 reduce-scatter.7

commit v4 on v3

--- a/solution.py
+++ b/solution.py
@@ -478,9 +478,10 @@
     attn_grad_rows = spread_rows(after(attn_grad.astype(bf16), up_terms))
     out_terms = fold_cores(contract_rows(attn_grad_rows, mixed_low))
     mixed_grad = after(mm(attn_grad_rows, out_full).astype(bf16), down_sums, out_terms)
-    delta = jnp.sum(
-        (mixed_grad.astype(f32) * mixed).reshape(-1, 2, HEAD_DIM), axis=-1
-    ).T
+    products = mixed_grad.astype(f32) * mixed
+    delta = jnp.stack(
+        [jnp.sum(products[:, :HEAD_DIM], axis=-1), jnp.sum(products[:, HEAD_DIM:], axis=-1)]
+    )
     query_grad, key_value_grad, sent = attend_back(
         key_bases, limit, lse, delta, query_rot, mixed_grad, keys, values
     )

time: 970 us -> 966 us (level)
    unnamed x178 -> x164, local copies, waits for them, and re-layouts: 35.3 us -> 35.3 us
  transfers between devices with their start and end apart: 70 -> 70, of which waited for: 45 -> 45; matrix products, arithmetic and copies ran while one was open for 20% -> 19% of each run, Pallas kernels for 3% -> 3%
where the time goes in v4:
time: 966 us; the launch traced here: 961 us
  waiting for transfers between devices  595 us (62%)
  matrix products  117 us (12%)
  other arithmetic  71.6 us (7%)
  starting transfers between devices  66.8 us (7%)
  local copies, waits for them, and re-layouts  60.3 us (6%)
  Pallas kernels  32.9 us (3%)
  between operations  17.2 us (2%)
    ppermute x63, waiting for transfers between devices, swap(): return lax.ppermute(value, AXES, [(i, i ^ mask) for i in range(count)])  494 us
    ppermute x63, starting transfers between devices, swap(): return lax.ppermute(value, AXES, [(i, i ^ mask) for i in range(count)])  66.4 us
    all_gather x1, waiting for transfers between devices, gather_attention_weight(): full = lax.all_gather(full, ('outer', 'zh', 'zl', 'c'), axis=0, tiled=True)  55.4 us
    dot_general x5, matrix products, mm(): return jnp.dot(left, right, preferred_element_type=f32)  46.3 us
    all_gather x3, waiting for transfers between devices, gather_ffn_weight(): lax.all_gather(block, ('outer', 'zh', 'zl'), axis=0, tiled=True)  45.9 us
    dot_general x10, matrix products, contract_cols(): lax.dot_general(left, right, (((1,), (1,)), ((), ())), preferred_element_...  36 us
    unnamed x164, local copies, waits for them, and re-layouts  35.3 us
    dot_general x5, matrix products, contract_rows(): lax.dot_general(left, right, (((0,), (0,)), ((), ())), preferred_element_...  34.3 us
  transfers between devices with their start and end apart: 70, of which 45 were waited for; matrix products, arithmetic and copies ran while one was open for 19% of the time, Pallas kernels for 3%

profile of v4, /device:TPU:0, one launch (start us, length us, event | category | flops | bytes accessed | tf_op | source)
XLA Modules:
  0.0 960.6 jit_solution(15697522852712875954)
XLA Ops:
  11.0 3.0 collective-permute-start.3
  14.1 11.0 %collective-permute-done.3.refs_1_ = bf16[144,1664]{1,0:T(8,128)(2,1)S(1)} collective-permute-done((bf16[144,1664]{1,0:T(8,128)(2,1)S(1)}, bf16[144,1664]{1,0:T(8,128)(2,1)S(1)}, u32[]{:S(2)}, u32[]{:S(2)}) %collective-permute-start.3) | collective-permute-done | bytes 479264 | tf_op jit(solution)/shard_map/ppermute | solution.py:32
  30.0 14.4 %collective-permute-done.17.refs_1_ = bf16[144,2304]{1,0:T(8,128)(2,1)S(1)} collective-permute-done((bf16[144,2304]{1,0:T(8,128)(2,1)S(1)}, bf16[144,2304]{1,0:T(8,128)(2,1)S(1)}, u32[]{:S(2)}, u32[]{:S(2)}) %collective-permute-start.17) | collective-permute-done | bytes 663584 | tf_op jit(solution)/shard_map/ppermute | solution.py:32
  48.5 55.4 %all-gather.5.cloned.1.call-done = bf16[2304,1664]{1,0:T(8,128)(2,1)} async-done(((bf16[288,1664]{1,0:T(8,128)(2,1)}), bf16[2304,1664]{1,0:T(8,128)(2,1)}) %all-gather.5.cloned.1.call-update) | async-done | bytes 7667728 | tf_op jit(solution)/shard_map/all_gather | solution.py:304
  103.9 3.7 copy.64
  107.7 3.1 copy-done.2
  117.9 25.4 %collective-permute-done.19.refs_1_ = bf16[144,2304]{1,0:T(8,128)(2,1)S(1)} collective-permute-done((bf16[144,2304]{1,0:T(8,128)(2,1)S(1)}, bf16[144,2304]{1,0:T(8,128)(2,1)S(1)}, u32[]{:S(2)}, u32[]{:S(2)}) %collective-permute-start.19) | collective-permute-done | bytes 663584 | tf_op jit(solution)/shard_map/ppermute | solution.py:32
  143.8 11.6 %collective-permute-done.1 = bf16[128,2304]{1,0:T(8,128)(2,1)} collective-permute-done((bf16[128,2304]{1,0:T(8,128)(2,1)}, bf16[128,2304]{1,0:T(8,128)(2,1)}, u32[]{:S(2)}, u32[]{:S(2)}) %collective-permute-start.1) | collective-permute-done | bytes 589856 | tf_op jit(solution)/shard_map/ppermute | solution.py:32
  162.6 5.7 fusion.23
  171.6 32.2 %collective-permute-done.4 = bf16[512,256]{1,0:T(8,128)(2,1)S(1)} collective-permute-done((bf16[512,256]{1,0:T(8,128)(2,1)S(1)}, bf16[512,256]{1,0:T(8,128)(2,1)S(1)}, u32[]{:S(2)}, u32[]{:S(2)}) %collective-permute-start.4) | collective-permute-done | bytes 262176 | tf_op jit(solution)/shard_map/ppermute | solution.py:32
  208.7 18.3 %collective-permute-done.7 = bf16[512,256]{1,0:T(8,128)(2,1)S(1)} collective-permute-done((bf16[512,256]{1,0:T(8,128)(2,1)S(1)}, bf16[512,256]{1,0:T(8,128)(2,1)S(1)}, u32[]{:S(2)}, u32[]{:S(2)}) %collective-permute-start.7) | collective-permute-done | bytes 262176 | tf_op jit(solution)/shard_map/ppermute | solution.py:32
  227.0 4.6 collective-permute-start.8
  235.9 31.9 %collective-permute-done.8 = bf16[1024,256]{1,0:T(8,128)(2,1)S(1)} collective-permute-done((bf16[1024,256]{1,0:T(8,128)(2,1)S(1)}, bf16[1024,256]{1,0:T(8,128)(2,1)S(1)}, u32[]{:S(2)}, u32[]{:S(2)}) %collective-permute-start.8) | collective-permute-done | bytes 524320 | tf_op jit(solution)/shard_map/ppermute | solution.py:32
  272.3 11.6 %attend.1 = (f32[512,512]{1,0:T(8,128)S(1)}, bf16[512,512]{1,0:T(8,128)(2,1)S(1)}, f32[2,512]{1,0:T(2,128)S(1)}) custom-call(s32[32]{0:T(128)S(1)} %stack.289.base_ref, s32[1,512]{1,0:T(1,128)S(1)} %add_maximum_fusion.limit_ref, bf16[512,512]{1,0:T(8,128)(2,1)S(1)} %pad_maximum_fusion.15.q_ref, bf16[4096,256]{1,0:T(8,128)(2,1)S(1)} %pad_maximum_fusion.4.k_ref, ...), custom_call_target="tpu_custom_call" | custom-call | flops 4294967296 | bytes 8388608 | tf_op jit(solution)/shard_map/attend/pallas_call | solution.py:179
  283.9 3.2 convolution_convert_fusion.5
  288.0 2.8 collective-permute-start.12
  293.3 12.2 %collective-permute-done.12 = bf16[128,2304]{1,0:T(8,128)(2,1)} collective-permute-done((bf16[128,2304]{1,0:T(8,128)(2,1)}, bf16[128,2304]{1,0:T(8,128)(2,1)}, u32[]{:S(2)}, u32[]{:S(2)}) %collective-permute-start.12) | collective-permute-done | bytes 589856 | tf_op jit(solution)/shard_map/ppermute | solution.py:32
  305.5 11.9 %collective-permute-done.11 = bf16[128,2304]{1,0:T(8,128)(2,1)} collective-permute-done((bf16[128,2304]{1,0:T(8,128)(2,1)S(1)}, bf16[128,2304]{1,0:T(8,128)(2,1)}, u32[]{:S(2)}, u32[]{:S(2)}) %collective-permute-start.11) | collective-permute-done | bytes 589856 | tf_op jit(solution)/shard_map/ppermute | solution.py:32
  317.7 3.2 multiply_reduce_fusion.6
  327.9 12.7 %collective-permute-done.13 = bf16[128,2304]{1,0:T(8,128)(2,1)S(1)} collective-permute-done((bf16[128,2304]{1,0:T(8,128)(2,1)S(1)}, bf16[128,2304]{1,0:T(8,128)(2,1)S(1)}, u32[]{:S(2)}, u32[]{:S(2)}) %collective-permute-start.13) | collective-permute-done | bytes 589856 | tf_op jit(solution)/shard_map/ppermute | solution.py:32
  340.6 12.8 %collective-permute-done.14 = bf16[128,2304]{1,0:T(8,128)(2,1)S(1)} collective-permute-done((bf16[128,2304]{1,0:T(8,128)(2,1)S(1)}, bf16[128,2304]{1,0:T(8,128)(2,1)S(1)}, u32[]{:S(2)}, u32[]{:S(2)}) %collective-permute-start.14) | collective-permute-done | bytes 589856 | tf_op jit(solution)/shard_map/ppermute | solution.py:32
  359.7 11.5 %fusion.197.refs_0_ = f32[1024,1152]{1,0:T(8,128)} fusion(bf16[1024,2304]{1,0:T(8,128)(2,1)} %constant_dynamic-update-slice_fusion.1, bf16[2304,1152]{1,0:T(8,128)(2,1)} %all-gather.7.cloned.1.call-done), kind=kOutput, calls=%fused_computation.399 | convolution fusion | flops 5435817984 | bytes 14745600 | tf_op jit(solution)/shard_map/dot_general | solution.py:123
  371.2 12.5 %fusion.18 = (bf16[1024,1152]{1,0:T(8,128)(2,1)}, f32[1024,1152]{1,0:T(8,128)}) fusion(f32[1024,1152]{1,0:T(8,128)} %fusion.197.refs_0_, bf16[1024,2304]{1,0:T(8,128)(2,1)} %constant_dynamic-update-slice_fusion.1, bf16[2304,1152]{1,0:T(8,128)(2,1)} %all-gather.9.cloned.1.call-done), kind=kOutput, calls=%fused_computation.28 | convolution fusion | flops 5447614464 | bytes 21823488 | tf_op jit(solution)/shard_map/dot_general | solution.py:123
  383.7 45.9 %all-gather.11.cloned.1.call-done = bf16[2304,1152]{1,0:T(8,128)(2,1)} async-done(((bf16[576,1152]{1,0:T(8,128)(2,1)}), bf16[2304,1152]{1,0:T(8,128)(2,1)}) %all-gather.11.cloned.1.call-update) | async-done | bytes 5308432 | tf_op jit(solution)/shard_map/all_gather | solution.py:331
  429.6 6.2 convolution_convert_fusion.3
  436.0 4.5 collective-permute-done.23
  440.5 3.2 fusion.195
  447.4 13.6 %collective-permute-done.26 = bf16[128,2304]{1,0:T(8,128)(2,1)S(1)} collective-permute-done((bf16[128,2304]{1,0:T(8,128)(2,1)S(1)}, bf16[128,2304]{1,0:T(8,128)(2,1)S(1)}, u32[]{:S(2)}, u32[]{:S(2)}) %collective-permute-start.26) | collective-permute-done | bytes 589856 | tf_op jit(solution)/shard_map/ppermute | solution.py:32
  461.1 11.8 %collective-permute-done.25 = bf16[128,2304]{1,0:T(8,128)(2,1)S(1)} collective-permute-done((bf16[128,2304]{1,0:T(8,128)(2,1)S(1)}, bf16[128,2304]{1,0:T(8,128)(2,1)S(1)}, u32[]{:S(2)}, u32[]{:S(2)}) %collective-permute-start.25) | collective-permute-done | bytes 589856 | tf_op jit(solution)/shard_map/ppermute | solution.py:32
  478.9 12.7 %collective-permute-done.27 = bf16[128,2304]{1,0:T(8,128)(2,1)S(1)} collective-permute-done((bf16[128,2304]{1,0:T(8,128)(2,1)S(1)}, bf16[128,2304]{1,0:T(8,128)(2,1)S(1)}, u32[]{:S(2)}, u32[]{:S(2)}) %collective-permute-start.27) | collective-permute-done | bytes 589856 | tf_op jit(solution)/shard_map/ppermute | solution.py:32
  491.6 12.8 %collective-permute-done.28 = bf16[128,2304]{1,0:T(8,128)(2,1)S(1)} collective-permute-done((bf16[128,2304]{1,0:T(8,128)(2,1)S(1)}, bf16[128,2304]{1,0:T(8,128)(2,1)S(1)}, u32[]{:S(2)}, u32[]{:S(2)}) %collective-permute-start.28) | collective-permute-done | bytes 589856 | tf_op jit(solution)/shard_map/ppermute | solution.py:32
  504.8 4.4 collective-permute-done.30
  511.5 8.1 convolution_convert_fusion.2.refs_1_
  522.2 3.3 copy-done.12
  529.5 13.2 %multiply_convert_fusion = (bf16[1024,1152]{1,0:T(8,128)(2,1)S(1)}, bf16[1024,1152]{1,0:T(8,128)(2,1)S(1)}) fusion(f32[1024,1152]{1,0:T(8,128)} %copy-done.13, f32[1024,1152]{1,0:T(8,128)} %get-tuple-element.123, bf16[1024,2304]{1,0:T(8,128)(2,1)S(1)} %copy-done.43, bf16[2304,1152]{1,0:T(8,128)(2,1)} %all-gather.11.cloned.1.call-done), kind=kOutput, calls=%fused_computation.32 | convolution fusion | flops 5464129536 | bytes 24182784 | tf_op jit(solution)/shard_map/dot_general | solution.py:123
  542.8 3.2 fusion.59
  546.1 3.5 fusion.19
  549.8 4.5 fusion.64
  554.4 9.8 %convolution_convert_fusion.1.refs_1_.refs_0_ = bf16[2304,1152]{1,0:T(8,128)(2,1)} fusion(bf16[1024,2304]{1,0:T(8,128)(2,1)} %constant_dynamic-update-slice_fusion.1, bf16[1024,1152]{1,0:T(8,128)(2,1)S(1)} %get-tuple-element.50), kind=kOutput, calls=%fused_computation.1 | convolution fusion | flops 5438472192 | bytes 12386304 | tf_op jit(solution)/shard_map/dot_general | solution.py:127
  564.1 5.2 fusion.196
  574.1 9.7 %convolution_convert_fusion = bf16[2304,1152]{1,0:T(8,128)(2,1)} fusion(bf16[1024,2304]{1,0:T(8,128)(2,1)} %constant_dynamic-update-slice_fusion.1, bf16[1024,1152]{1,0:T(8,128)(2,1)S(1)} %copy-done.63), kind=kOutput, calls=%fused_computation | convolution fusion | flops 5438472192 | bytes 12386304 | tf_op jit(solution)/shard_map/dot_general | solution.py:127
  583.9 4.0 collective-permute-done.34
  588.0 11.5 %collective-permute-done.33 = bf16[128,2304]{1,0:T(8,128)(2,1)S(1)} collective-permute-done((bf16[128,2304]{1,0:T(8,128)(2,1)}, bf16[128,2304]{1,0:T(8,128)(2,1)S(1)}, u32[]{:S(2)}, u32[]{:S(2)}) %collective-permute-start.33) | collective-permute-done | bytes 589856 | tf_op jit(solution)/shard_map/ppermute | solution.py:32
  599.5 2.8 multiply_reduce_fusion
  609.5 13.7 %collective-permute-done.37 = bf16[128,2304]{1,0:T(8,128)(2,1)S(1)} collective-permute-done((bf16[128,2304]{1,0:T(8,128)(2,1)S(1)}, bf16[128,2304]{1,0:T(8,128)(2,1)S(1)}, u32[]{:S(2)}, u32[]{:S(2)}) %collective-permute-start.37) | collective-permute-done | bytes 589856 | tf_op jit(solution)/shard_map/ppermute | solution.py:32
  623.2 11.3 %collective-permute-done.36 = bf16[128,2304]{1,0:T(8,128)(2,1)S(1)} collective-permute-done((bf16[128,2304]{1,0:T(8,128)(2,1)S(1)}, bf16[128,2304]{1,0:T(8,128)(2,1)S(1)}, u32[]{:S(2)}, u32[]{:S(2)}) %collective-permute-start.36) | collective-permute-done | bytes 589856 | tf_op jit(solution)/shard_map/ppermute | solution.py:32
  638.5 3.4 fusion.42.refs_0_
  646.7 21.2 %attend_back.1 = (f32[512,512]{1,0:T(8,128)S(1)}, f32[2048,512]{1,0:T(8,128)}, bf16[2048,512]{1,0:T(8,128)(2,1)}) custom-call(s32[32]{0:T(128)S(1)} %copy-done.23, s32[1,512]{1,0:T(1,128)S(1)} %copy-done.21, f32[2,512]{1,0:T(2,128)S(1)} %get-tuple-element.20.lse_ref, f32[2,512]{1,0:T(2,128)S(1)} %pad_maximum_fusion.21.delta_ref, ...), custom_call_target="tpu_custom_call" | custom-call | tf_op jit(solution)/shard_map/attend_back/pallas_call | solution.py:265
  669.5 39.4 %collective-permute-done.49 = bf16[2,288,512]{2,1,0:T(8,128)(2,1)S(1)} collective-permute-done((bf16[2,288,512]{2,1,0:T(8,128)(2,1)S(1)}, bf16[2,288,512]{2,1,0:T(8,128)(2,1)S(1)}, u32[]{:S(2)}, u32[]{:S(2)}) %collective-permute-start.49) | collective-permute-done | bytes 589856 | tf_op jit(solution)/shard_map/ppermute | solution.py:32
  709.6 3.6 convert_add_fusion.2
  718.7 9.8 %collective-permute-done.50 = bf16[288,512]{1,0:T(8,128)(2,1)S(1)} collective-permute-done((bf16[288,512]{1,0:T(8,128)(2,1)S(1)}, bf16[288,512]{1,0:T(8,128)(2,1)S(1)}, u32[]{:S(2)}, u32[]{:S(2)}) %collective-permute-start.50) | collective-permute-done | bytes 294944 | tf_op jit(solution)/shard_map/ppermute | solution.py:32
  732.3 3.2 collective-permute-done.51
  738.6 11.1 %collective-permute-done.40 = bf16[1024,512]{1,0:T(8,128)(2,1)} collective-permute-done((bf16[1024,512]{1,0:T(8,128)(2,1)}, bf16[1024,512]{1,0:T(8,128)(2,1)}, u32[]{:S(2)}, u32[]{:S(2)}) %collective-permute-start.40) | collective-permute-done | bytes 1048608 | tf_op jit(solution)/shard_map/ppermute | solution.py:32
  751.9 2.8 collective-permute-start.41
  758.2 19.7 %collective-permute-done.41.refs_1_ = bf16[512,512]{1,0:T(8,128)(2,1)S(1)} collective-permute-done((bf16[512,512]{1,0:T(8,128)(2,1)S(1)}, bf16[512,512]{1,0:T(8,128)(2,1)S(1)}, u32[]{:S(2)}, u32[]{:S(2)}) %collective-permute-start.41) | collective-permute-done | bytes 524320 | tf_op jit(solution)/shard_map/ppermute | solution.py:32
  793.9 5.3 fusion.79
  803.0 11.3 %collective-permute-done.52 = bf16[2,144,1152]{2,1,0:T(8,128)(2,1)S(1)} collective-permute-done((bf16[2,144,1152]{2,1,0:T(8,128)(2,1)S(1)}, bf16[2,144,1152]{2,1,0:T(8,128)(2,1)S(1)}, u32[]{:S(2)}, u32[]{:S(2)}) %collective-permute-start.52) | collective-permute-done | bytes 663584 | tf_op jit(solution)/shard_map/ppermute | solution.py:32
  816.0 25.1 %collective-permute-done.56 = bf16[2,144,1152]{2,1,0:T(8,128)(2,1)S(1)} collective-permute-done((bf16[2,144,1152]{2,1,0:T(8,128)(2,1)S(1)}, bf16[2,144,1152]{2,1,0:T(8,128)(2,1)S(1)}, u32[]{:S(2)}, u32[]{:S(2)}) %collective-permute-start.56) | collective-permute-done | bytes 663584 | tf_op jit(solution)/shard_map/ppermute | solution.py:32
  853.6 6.0 collective-permute-done.58
  872.7 33.7 %collective-permute-done.46 = bf16[2,288,1024]{2,1,0:T(8,128)(2,1)} collective-permute-done((bf16[2,288,1024]{2,1,0:T(8,128)(2,1)S(1)}, bf16[2,288,1024]{2,1,0:T(8,128)(2,1)}, u32[]{:S(2)}, u32[]{:S(2)}) %collective-permute-start.46) | collective-permute-done | bytes 1179680 | tf_op jit(solution)/shard_map/ppermute | solution.py:32
  909.6 2.8 collective-permute-start.47
  915.2 2.8 fusion.49
  919.3 19.3 %collective-permute-done.47 = bf16[288,1024]{1,0:T(8,128)(2,1)} collective-permute-done((bf16[288,1024]{1,0:T(8,128)(2,1)}, bf16[288,1024]{1,0:T(8,128)(2,1)}, u32[]{:S(2)}, u32[]{:S(2)}) %collective-permute-start.47) | collective-permute-done | bytes 589856 | tf_op jit(solution)/shard_map/ppermute | solution.py:32
  941.9 7.1 collective-permute-done.48
  (454 shorter events, 182.0 us)
Async XLA Ops:
  7.2 96.7 %all-gather.5.cloned.1.call-start = ((), (), s32[]{:S(2)}) async-start(), calls=%async_computation.3 | async-start | bytes 8626176 | tf_op jit(solution)/shard_map/all_gather | solution.py:304
  11.0 14.0 %collective-permute-start.3 = (bf16[144,1664]{1,0:T(8,128)(2,1)S(1)}, bf16[144,1664]{1,0:T(8,128)(2,1)S(1)}, u32[]{:S(2)}, u32[]{:S(2)}) collective-permute-start(bf16[144,1664]{1,0:T(8,128)(2,1)S(1)} %dynamic-slice_bitcast_fusion.3), channel_id=1, source_target_pairs={{0,4},{1,5},{2,6},{3,7},{4,0},{5,1},{6,2},{7,3},{8,12},{9,13},{10,... | collective-permute-start | bytes 1437704 | tf_op jit(solution)/shard_map/ppermute | solution.py:32
  26.2 333.5 %all-gather.7.cloned.1.call-start = ((), (), s32[]{:S(2)}) async-start(), calls=%async_computation.4 | async-start | bytes 6635520 | tf_op jit(solution)/shard_map/all_gather | solution.py:331
  28.2 16.2 %collective-permute-start.17 = (bf16[144,2304]{1,0:T(8,128)(2,1)S(1)}, bf16[144,2304]{1,0:T(8,128)(2,1)S(1)}, u32[]{:S(2)}, u32[]{:S(2)}) collective-permute-start(bf16[144,2304]{1,0:T(8,128)(2,1)S(1)} %after.13), channel_id=1, source_target_pairs={{0,4},{1,5},{2,6},{3,7},{4,0},{5,1},{6,2},{7,3},{8,12},{9,13},{10,... | collective-permute-start | bytes 1990664 | tf_op jit(solution)/shard_map/ppermute | solution.py:32
  110.8 260.4 %all-gather.9.cloned.1.call-start = ((), (), s32[]{:S(2)}) async-start(), calls=%async_computation.5 | async-start | bytes 6635520 | tf_op jit(solution)/shard_map/all_gather | solution.py:331
  112.9 30.4 %collective-permute-start.19 = (bf16[144,2304]{1,0:T(8,128)(2,1)S(1)}, bf16[144,2304]{1,0:T(8,128)(2,1)S(1)}, u32[]{:S(2)}, u32[]{:S(2)}) collective-permute-start(bf16[144,2304]{1,0:T(8,128)(2,1)S(1)} %after.15), channel_id=1, source_target_pairs={{0,4},{1,5},{2,6},{3,7},{4,0},{5,1},{6,2},{7,3},{8,12},{9,13},{10,... | collective-permute-start | bytes 1990664 | tf_op jit(solution)/shard_map/ppermute | solution.py:32
  114.4 29.3 %collective-permute-start.2 = (bf16[128,2304]{1,0:T(8,128)(2,1)}, bf16[128,2304]{1,0:T(8,128)(2,1)}, u32[]{:S(2)}, u32[]{:S(2)}) collective-permute-start(bf16[128,2304]{1,0:T(8,128)(2,1)} %param.14), channel_id=1, source_target_pairs={{0,5},{1,4},{2,7},{3,6},{4,1},{5,0},{6,3},{7,2},{8,13},{9,12},{10,... | collective-permute-start | bytes 1769480 | tf_op jit(solution)/shard_map/ppermute | solution.py:32
  115.9 39.5 %collective-permute-start.1 = (bf16[128,2304]{1,0:T(8,128)(2,1)}, bf16[128,2304]{1,0:T(8,128)(2,1)}, u32[]{:S(2)}, u32[]{:S(2)}) collective-permute-start(bf16[128,2304]{1,0:T(8,128)(2,1)} %param.14), channel_id=1, source_target_pairs={{0,4},{1,5},{2,6},{3,7},{4,0},{5,1},{6,2},{7,3},{8,12},{9,13},{10,... | collective-permute-start | bytes 1769480 | tf_op jit(solution)/shard_map/ppermute | solution.py:32
  117.4 38.0 %collective-permute-start = (bf16[128,2304]{1,0:T(8,128)(2,1)}, bf16[128,2304]{1,0:T(8,128)(2,1)}, u32[]{:S(2)}, u32[]{:S(2)}) collective-permute-start(bf16[128,2304]{1,0:T(8,128)(2,1)} %param.14), channel_id=1, source_target_pairs={{0,1},{1,0},{2,3},{3,2},{4,5},{5,4},{6,7},{7,6},{8,9},{9,8},{10,11... | collective-permute-start | bytes 1769480 | tf_op jit(solution)/shard_map/ppermute | solution.py:32
  143.6 13.6 %collective-permute-start.20 = (bf16[2,144,1152]{2,1,0:T(8,128)(2,1)S(1)}, bf16[2,144,1152]{2,1,0:T(8,128)(2,1)S(1)}, u32[]{:S(2)}, u32[]{:S(2)}) collective-permute-start(bf16[2,144,1152]{2,1,0:T(8,128)(2,1)S(1)} %broadcast_select_fusion.14), channel_id=1, source_target_pairs={{0,2},{1,3},{2,0},{3,1},{4,6},{5,7},{6,4},{7,5},{8,10},{9,11},{10,... | collective-permute-start | bytes 1990664 | tf_op jit(solution)/shard_map/ppermute | solution.py:32
  159.0 270.6 %all-gather.11.cloned.1.call-start = ((), (), s32[]{:S(2)}) async-start(), calls=%async_computation.6 | async-start | bytes 6635520 | tf_op jit(solution)/shard_map/all_gather | solution.py:331
  170.4 33.5 %collective-permute-start.4 = (bf16[512,256]{1,0:T(8,128)(2,1)S(1)}, bf16[512,256]{1,0:T(8,128)(2,1)S(1)}, u32[]{:S(2)}, u32[]{:S(2)}) collective-permute-start(bf16[512,256]{1,0:T(8,128)(2,1)S(1)} %pad_maximum_fusion.20), channel_id=1, source_target_pairs={{0,16},{1,17},{2,18},{3,19},{4,20},{5,21},{6,22},{7,23},{8,24},{9,... | collective-permute-start | bytes 786440 | tf_op jit(solution)/shard_map/ppermute | solution.py:32
  204.7 28.7 %collective-permute-start.5 = (bf16[1024,256]{1,0:T(8,128)(2,1)}, bf16[1024,256]{1,0:T(8,128)(2,1)}, u32[]{:S(2)}, u32[]{:S(2)}) collective-permute-start(bf16[1024,256]{1,0:T(8,128)(2,1)} %pad_maximum_fusion.16), channel_id=1, source_target_pairs={{0,8},{1,9},{2,10},{3,11},{4,12},{5,13},{6,14},{7,15},{8,0},{9,1},... | collective-permute-start | bytes 1572872 | tf_op jit(solution)/shard_map/ppermute | solution.py:32
  204.7 29.9 %collective-permute-start.21 = (bf16[144,2304]{1,0:T(8,128)(2,1)S(1)}, bf16[144,2304]{1,0:T(8,128)(2,1)}, u32[]{:S(2)}, u32[]{:S(2)}) collective-permute-start(bf16[144,2304]{1,0:T(8,128)(2,1)S(1)} %after.16), channel_id=1, source_target_pairs={{0,4},{1,5},{2,6},{3,7},{4,0},{5,1},{6,2},{7,3},{8,12},{9,13},{10,... | collective-permute-start | bytes 1990664 | tf_op jit(solution)/shard_map/ppermute | solution.py:32
  206.3 20.6 %collective-permute-start.7 = (bf16[512,256]{1,0:T(8,128)(2,1)S(1)}, bf16[512,256]{1,0:T(8,128)(2,1)S(1)}, u32[]{:S(2)}, u32[]{:S(2)}) collective-permute-start(bf16[512,256]{1,0:T(8,128)(2,1)S(1)} %slice.680), channel_id=1, source_target_pairs={{0,16},{1,17},{2,18},{3,19},{4,20},{5,21},{6,22},{7,23},{8,24},{9,... | collective-permute-start | bytes 786440 | tf_op jit(solution)/shard_map/ppermute | solution.py:32
  227.0 40.8 %collective-permute-start.8 = (bf16[1024,256]{1,0:T(8,128)(2,1)S(1)}, bf16[1024,256]{1,0:T(8,128)(2,1)S(1)}, u32[]{:S(2)}, u32[]{:S(2)}) collective-permute-start(bf16[1024,256]{1,0:T(8,128)(2,1)S(1)} %pad_maximum_fusion.17), channel_id=1, source_target_pairs={{0,8},{1,9},{2,10},{3,11},{4,12},{5,13},{6,14},{7,15},{8,0},{9,1},... | collective-permute-start | bytes 1572872 | tf_op jit(solution)/shard_map/ppermute | solution.py:32
  234.5 34.3 %collective-permute-start.6 = (bf16[2048,256]{1,0:T(8,128)(2,1)S(1)}, bf16[2048,256]{1,0:T(8,128)(2,1)S(1)}, u32[]{:S(2)}, u32[]{:S(2)}) collective-permute-start(bf16[2048,256]{1,0:T(8,128)(2,1)S(1)} %pad_maximum_fusion.9), channel_id=1, source_target_pairs={{0,2},{1,3},{2,0},{3,1},{4,6},{5,7},{6,4},{7,5},{8,10},{9,11},{10,... | collective-permute-start | bytes 3145736 | tf_op jit(solution)/shard_map/ppermute | solution.py:32
  268.1 23.4 %collective-permute-start.22 = (bf16[2,144,1152]{2,1,0:T(8,128)(2,1)S(1)}, bf16[2,144,1152]{2,1,0:T(8,128)(2,1)S(1)}, u32[]{:S(2)}, u32[]{:S(2)}) collective-permute-start(bf16[2,144,1152]{2,1,0:T(8,128)(2,1)S(1)} %broadcast_select_fusion.12), channel_id=1, source_target_pairs={{0,2},{1,3},{2,0},{3,1},{4,6},{5,7},{6,4},{7,5},{8,10},{9,11},{10,... | collective-permute-start | bytes 1990664 | tf_op jit(solution)/shard_map/ppermute | solution.py:32
  288.0 17.4 %collective-permute-start.12 = (bf16[128,2304]{1,0:T(8,128)(2,1)}, bf16[128,2304]{1,0:T(8,128)(2,1)}, u32[]{:S(2)}, u32[]{:S(2)}) collective-permute-start(bf16[128,2304]{1,0:T(8,128)(2,1)} %get-tuple-element.92), channel_id=1, source_target_pairs={{0,5},{1,4},{2,7},{3,6},{4,1},{5,0},{6,3},{7,2},{8,13},{9,12},{10,... | collective-permute-start | bytes 1769480 | tf_op jit(solution)/shard_map/ppermute | solution.py:32
  290.9 26.5 %collective-permute-start.11 = (bf16[128,2304]{1,0:T(8,128)(2,1)S(1)}, bf16[128,2304]{1,0:T(8,128)(2,1)}, u32[]{:S(2)}, u32[]{:S(2)}) collective-permute-start(bf16[128,2304]{1,0:T(8,128)(2,1)S(1)} %get-tuple-element.93), channel_id=1, source_target_pairs={{0,4},{1,5},{2,6},{3,7},{4,0},{5,1},{6,2},{7,3},{8,12},{9,13},{10,... | collective-permute-start | bytes 1769480 | tf_op jit(solution)/shard_map/ppermute | solution.py:32
  291.4 26.2 %collective-permute-start.10 = (bf16[128,2304]{1,0:T(8,128)(2,1)S(1)}, bf16[128,2304]{1,0:T(8,128)(2,1)}, u32[]{:S(2)}, u32[]{:S(2)}) collective-permute-start(bf16[128,2304]{1,0:T(8,128)(2,1)S(1)} %get-tuple-element.91), channel_id=1, source_target_pairs={{0,1},{1,0},{2,3},{3,2},{4,5},{5,4},{6,7},{7,6},{8,9},{9,8},{10,11... | collective-permute-start | bytes 1769480 | tf_op jit(solution)/shard_map/ppermute | solution.py:32
  293.3 350.4 %reduce-scatter.4.cloned.1.call-start = ((), (), s32[]{:S(2)}) async-start(), calls=%async_computation.7 | async-start | bytes 6635520 | tf_op jit(solution)/shard_map/reduce_scatter | solution.py:335
  324.4 16.2 %collective-permute-start.13 = (bf16[128,2304]{1,0:T(8,128)(2,1)S(1)}, bf16[128,2304]{1,0:T(8,128)(2,1)S(1)}, u32[]{:S(2)}, u32[]{:S(2)}) collective-permute-start(bf16[128,2304]{1,0:T(8,128)(2,1)S(1)} %get-tuple-element.47), channel_id=1, source_target_pairs={{0,1},{1,0},{2,3},{3,2},{4,5},{5,4},{6,7},{7,6},{8,9},{9,8},{10,11... | collective-permute-start | bytes 1769480 | tf_op jit(solution)/shard_map/ppermute | solution.py:32
  325.9 27.6 %collective-permute-start.14 = (bf16[128,2304]{1,0:T(8,128)(2,1)S(1)}, bf16[128,2304]{1,0:T(8,128)(2,1)S(1)}, u32[]{:S(2)}, u32[]{:S(2)}) collective-permute-start(bf16[128,2304]{1,0:T(8,128)(2,1)S(1)} %get-tuple-element.47), channel_id=1, source_target_pairs={{0,4},{1,5},{2,6},{3,7},{4,0},{5,1},{6,2},{7,3},{8,12},{9,13},{10,... | collective-permute-start | bytes 1769480 | tf_op jit(solution)/shard_map/ppermute | solution.py:32
  326.4 27.0 %collective-permute-start.15 = (bf16[128,2304]{1,0:T(8,128)(2,1)S(1)}, bf16[128,2304]{1,0:T(8,128)(2,1)S(1)}, u32[]{:S(2)}, u32[]{:S(2)}) collective-permute-start(bf16[128,2304]{1,0:T(8,128)(2,1)S(1)} %get-tuple-element.47), channel_id=1, source_target_pairs={{0,5},{1,4},{2,7},{3,6},{4,1},{5,0},{6,3},{7,2},{8,13},{9,12},{10,... | collective-permute-start | bytes 1769480 | tf_op jit(solution)/shard_map/ppermute | solution.py:32
  353.6 4.6 collective-permute-start.16
  435.9 4.6 collective-permute-start.23
  443.9 17.2 %collective-permute-start.26 = (bf16[128,2304]{1,0:T(8,128)(2,1)S(1)}, bf16[128,2304]{1,0:T(8,128)(2,1)S(1)}, u32[]{:S(2)}, u32[]{:S(2)}) collective-permute-start(bf16[128,2304]{1,0:T(8,128)(2,1)S(1)} %get-tuple-element.56), channel_id=1, source_target_pairs={{0,5},{1,4},{2,7},{3,6},{4,1},{5,0},{6,3},{7,2},{8,13},{9,12},{10,... | collective-permute-start | bytes 1769480 | tf_op jit(solution)/shard_map/ppermute | solution.py:32
  446.3 26.5 %collective-permute-start.25 = (bf16[128,2304]{1,0:T(8,128)(2,1)S(1)}, bf16[128,2304]{1,0:T(8,128)(2,1)S(1)}, u32[]{:S(2)}, u32[]{:S(2)}) collective-permute-start(bf16[128,2304]{1,0:T(8,128)(2,1)S(1)} %get-tuple-element.57), channel_id=1, source_target_pairs={{0,4},{1,5},{2,6},{3,7},{4,0},{5,1},{6,2},{7,3},{8,12},{9,13},{10,... | collective-permute-start | bytes 1769480 | tf_op jit(solution)/shard_map/ppermute | solution.py:32
  446.9 26.0 %collective-permute-start.24 = (bf16[128,2304]{1,0:T(8,128)(2,1)S(1)}, bf16[128,2304]{1,0:T(8,128)(2,1)S(1)}, u32[]{:S(2)}, u32[]{:S(2)}) collective-permute-start(bf16[128,2304]{1,0:T(8,128)(2,1)S(1)} %get-tuple-element.55), channel_id=1, source_target_pairs={{0,1},{1,0},{2,3},{3,2},{4,5},{5,4},{6,7},{7,6},{8,9},{9,8},{10,11... | collective-permute-start | bytes 1769480 | tf_op jit(solution)/shard_map/ppermute | solution.py:32
  475.3 16.3 %collective-permute-start.27 = (bf16[128,2304]{1,0:T(8,128)(2,1)S(1)}, bf16[128,2304]{1,0:T(8,128)(2,1)S(1)}, u32[]{:S(2)}, u32[]{:S(2)}) collective-permute-start(bf16[128,2304]{1,0:T(8,128)(2,1)S(1)} %get-tuple-element.43), channel_id=1, source_target_pairs={{0,1},{1,0},{2,3},{3,2},{4,5},{5,4},{6,7},{7,6},{8,9},{9,8},{10,11... | collective-permute-start | bytes 1769480 | tf_op jit(solution)/shard_map/ppermute | solution.py:32
  476.9 27.6 %collective-permute-start.28 = (bf16[128,2304]{1,0:T(8,128)(2,1)S(1)}, bf16[128,2304]{1,0:T(8,128)(2,1)S(1)}, u32[]{:S(2)}, u32[]{:S(2)}) collective-permute-start(bf16[128,2304]{1,0:T(8,128)(2,1)S(1)} %get-tuple-element.43), channel_id=1, source_target_pairs={{0,4},{1,5},{2,6},{3,7},{4,0},{5,1},{6,2},{7,3},{8,12},{9,13},{10,... | collective-permute-start | bytes 1769480 | tf_op jit(solution)/shard_map/ppermute | solution.py:32
  477.7 26.8 %collective-permute-start.29 = (bf16[128,2304]{1,0:T(8,128)(2,1)S(1)}, bf16[128,2304]{1,0:T(8,128)(2,1)S(1)}, u32[]{:S(2)}, u32[]{:S(2)}) collective-permute-start(bf16[128,2304]{1,0:T(8,128)(2,1)S(1)} %get-tuple-element.43), channel_id=1, source_target_pairs={{0,5},{1,4},{2,7},{3,6},{4,1},{5,0},{6,3},{7,2},{8,13},{9,12},{10,... | collective-permute-start | bytes 1769480 | tf_op jit(solution)/shard_map/ppermute | solution.py:32
  504.6 4.6 collective-permute-start.30
  519.6 268.9 %reduce-scatter.6.cloned.1.call-start = ((), (), s32[]{:S(2)}) async-start(), calls=%async_computation.8 | async-start | bytes 6635520 | tf_op jit(solution)/shard_map/reduce_scatter | solution.py:335
  549.6 14.6 %collective-permute-start.31 = (bf16[512,2304]{1,0:T(8,128)(2,1)S(1)}, bf16[512,2304]{1,0:T(8,128)(2,1)S(1)}, u32[]{:S(2)}, u32[]{:S(2)}) collective-permute-start(bf16[512,2304]{1,0:T(8,128)(2,1)S(1)} %fusion.19), channel_id=1, source_target_pairs={{0,2},{1,3},{2,0},{3,1},{4,6},{5,7},{6,4},{7,5},{8,10},{9,11},{10,... | collective-permute-start | bytes 7077896 | tf_op jit(solution)/shard_map/ppermute | solution.py:32
  570.6 17.3 %collective-permute-start.34 = (bf16[128,2304]{1,0:T(8,128)(2,1)}, bf16[128,2304]{1,0:T(8,128)(2,1)S(1)}, u32[]{:S(2)}, u32[]{:S(2)}) collective-permute-start(bf16[128,2304]{1,0:T(8,128)(2,1)} %get-tuple-element.53), channel_id=1, source_target_pairs={{0,5},{1,4},{2,7},{3,6},{4,1},{5,0},{6,3},{7,2},{8,13},{9,12},{10,... | collective-permute-start | bytes 1769480 | tf_op jit(solution)/shard_map/ppermute | solution.py:32
  571.3 28.2 %collective-permute-start.33 = (bf16[128,2304]{1,0:T(8,128)(2,1)}, bf16[128,2304]{1,0:T(8,128)(2,1)S(1)}, u32[]{:S(2)}, u32[]{:S(2)}) collective-permute-start(bf16[128,2304]{1,0:T(8,128)(2,1)} %get-tuple-element.54), channel_id=1, source_target_pairs={{0,4},{1,5},{2,6},{3,7},{4,0},{5,1},{6,2},{7,3},{8,12},{9,13},{10,... | collective-permute-start | bytes 1769480 | tf_op jit(solution)/shard_map/ppermute | solution.py:32
  571.8 27.6 %collective-permute-start.32 = (bf16[128,2304]{1,0:T(8,128)(2,1)}, bf16[128,2304]{1,0:T(8,128)(2,1)}, u32[]{:S(2)}, u32[]{:S(2)}) collective-permute-start(bf16[128,2304]{1,0:T(8,128)(2,1)} %get-tuple-element.52), channel_id=1, source_target_pairs={{0,1},{1,0},{2,3},{3,2},{4,5},{5,4},{6,7},{7,6},{8,9},{9,8},{10,11... | collective-permute-start | bytes 1769480 | tf_op jit(solution)/shard_map/ppermute | solution.py:32
  583.9 328.6 %reduce-scatter.8.cloned.1.call-start = ((), (), s32[]{:S(2)}) async-start(), calls=%async_computation.9 | async-start | bytes 6635520 | tf_op jit(solution)/shard_map/reduce_scatter | solution.py:335
  606.0 17.2 %collective-permute-start.37 = (bf16[128,2304]{1,0:T(8,128)(2,1)S(1)}, bf16[128,2304]{1,0:T(8,128)(2,1)S(1)}, u32[]{:S(2)}, u32[]{:S(2)}) collective-permute-start(bf16[128,2304]{1,0:T(8,128)(2,1)S(1)} %after.18), channel_id=1, source_target_pairs={{0,5},{1,4},{2,7},{3,6},{4,1},{5,0},{6,3},{7,2},{8,13},{9,12},{10,... | collective-permute-start | bytes 1769480 | tf_op jit(solution)/shard_map/ppermute | solution.py:32
  607.2 27.3 %collective-permute-start.36 = (bf16[128,2304]{1,0:T(8,128)(2,1)S(1)}, bf16[128,2304]{1,0:T(8,128)(2,1)S(1)}, u32[]{:S(2)}, u32[]{:S(2)}) collective-permute-start(bf16[128,2304]{1,0:T(8,128)(2,1)S(1)} %after.18), channel_id=1, source_target_pairs={{0,4},{1,5},{2,6},{3,7},{4,0},{5,1},{6,2},{7,3},{8,12},{9,13},{10,... | collective-permute-start | bytes 1769480 | tf_op jit(solution)/shard_map/ppermute | solution.py:32
  607.9 26.6 %collective-permute-start.35 = (bf16[128,2304]{1,0:T(8,128)(2,1)S(1)}, bf16[128,2304]{1,0:T(8,128)(2,1)S(1)}, u32[]{:S(2)}, u32[]{:S(2)}) collective-permute-start(bf16[128,2304]{1,0:T(8,128)(2,1)S(1)} %after.18), channel_id=1, source_target_pairs={{0,1},{1,0},{2,3},{3,2},{4,5},{5,4},{6,7},{7,6},{8,9},{9,8},{10,11... | collective-permute-start | bytes 1769480 | tf_op jit(solution)/shard_map/ppermute | solution.py:32
  668.9 40.7 %collective-permute-start.39 = (bf16[2048,512]{1,0:T(8,128)(2,1)}, bf16[2048,512]{1,0:T(8,128)(2,1)}, u32[]{:S(2)}, u32[]{:S(2)}) collective-permute-start(bf16[2048,512]{1,0:T(8,128)(2,1)} %get-tuple-element.24), channel_id=1, source_target_pairs={{0,2},{1,3},{2,0},{3,1},{4,6},{5,7},{6,4},{7,5},{8,10},{9,11},{10,... | collective-permute-start | bytes 6291464 | tf_op jit(solution)/shard_map/ppermute | solution.py:32
  669.3 39.6 %collective-permute-start.49 = (bf16[2,288,512]{2,1,0:T(8,128)(2,1)S(1)}, bf16[2,288,512]{2,1,0:T(8,128)(2,1)S(1)}, u32[]{:S(2)}, u32[]{:S(2)}) collective-permute-start(bf16[2,288,512]{2,1,0:T(8,128)(2,1)S(1)} %fusion.104), channel_id=1, source_target_pairs={{0,8},{1,9},{2,10},{3,11},{4,12},{5,13},{6,14},{7,15},{8,0},{9,1},... | collective-permute-start | bytes 1769480 | tf_op jit(solution)/shard_map/ppermute | solution.py:32
  709.2 19.4 %collective-permute-start.50 = (bf16[288,512]{1,0:T(8,128)(2,1)S(1)}, bf16[288,512]{1,0:T(8,128)(2,1)S(1)}, u32[]{:S(2)}, u32[]{:S(2)}) collective-permute-start(bf16[288,512]{1,0:T(8,128)(2,1)S(1)} %fusion.135), channel_id=1, source_target_pairs={{0,16},{1,17},{2,18},{3,19},{4,20},{5,21},{6,22},{7,23},{8,24},{9,... | collective-permute-start | bytes 884744 | tf_op jit(solution)/shard_map/ppermute | solution.py:32
  716.3 33.4 %collective-permute-start.40 = (bf16[1024,512]{1,0:T(8,128)(2,1)}, bf16[1024,512]{1,0:T(8,128)(2,1)}, u32[]{:S(2)}, u32[]{:S(2)}) collective-permute-start(bf16[1024,512]{1,0:T(8,128)(2,1)} %slice.678), channel_id=1, source_target_pairs={{0,8},{1,9},{2,10},{3,11},{4,12},{5,13},{6,14},{7,15},{8,0},{9,1},... | collective-permute-start | bytes 3145736 | tf_op jit(solution)/shard_map/ppermute | solution.py:32
  730.0 5.5 collective-permute-start.51
  751.9 26.1 %collective-permute-start.41 = (bf16[512,512]{1,0:T(8,128)(2,1)S(1)}, bf16[512,512]{1,0:T(8,128)(2,1)S(1)}, u32[]{:S(2)}, u32[]{:S(2)}) collective-permute-start(bf16[512,512]{1,0:T(8,128)(2,1)S(1)} %slice.679), channel_id=1, source_target_pairs={{0,16},{1,17},{2,18},{3,19},{4,20},{5,21},{6,22},{7,23},{8,24},{9,... | collective-permute-start | bytes 1572872 | tf_op jit(solution)/shard_map/ppermute | solution.py:32
  783.6 64.9 %collective-permute-start.45 = (bf16[128,2304]{1,0:T(8,128)(2,1)}, bf16[128,2304]{1,0:T(8,128)(2,1)S(1)}, u32[]{:S(2)}, u32[]{:S(2)}) collective-permute-start(bf16[128,2304]{1,0:T(8,128)(2,1)} %get-tuple-element.89), channel_id=1, source_target_pairs={{0,5},{1,4},{2,7},{3,6},{4,1},{5,0},{6,3},{7,2},{8,13},{9,12},{10,... | collective-permute-start | bytes 1769480 | tf_op jit(solution)/shard_map/ppermute | solution.py:32
  793.4 20.9 %collective-permute-start.52 = (bf16[2,144,1152]{2,1,0:T(8,128)(2,1)S(1)}, bf16[2,144,1152]{2,1,0:T(8,128)(2,1)S(1)}, u32[]{:S(2)}, u32[]{:S(2)}) collective-permute-start(bf16[2,144,1152]{2,1,0:T(8,128)(2,1)S(1)} %dynamic-slice_bitcast_fusion.2), channel_id=1, source_target_pairs={{0,4},{1,5},{2,6},{3,7},{4,0},{5,1},{6,2},{7,3},{8,12},{9,13},{10,... | collective-permute-start | bytes 1990664 | tf_op jit(solution)/shard_map/ppermute | solution.py:32
  799.5 47.8 %collective-permute-start.43 = (bf16[8,144,1024]{2,1,0:T(8,128)(2,1)S(1)}, bf16[8,144,1024]{2,1,0:T(8,128)(2,1)S(1)}, u32[]{:S(2)}, u32[]{:S(2)}) collective-permute-start(bf16[8,144,1024]{2,1,0:T(8,128)(2,1)S(1)} %fusion.25), channel_id=1, source_target_pairs={{0,2},{1,3},{2,0},{3,1},{4,6},{5,7},{6,4},{7,5},{8,10},{9,11},{10,... | collective-permute-start | bytes 7077896 | tf_op jit(solution)/shard_map/ppermute | solution.py:32
  799.6 49.0 %collective-permute-start.44 = (bf16[128,2304]{1,0:T(8,128)(2,1)S(1)}, bf16[128,2304]{1,0:T(8,128)(2,1)S(1)}, u32[]{:S(2)}, u32[]{:S(2)}) collective-permute-start(bf16[128,2304]{1,0:T(8,128)(2,1)S(1)} %get-tuple-element.90), channel_id=1, source_target_pairs={{0,4},{1,5},{2,6},{3,7},{4,0},{5,1},{6,2},{7,3},{8,12},{9,13},{10,... | collective-permute-start | bytes 1769480 | tf_op jit(solution)/shard_map/ppermute | solution.py:32
  800.9 47.7 %collective-permute-start.42 = (bf16[128,2304]{1,0:T(8,128)(2,1)S(1)}, bf16[128,2304]{1,0:T(8,128)(2,1)S(1)}, u32[]{:S(2)}, u32[]{:S(2)}) collective-permute-start(bf16[128,2304]{1,0:T(8,128)(2,1)S(1)} %get-tuple-element.88), channel_id=1, source_target_pairs={{0,1},{1,0},{2,3},{3,2},{4,5},{5,4},{6,7},{7,6},{8,9},{9,8},{10,11... | collective-permute-start | bytes 1769480 | tf_op jit(solution)/shard_map/ppermute | solution.py:32
  814.3 26.8 %collective-permute-start.56 = (bf16[2,144,1152]{2,1,0:T(8,128)(2,1)S(1)}, bf16[2,144,1152]{2,1,0:T(8,128)(2,1)S(1)}, u32[]{:S(2)}, u32[]{:S(2)}) collective-permute-start(bf16[2,144,1152]{2,1,0:T(8,128)(2,1)S(1)} %dynamic-slice_bitcast_fusion), channel_id=1, source_target_pairs={{0,4},{1,5},{2,6},{3,7},{4,0},{5,1},{6,2},{7,3},{8,12},{9,13},{10,... | collective-permute-start | bytes 1990664 | tf_op jit(solution)/shard_map/ppermute | solution.py:32
  853.4 6.1 collective-permute-start.58
  859.6 6.5 collective-permute-start.59
  862.5 43.8 %collective-permute-start.46 = (bf16[2,288,1024]{2,1,0:T(8,128)(2,1)S(1)}, bf16[2,288,1024]{2,1,0:T(8,128)(2,1)}, u32[]{:S(2)}, u32[]{:S(2)}) collective-permute-start(bf16[2,288,1024]{2,1,0:T(8,128)(2,1)S(1)} %fusion.54), channel_id=1, source_target_pairs={{0,8},{1,9},{2,10},{3,11},{4,12},{5,13},{6,14},{7,15},{8,0},{9,1},... | collective-permute-start | bytes 3538952 | tf_op jit(solution)/shard_map/ppermute | solution.py:32
  866.1 3.7 collective-permute-start.60
  871.1 46.8 %collective-permute-start.62 = (f32[1,4,144]{2,0,1:T(1,128)S(1)}, f32[1,4,144]{2,0,1:T(1,128)}, u32[]{:S(2)}, u32[]{:S(2)}) collective-permute-start(f32[1,4,144]{2,0,1:T(1,128)S(1)} %fusion.176), channel_id=1, source_target_pairs={{0,1},{1,0},{2,3},{3,2},{4,5},{5,4},{6,7},{7,6},{8,9},{9,8},{10,11... | collective-permute-start | bytes 6920 | tf_op jit(solution)/shard_map/ppermute | solution.py:32
  909.6 29.0 %collective-permute-start.47 = (bf16[288,1024]{1,0:T(8,128)(2,1)}, bf16[288,1024]{1,0:T(8,128)(2,1)}, u32[]{:S(2)}, u32[]{:S(2)}) collective-permute-start(bf16[288,1024]{1,0:T(8,128)(2,1)} %fusion.103), channel_id=1, source_target_pairs={{0,16},{1,17},{2,18},{3,19},{4,20},{5,21},{6,22},{7,23},{8,24},{9,... | collective-permute-start | bytes 1769480 | tf_op jit(solution)/shard_map/ppermute | solution.py:32
  913.6 27.9 %collective-permute-start.54 = (bf16[2,144,1152]{2,1,0:T(8,128)(2,1)S(1)}, bf16[2,144,1152]{2,1,0:T(8,128)(2,1)S(1)}, u32[]{:S(2)}, u32[]{:S(2)}) collective-permute-start(bf16[2,144,1152]{2,1,0:T(8,128)(2,1)S(1)} %dynamic-slice_bitcast_fusion.1), channel_id=1, source_target_pairs={{0,4},{1,5},{2,6},{3,7},{4,0},{5,1},{6,2},{7,3},{8,12},{9,13},{10,... | collective-permute-start | bytes 1990664 | tf_op jit(solution)/shard_map/ppermute | solution.py:32
  939.9 9.0 collective-permute-start.48
  941.8 9.8 %collective-permute-start.55 = (bf16[2,144,1152]{2,1,0:T(8,128)(2,1)S(1)}, bf16[2,144,1152]{2,1,0:T(8,128)(2,1)S(1)}, u32[]{:S(2)}, u32[]{:S(2)}) collective-permute-start(bf16[2,144,1152]{2,1,0:T(8,128)(2,1)S(1)} %fusion.90), channel_id=1, source_target_pairs={{0,2},{1,3},{2,0},{3,1},{4,6},{5,7},{6,4},{7,5},{8,10},{9,11},{10,... | collective-permute-start | bytes 1990664 | tf_op jit(solution)/shard_map/ppermute | solution.py:32
  (82 other events, 803.4 us)
Sparse Core Ops, SparseCore 0:
  26.3 77.5 all-gather.4
  110.9 114.4 all-gather.6
  227.1 102.7 all-gather.8
  331.3 98.2 all-gather.10
  519.7 92.2 reduce-scatter.3
  614.3 114.9 reduce-scatter.5
  788.6 107.1 reduce-scatter.7
